TPU v7x, 32 devices: a whole 2x2x4 slice. The times are simulated.
32 devices in a mesh: grp: 2 (over y), gx: 4 (over z), gy: 2 (over x), col: 2 (over core).
Axes of the slice: x: 2, y: 2, z: 4, core: 2. Of those that a mesh axis runs over, the one named last changes fastest.
Arguments:
- field: bfloat16 [64, 32, 32, 128], P('grp', 'gx', ('gy', 'col')), parts along dimension 0, may hold values from -6 to 6
- cotangent: bfloat16 [64, 32, 32, 128], P('grp', 'gx', ('gy', 'col')), parts along dimension 0, may hold values from -6 to 6
- mode_weight: bfloat16 [2, 32, 32, 32, 32, 32], P(None, None, None, ('gy', 'col'), 'gx'), may hold values from -3 to 3
- skip_weight: bfloat16 [32, 32], replicated, may hold values from -1 to 1
- lift_weight: bfloat16 [128, 32], replicated, may hold values from -1 to 1
- proj_weight: bfloat16 [32, 128], replicated, may hold values from -0.5 to 0.5
Outputs:
- field_grad: bfloat16 [64, 32, 32, 128], P('grp', 'gx', ('gy', 'col')), parts along dimension 0
- mode_grad: bfloat16 [4, 32, 32, 32, 32, 32], P('grp', None, None, ('gy', 'col'), 'gx'), parts along dimension 0
- skip_grad: float32 [64, 32], P('grp'), parts along dimension 0
- lift_grad: float32 [256, 32], P('grp'), parts along dimension 0
- proj_grad: float32 [64, 128], P('grp'), parts along dimension 0
There are 2 independent parts, one for each index of `grp`. A program takes and returns all parts, laid end to end along the dimension named above; an argument that names none is the same for every part. Nothing has to cross between parts.
All inputs are finite; a program needn't handle non-finite values.
Results may differ from a plain program's by a relative error of at most 0.023.
Values may be sent and summed in bfloat16 or wider, within the bound.
No kernel may reach another device: no remote copies, remote signals or barrier semaphores. Data moves between devices by JAX's collectives and lax.ppermute only.
A program may use at most 192 MiB of HBM per device.

v0:
```python
import functools
import math

import jax
import jax.numpy as jnp
import ml_dtypes
import numpy as np
from jax import lax
from jax.experimental import pallas as pl
from jax.experimental.pallas import tpu as pltpu
from jax.sharding import PartitionSpec as P

MX = 32
MY = 32
MZ = 32


KAPPA = 0.7978845608028654
CUBIC = 0.044715


def gelu_slope(value):
    inner = KAPPA * (value + CUBIC * value * value * value)
    tangent = jnp.tanh(inner)
    result = 0.5 * value * (1.0 + tangent)
    slope = 0.5 * (1.0 + tangent) + 0.5 * value * (1.0 - tangent * tangent) * KAPPA * (
        1.0 + 3.0 * CUBIC * value * value
    )
    return (result, slope)


def trig_pair(freqs, length):
    positions = jnp.arange(length, dtype=jnp.int32)
    turns = positions[:, None] * (freqs[None, :] % length) % length
    angle = turns.astype(jnp.float32) * (2.0 * math.pi / length)
    factor = 1.0 / math.sqrt(length)
    return (jnp.cos(angle) * factor, jnp.sin(angle) * factor)


def real_table(freqs, length):
    cosine, sine = trig_pair(freqs, length)
    return jnp.stack([cosine.T, -sine.T]).astype(jnp.bfloat16)


def complex_table(freqs, length):
    cosine, sine = trig_pair(freqs, length)
    upper = jnp.stack([cosine, -sine], axis=1)
    lower = jnp.stack([sine, cosine], axis=1)
    return jnp.stack([upper, lower]).astype(jnp.bfloat16)


def centered(count):
    return jnp.arange(count, dtype=jnp.int32) - count // 2


def to_modes(values, tables):
    z_table, y_table, x_table = tables
    chans, xrows, yrows, zlen = values.shape
    first = jnp.einsum("cxyn,qkn->qkycx", values, z_table, preferred_element_type=jnp.float32)
    first = first.astype(jnp.bfloat16).reshape(2, MZ, yrows, chans * xrows)
    moved = lax.all_to_all(first, ("gy", "col"), split_axis=1, concat_axis=2, tiled=True)
    second = jnp.einsum("pkyr,pyqj->qkjr", moved, y_table, preferred_element_type=jnp.float32)
    second = second.astype(jnp.bfloat16)[:, :, :, None, :]
    crossed = lax.all_to_all(second, "gx", split_axis=2, concat_axis=3, tiled=True)
    crossed = crossed.reshape(crossed.shape[:4] + (chans, xrows))
    third = jnp.einsum("pkjgcx,pgxql->qckjl", crossed, x_table, preferred_element_type=jnp.float32)
    return third.astype(jnp.bfloat16).reshape(2, chans, -1)


def to_grid(spec, tables, shape, local_modes):
    z_table, y_table, x_table = tables
    chans, xrows, yrows, zlen = shape
    spec = spec.reshape((2, chans) + local_modes)
    first = jnp.einsum("pckjl,qgxpl->qkjgcx", spec, x_table, preferred_element_type=jnp.float32)
    first = first.astype(jnp.bfloat16)
    first = first.reshape(first.shape[:4] + (chans * xrows,))
    joined = lax.all_to_all(first, "gx", split_axis=3, concat_axis=2, tiled=True)
    joined = joined.reshape(joined.shape[:3] + (chans * xrows,))
    second = jnp.einsum("pkjr,qypj->qkyr", joined, y_table, preferred_element_type=jnp.float32)
    second = second.astype(jnp.bfloat16)
    returned = lax.all_to_all(second, ("gy", "col"), split_axis=2, concat_axis=1, tiled=True)
    grid = jnp.einsum("pkyr,pkn->ryn", returned, z_table, preferred_element_type=jnp.float32)
    return grid.reshape(chans, xrows, yrows, zlen)


def mix(weight, modes):
    real = jnp.einsum("iok,ik->ok", weight[0], modes[0], preferred_element_type=jnp.float32)
    real = real - jnp.einsum("iok,ik->ok", weight[1], modes[1], preferred_element_type=jnp.float32)
    imag = jnp.einsum("iok,ik->ok", weight[0], modes[1], preferred_element_type=jnp.float32)
    imag = imag + jnp.einsum("iok,ik->ok", weight[1], modes[0], preferred_element_type=jnp.float32)
    return jnp.stack([real, imag]).astype(jnp.bfloat16)


def general(field, cotangent, mode_weight, skip_weight, lift_weight, proj_weight):
    chans, xrows, yrows, zlen = field.shape
    groups_x = lax.axis_size("gx")
    groups_y = lax.axis_size("gy")
    groups_c = lax.axis_size("col")
    span_x = xrows * groups_x
    span_y = yrows * groups_y * groups_c
    column = jnp.arange(MZ, dtype=jnp.int32)
    z_table = real_table(column, zlen)
    y_table = complex_table(centered(MY), span_y)
    x_table = complex_table(centered(MX), span_x).reshape(2, groups_x, xrows, 2, MX)
    tables = (z_table, y_table, x_table)
    local_modes = (mode_weight.shape[3], mode_weight.shape[4], mode_weight.shape[5])
    weight_flat = mode_weight.reshape(2, chans, chans, -1)
    modes = to_modes(field, tables)
    spectral = to_grid(mix(weight_flat, modes), tables, field.shape, local_modes).reshape(chans, -1)
    flat_field = field.reshape(chans, -1)
    flat_grad = cotangent.reshape(chans, -1)
    pre = spectral + jnp.dot(skip_weight, flat_field, preferred_element_type=jnp.float32)
    lifted, slope_pre = gelu_slope(pre)
    lifted = lifted.astype(jnp.bfloat16)
    hidden = jnp.dot(lift_weight, lifted, preferred_element_type=jnp.float32)
    activated, slope_hid = gelu_slope(hidden)
    activated = activated.astype(jnp.bfloat16)
    back_hidden = jnp.dot(proj_weight.T, flat_grad, preferred_element_type=jnp.float32)
    hidden_grad = (back_hidden * slope_hid).astype(jnp.bfloat16)
    grad_up = flat_grad.astype(jnp.float32) + jnp.dot(
        lift_weight.T, hidden_grad, preferred_element_type=jnp.float32
    )
    pre_grad = (grad_up * slope_pre).astype(jnp.bfloat16)
    proj_part = jnp.einsum("cr,hr->ch", flat_grad, activated, preferred_element_type=jnp.float32)
    lift_part = jnp.einsum("hr,cr->hc", hidden_grad, lifted, preferred_element_type=jnp.float32)
    skip_part = jnp.einsum("or,ir->oi", pre_grad, flat_field, preferred_element_type=jnp.float32)
    proj_grad, lift_grad, skip_grad = lax.psum(
        (proj_part, lift_part, skip_part), ("gx", "gy", "col")
    )
    pre_modes = to_modes(pre_grad.reshape(field.shape), tables)
    grad_real = jnp.einsum("ik,ok->iok", modes[0], pre_modes[0], preferred_element_type=jnp.float32)
    grad_real = grad_real + jnp.einsum(
        "ik,ok->iok", modes[1], pre_modes[1], preferred_element_type=jnp.float32
    )
    grad_imag = jnp.einsum("ik,ok->iok", modes[0], pre_modes[1], preferred_element_type=jnp.float32)
    grad_imag = grad_imag - jnp.einsum(
        "ik,ok->iok", modes[1], pre_modes[0], preferred_element_type=jnp.float32
    )
    mode_grad = jnp.stack([grad_real, grad_imag]).astype(jnp.bfloat16).reshape(mode_weight.shape)
    back_real = jnp.einsum(
        "iok,ok->ik", weight_flat[0], pre_modes[0], preferred_element_type=jnp.float32
    )
    back_real = back_real + jnp.einsum(
        "iok,ok->ik", weight_flat[1], pre_modes[1], preferred_element_type=jnp.float32
    )
    back_imag = jnp.einsum(
        "iok,ok->ik", weight_flat[0], pre_modes[1], preferred_element_type=jnp.float32
    )
    back_imag = back_imag - jnp.einsum(
        "iok,ok->ik", weight_flat[1], pre_modes[0], preferred_element_type=jnp.float32
    )
    modes_grad = jnp.stack([back_real, back_imag]).astype(jnp.bfloat16)
    spectral_grad = to_grid(modes_grad, tables, field.shape, local_modes).reshape(chans, -1)
    skip_back = jnp.dot(skip_weight.T, pre_grad, preferred_element_type=jnp.float32)
    field_grad = (spectral_grad + skip_back).astype(jnp.bfloat16).reshape(field.shape)
    return (field_grad, mode_grad, skip_grad, lift_grad, proj_grad)


def np_trig(freqs, length):
    positions = np.arange(length)
    turns = positions[:, None] * (freqs[None, :] % length) % length
    angle = turns.astype(np.float32) * np.float32(2.0 * math.pi / length)
    factor = np.float32(1.0 / math.sqrt(length))
    return np.cos(angle) * factor, np.sin(angle) * factor


def np_complex(cosine, sine, sign):
    table = np.zeros((cosine.shape[0], 2, cosine.shape[1], 2), np.float32)
    table[:, 0, :, 0] = cosine
    table[:, 1, :, 0] = -sign * sine
    table[:, 1, :, 1] = cosine
    table[:, 0, :, 1] = sign * sine
    return table


def make_tables(zlen, span_y, span_x, nb, xrows, yrows):
    kzb, kyb = MZ // nb, MY // nb
    zc, zs = np_trig(np.arange(MZ), zlen)
    yc, ys = np_trig(np.arange(MY) - MY // 2, span_y)
    xc, xs = np_trig(np.arange(MX) - MX // 2, span_x)
    zpart = np.stack([zc, -zs]).reshape(2, zlen, nb, kzb)
    zf = np.einsum("pzbk,yw->yzbwpk", zpart, np.eye(yrows, dtype=np.float32))
    zf = zf.reshape(yrows * zlen, nb, yrows * 2 * kzb).transpose(1, 0, 2)
    zi = np.ascontiguousarray(zf.transpose(0, 2, 1))
    yt = np_complex(yc, ys, -1).reshape(nb, yrows, 2, nb, kyb, 2)
    eye = np.eye(kzb, dtype=np.float32)
    yf = np.einsum("bypjmq,kh->bjypkqhm", yt, eye).reshape(nb, nb, yrows * 2 * kzb, 2 * kzb * kyb)
    yi_t = np_complex(yc, ys, -1).reshape(nb, yrows, 2, nb, kyb, 2)
    yi = np.einsum("bypjmq,kh->jbqhmypk", yi_t, eye).reshape(nb, nb, 2 * kzb * kyb, yrows * 2 * kzb)
    xt = np_complex(xc, xs, -1).reshape(nb, xrows, 2, MX, 2)
    four = np.eye(4, dtype=np.float32)
    xf = np.einsum("bxplq,cd->bpcxqdl", xt, four).reshape(nb, 2, 4 * xrows, 8 * MX)
    xr = np.einsum("bxplq,cd,r->bpcxdqrl", xt, four, np.ones(4, np.float32))
    xr = xr.reshape(nb, 2, 4 * xrows, 32 * MX)
    both = np.stack([xc, xs]).reshape(2, nb, xrows, MX)
    xi = np.einsum("tbxl,r->bxtrl", both, np.ones(4, np.float32)).reshape(nb, xrows, 8 * MX)
    xd = np.einsum("tbxl,cd->bcxtdl", both, four).reshape(nb, 4 * xrows, 8 * MX)
    bf = ml_dtypes.bfloat16
    return [np.asarray(t).astype(bf) for t in (zf, zi, yf, yi, xf, xr)] + [
        xi.astype(bf).astype(np.float32),
        xd.astype(bf),
    ]


def dot(a, b):
    return lax.dot_general(a, b, (((1,), (0,)), ((), ())), preferred_element_type=jnp.float32)


def dot_nt(a, b):
    return lax.dot_general(a, b, (((1,), (1,)), ((), ())), preferred_element_type=jnp.float32)


BF = jnp.bfloat16
F32 = jnp.float32


def z_forward_kernel(rows, yrows, zlen, idx, field, zf, o0, o1, o2, o3, wide):
    wide[...] = field[...].astype(F32)
    side = jnp.concatenate(
        [wide[pl.ds(y, rows, stride=yrows), :].astype(BF) for y in range(yrows)], axis=1
    )
    table = jnp.concatenate([zf[idx[0] ^ s] for s in range(4)], axis=1)
    out = dot(side, table).astype(BF)
    for s, o in enumerate((o0, o1, o2, o3)):
        o[...] = out[:, s * 128 : (s + 1) * 128]


def lane_kernel(near, far, idx, r0, r1, r2, r3, table, o0, o1, o2, o3):
    side = jnp.concatenate([r0[...], r1[...], r2[...], r3[...]], axis=1)
    cols = []
    for t in range(4):
        cols.append(
            jnp.concatenate([table[idx[near] ^ s, idx[far] ^ t] for s in range(4)], axis=0)
        )
    out = dot(side, jnp.concatenate(cols, axis=1)).astype(BF)
    for t, o in enumerate((o0, o1, o2, o3)):
        o[...] = out[:, t * 128 : (t + 1) * 128]


def x_side(idx, refs, tab):
    parts = []
    for g in range(8):
        block = jnp.concatenate([r[g * 32 : (g + 1) * 32, :] for r in refs], axis=0)
        turned = block.astype(F32).T.astype(BF)
        parts.append(jnp.concatenate([turned[:64, :], turned[64:, :]], axis=1))
    side = jnp.concatenate(parts, axis=0)
    table = jnp.concatenate([tab[idx[1] ^ s, p] for p in range(2) for s in range(4)], axis=0)
    return side, table


def mix_forward_kernel(idx, r0, r1, r2, r3, xf, xi, weight, modes, o0, o1, o2, o3):
    side, table = x_side(idx, (r0, r1, r2, r3), xf)
    got = dot(side, table).astype(BF)
    for g in range(8):
        modes[g, 0] = got[g * 64 : (g + 1) * 64, :128]
        modes[g, 1] = got[g * 64 : (g + 1) * 64, 128:]
    left = jnp.concatenate([xi[idx[1] ^ s] for s in range(4)], axis=0).astype(BF)
    outs = (o0, o1, o2, o3)

    def pair(k, carry):
        rows = []
        for j in range(2):
            o = 2 * k + j
            real = jnp.zeros((64, 128), F32)
            imag = jnp.zeros((64, 128), F32)
            for g in range(8):
                wr = weight[g, 0, o].astype(F32)
                wi = weight[g, 1, o].astype(F32)
                mr = modes[g, 0].astype(F32)
                mi = modes[g, 1].astype(F32)
                real = real + wr * mr - wi * mi
                imag = imag + wr * mi + wi * mr
            rows.append(jnp.concatenate([real.astype(BF), (-imag).astype(BF)], axis=1))
            rows.append(jnp.concatenate([imag.astype(BF), real.astype(BF)], axis=1))
        got = dot_nt(left, jnp.concatenate(rows, axis=0))
        for s in range(4):
            both = jnp.concatenate(
                [got[s * 8 : (s + 1) * 8, :128], got[s * 8 : (s + 1) * 8, 128:]], axis=0
            )
            outs[s][pl.ds(pl.multiple_of(k * 16, 16), 16), :] = both.astype(BF)
        return carry

    lax.fori_loop(0, 16, pair, 0)


def mix_backward_kernel(idx, r0, r1, r2, r3, xr, xd, weight, pmodes, o0, o1, o2, o3):
    side, table = x_side(idx, (r0, r1, r2, r3), xr)
    for d in range(4):
        got = dot(side, table[:, d * 256 : (d + 1) * 256]).astype(BF)
        for g in range(8):
            pmodes[4 * g + d, 0] = got[g * 64 : (g + 1) * 64, :128]
            pmodes[4 * g + d, 1] = got[g * 64 : (g + 1) * 64, 128:]
    left = jnp.concatenate([xd[idx[1] ^ s] for s in range(4)], axis=0)
    outs = (o0, o1, o2, o3)

    def group(g, carry):
        real = jnp.zeros((64, 128), F32)
        imag = jnp.zeros((64, 128), F32)
        for o in range(32):
            wr = weight[g, 0, o].astype(F32)
            wi = weight[g, 1, o].astype(F32)
            pr = pmodes[o, 0].astype(F32)
            pi = pmodes[o, 1].astype(F32)
            real = real + wr * pr + wi * pi
            imag = imag + wr * pi - wi * pr
        rows = [
            jnp.concatenate([real.astype(BF), (-imag).astype(BF)], axis=1),
            jnp.concatenate([imag.astype(BF), real.astype(BF)], axis=1),
        ]
        got = dot_nt(left, jnp.concatenate(rows, axis=0)).astype(BF)
        for s in range(4):
            outs[s][pl.ds(pl.multiple_of(g * 32, 32), 32), :] = got[s * 32 : (s + 1) * 32]
        return carry

    lax.fori_loop(0, 8, group, 0)


def pack_kernel(weight, packed):
    def step(o, carry):
        for p in range(2):
            packed[0, p, o] = jnp.concatenate([weight[p, k, o] for k in range(4)], axis=1)
        return carry

    lax.fori_loop(0, 32, step, 0)


def outer_kernel(modes, pmodes, grad):
    def step(o, carry):
        mr = modes[0, 0].astype(F32)
        mi = modes[0, 1].astype(F32)
        pr = pmodes[o, 0].astype(F32)
        pi = pmodes[o, 1].astype(F32)
        real = (mr * pr + mi * pi).astype(BF)
        imag = (mr * pi - mi * pr).astype(BF)
        for k in range(4):
            grad[0, k, o] = real[:, k * 32 : (k + 1) * 32]
            grad[1, k, o] = imag[:, k * 32 : (k + 1) * 32]
        return carry

    lax.fori_loop(0, 32, step, 0)


def cells_kernel(yrows, field, cotangent, fx, cx, wide):
    for src, dst in ((field, fx), (cotangent, cx)):
        wide[...] = src[...].astype(F32)

        def step(k, carry):
            first = k * 2
            dst[k] = jnp.concatenate(
                [wide[pl.ds(first + j, 32, stride=64), :] for j in range(2)], axis=1
            ).astype(BF)
            return carry

        lax.fori_loop(0, 32, step, 0)


def point_kernel(
    idx, r0, r1, r2, r3, zi, zf, fx, cx, skip, lift, lift_t, proj_t,
    o0, o1, o2, o3, pg, sums, spectral, wide,
):
    side = jnp.concatenate([r0[...], r1[...], r2[...], r3[...]], axis=1)
    back = jnp.concatenate([zi[idx[0] ^ s] for s in range(4)], axis=0)
    for y in range(8):
        spectral[y] = dot(side, back[:, y * 128 : (y + 1) * 128])
    sums[...] = jnp.zeros_like(sums)

    def step(k, carry):
        x, part = k // 4, k % 4
        rows = pl.ds(x, 32, stride=8)
        values, grads = fx[k], cx[k]
        pre = jnp.concatenate([spectral[2 * part + j, rows, :] for j in range(2)], axis=1)
        pre = pre + dot(skip[...], values)
        lifted, slope_pre = gelu_slope(pre)
        lifted = lifted.astype(BF)
        hidden = dot(lift[...], lifted)
        activated, slope_hid = gelu_slope(hidden)
        activated = activated.astype(BF)
        hidden_grad = (dot(proj_t[...], grads) * slope_hid).astype(BF)
        grad_up = grads.astype(F32) + dot(lift_t[...], hidden_grad)
        pre_grad = grad_up * slope_pre
        pre_grad_b = pre_grad.astype(BF)
        for j in range(2):
            wide[2 * part + j, rows, :] = pre_grad[:, j * 128 : (j + 1) * 128]
        pg[k] = pre_grad_b
        tall = jnp.concatenate([activated, hidden_grad, pre_grad_b], axis=0)
        low = jnp.concatenate([grads, lifted, values], axis=0)
        sums[...] += dot_nt(tall, low)
        return carry

    lax.fori_loop(0, 32, step, 0)
    table = jnp.concatenate([zf[idx[0] ^ s] for s in range(4)], axis=1)
    side = jnp.concatenate([wide[y].astype(BF) for y in range(8)], axis=1)
    out = dot(side, table).astype(BF)
    for s, o in enumerate((o0, o1, o2, o3)):
        o[...] = out[:, s * 128 : (s + 1) * 128]


def finish_kernel(idx, r0, r1, r2, r3, zi, pg, skip_t, out, spectral, wide):
    side = jnp.concatenate([r0[...], r1[...], r2[...], r3[...]], axis=1)
    back = jnp.concatenate([zi[idx[0] ^ s] for s in range(4)], axis=0)
    for y in range(8):
        spectral[y] = dot(side, back[:, y * 128 : (y + 1) * 128])

    def step(k, carry):
        x, part = k // 4, k % 4
        rows = pl.ds(x, 32, stride=8)
        got = jnp.concatenate([spectral[2 * part + j, rows, :] for j in range(2)], axis=1)
        got = got + dot(skip_t[...], pg[k])
        first = k * 2
        wide[pl.ds(first, 32, stride=64), :] = got[:, :128]
        wide[pl.ds(first + 1, 32, stride=64), :] = got[:, 128:]
        return carry

    lax.fori_loop(0, 32, step, 0)
    out[...] = wide[...].astype(BF)


VM = pl.BlockSpec(memory_space=pltpu.VMEM)
SM = pl.BlockSpec(memory_space=pltpu.SMEM)
BLOCK = jax.ShapeDtypeStruct((256, 128), BF)
MIB = 1024 * 1024


def cost(us):
    return pl.CostEstimate(flops=0, bytes_accessed=int(us * 3.0e6), transcendentals=0)


def call(kernel, ins, outs, scratch=(), name=None, mib=16, us=1.0, smem=1):
    return pl.pallas_call(
        kernel,
        out_shape=outs,
        in_specs=[SM] * smem + [VM] * (len(ins) - smem),
        out_specs=jax.tree.map(lambda _: VM, outs),
        scratch_shapes=list(scratch),
        compiler_params=pltpu.CompilerParams(vmem_limit_bytes=mib * MIB),
        cost_estimate=cost(us),
        name=name,
    )(*ins)


def exchange(blocks, axes):
    pairs = [[(a, a ^ s) for a in range(4)] for s in range(4)]
    return [blocks[0]] + [lax.ppermute(blocks[s], axes, pairs[s]) for s in (1, 2, 3)]


def sum_over(part, axes):
    for axis, size in axes:
        step = 1
        while step < size:
            part = part + lax.ppermute(part, axis, [(a, a ^ step) for a in range(size)])
            step *= 2
    return part


def fast(field, cotangent, mode_weight, skip_weight, lift_weight, proj_weight):
    chans, xrows, yrows, zlen = field.shape
    tables = make_tables(zlen, yrows * 4, xrows * 4, 4, xrows, yrows)
    zf, zi, yf, yi, xf, xr, xi, xd = [jnp.asarray(t) for t in tables]
    gyc = ("gy", "col")
    idx = jnp.stack([lax.axis_index(gyc), lax.axis_index("gx")]).astype(jnp.int32)
    four = [BLOCK] * 4
    cells = chans * xrows * yrows
    flat_field = field.reshape(cells, zlen)
    flat_cot = cotangent.reshape(cells, zlen)
    rows = chans * xrows
    wide = pltpu.VMEM((cells, zlen), F32)
    tall = pltpu.VMEM((yrows, rows, zlen), F32)
    weight = mode_weight.reshape(2, chans, chans, 64, 32)

    packed = pl.pallas_call(
        pack_kernel,
        grid=(8,),
        out_shape=jax.ShapeDtypeStruct((8, 2, chans, 64, 128), BF),
        in_specs=[pl.BlockSpec((2, 4, chans, 64, 32), lambda g: (0, g, 0, 0, 0))],
        out_specs=pl.BlockSpec((1, 2, chans, 64, 128), lambda g: (g, 0, 0, 0, 0)),
        compiler_params=pltpu.CompilerParams(vmem_limit_bytes=20 * MIB),
        cost_estimate=cost(12.0),
        name="pack",
    )(weight)

    sent = call(
        functools.partial(z_forward_kernel, rows, yrows, zlen),
        (idx, flat_field, zf), four, [wide], "z_forward", 8, 2.0,
    )
    got = exchange(sent, gyc)
    fx, cx = call(
        functools.partial(cells_kernel, yrows),
        (flat_field, flat_cot),
        [jax.ShapeDtypeStruct((32, chans, 256), BF)] * 2, [wide], "cells", 8, 2.0, 0,
    )
    sent = call(functools.partial(lane_kernel, 0, 1), (idx, *got, yf), four, (), "y_forward", 8, 1.0)
    got = exchange(sent, "gx")
    modes, *sent = call(
        mix_forward_kernel, (idx, *got, xf, xi, packed),
        [jax.ShapeDtypeStruct((8, 2, 64, 128), BF)] + four, (), "mix_forward", 16, 5.0,
    )
    got = exchange(sent, "gx")
    sent = call(functools.partial(lane_kernel, 1, 0), (idx, *got, yi), four, (), "y_inverse", 8, 1.0)
    got = exchange(sent, gyc)
    *sent, pg, sums = call(
        point_kernel,
        (idx, *got, zi, zf, fx, cx, skip_weight, lift_weight, lift_weight.T, proj_weight.T),
        four + [
            jax.ShapeDtypeStruct((32, chans, 256), BF),
            jax.ShapeDtypeStruct((288, 96), F32),
        ],
        [tall, tall], "point", 16, 8.0,
    )
    got = exchange(sent, gyc)
    part = jnp.concatenate(
        [sums[:128, :32], sums[128:256, 32:64], sums[256:, 64:]], axis=0
    ).reshape(72, 128)
    part = sum_over(part, (("col", 2), ("gy", 2), ("gx", 4))).reshape(288, 32)
    proj_grad, lift_grad, skip_grad = part[:128].T, part[128:256], part[256:]
    sent = call(functools.partial(lane_kernel, 0, 1), (idx, *got, yf), four, (), "y_forward", 8, 1.0)
    got = exchange(sent, "gx")
    pmodes, *sent = call(
        mix_backward_kernel, (idx, *got, xr, xd, packed),
        [jax.ShapeDtypeStruct((32, 2, 64, 128), BF)] + four, (), "mix_backward", 16, 5.0,
    )
    got = exchange(sent, "gx")
    mode_grad = pl.pallas_call(
        outer_kernel,
        grid=(8,),
        out_shape=jax.ShapeDtypeStruct((2, chans, chans, 64, 32), BF),
        in_specs=[
            pl.BlockSpec((1, 2, 64, 128), lambda g: (g, 0, 0, 0)),
            pl.BlockSpec((32, 2, 64, 128), lambda g: (0, 0, 0, 0)),
        ],
        out_specs=pl.BlockSpec((2, 4, chans, 64, 32), lambda g: (0, g, 0, 0, 0)),
        compiler_params=pltpu.CompilerParams(vmem_limit_bytes=20 * MIB),
        cost_estimate=cost(12.0),
        name="outer",
    )(modes, pmodes)
    sent = call(functools.partial(lane_kernel, 1, 0), (idx, *got, yi), four, (), "y_inverse", 8, 1.0)
    got = exchange(sent, gyc)
    field_grad = call(
        finish_kernel, (idx, *got, zi, pg, skip_weight.T),
        jax.ShapeDtypeStruct((cells, zlen), BF), [tall, wide], "finish", 8, 2.0,
    )
    return (
        field_grad.reshape(field.shape),
        mode_grad.reshape(mode_weight.shape),
        skip_grad,
        lift_grad,
        proj_grad,
    )


def fits(field, mode_weight):
    sizes = [lax.axis_size(a) for a in ("gx", "gy", "col")]
    return (
        sizes == [4, 2, 2]
        and field.shape == (32, 8, 8, 128)
        and mode_weight.shape == (2, 32, 32, 8, 8, 32)
    )


def on_device(*args):
    return fast(*args) if fits(args[0], args[2]) else general(*args)


def solution(mesh):
    in_specs = (
        P("grp", "gx", ("gy", "col"), None),
        P("grp", "gx", ("gy", "col"), None),
        P(None, None, None, ("gy", "col"), "gx", None),
        P(),
        P(),
        P(),
    )
    out_specs = (
        P("grp", "gx", ("gy", "col"), None),
        P("grp", None, None, ("gy", "col"), "gx", None),
        P("grp", None),
        P("grp", None),
        P("grp", None),
    )
    return jax.shard_map(
        on_device, mesh=mesh, in_specs=in_specs, out_specs=out_specs, check_vma=False
    )
```

profile of v0, /device:TPU:0, one launch (start us, length us, event | category | flops | bytes accessed | tf_op | source)
XLA Modules:
  0.0 178.4 jit_solution(11702622576152036486)
XLA Ops:
  0.7 1.2 copy-done.2
  4.6 2.6 %collective-permute-start.1 = (bf16[256,128]{1,0:T(8,128)(2,1)S(1)}, bf16[256,128]{1,0:T(8,128)(2,1)S(1)}, u32[]{:S(2)}, u32[]{:S(2)}) collective-permute-start(bf16[256,128]{1,0:T(8,128)(2,1)S(1)} %get-tuple-element.45), channel_id=1, source_target_pairs={{0,2},{1,3},{2,0},{3,1},{4,6},{5,7},{6,4},{7,5},{8,10},{9,11},{10,... | collective-permute-start | bytes 196616 | tf_op jit(solution)/shard_map/ppermute | solution.py:443
  7.2 2.6 %collective-permute-done.1.r2 = bf16[256,128]{1,0:T(8,128)(2,1)S(1)} collective-permute-done((bf16[256,128]{1,0:T(8,128)(2,1)S(1)}, bf16[256,128]{1,0:T(8,128)(2,1)S(1)}, u32[]{:S(2)}, u32[]{:S(2)}) %collective-permute-start.1) | collective-permute-done | bytes 65568 | tf_op jit(solution)/shard_map/ppermute | solution.py:443
  9.8 1.4 collective-permute-done.2.r3
  11.2 1.0 copy-done.8
  13.1 1.6 collective-permute-start.3
  14.7 2.6 %collective-permute-start.4 = (bf16[256,128]{1,0:T(8,128)(2,1)S(1)}, bf16[256,128]{1,0:T(8,128)(2,1)S(1)}, u32[]{:S(2)}, u32[]{:S(2)}) collective-permute-start(bf16[256,128]{1,0:T(8,128)(2,1)S(1)} %get-tuple-element.49), channel_id=1, source_target_pairs={{0,8},{4,12},{8,0},{12,4},{1,9},{5,13},{9,1},{13,5},{2,10},{6,14},... | collective-permute-start | bytes 196616 | tf_op jit(solution)/shard_map/ppermute | solution.py:443
  17.5 26.4 %pack.1.weight = bf16[8,2,32,64,128]{4,3,2,1,0:T(8,128)(2,1)S(1)} custom-call(bf16[2,32,32,64,32]{4,3,2,1,0:T(8,128)(2,1)} %bitcast.17), custom_call_target="tpu_custom_call" | custom-call | bytes 36000000 | tf_op jit(solution)/shard_map/pack/pallas_call | solution.py:470
  44.0 5.8 %mix_forward.1 = (bf16[8,2,64,128]{3,2,1,0:T(8,128)(2,1)S(1)}, bf16[256,128]{1,0:T(8,128)(2,1)S(1)}, bf16[256,128]{1,0:T(8,128)(2,1)S(1)}, bf16[256,128]{1,0:T(8,128)(2,1)S(1)}, bf16[256,128]{1,0:T(8,128)(2,1)S(1)}) custom-call(s32[2]{0:T(128)S(1)} %pad_add_fusion.idx, bf16[256,128]{1,0:T(8,128)(2,1)S(1)} %get-tuple-element.47.r0, ...), custom_call_target="tpu_custom_call" | custom-call | bytes 15000000 | tf_op jit(solution)/shard_map/mix_forward/pallas_call | solution.py:429
  49.8 3.4 %copy-done = bf16[8,2,32,64,128]{4,3,2,1,0:T(8,128)(2,1)} copy-done((bf16[8,2,32,64,128]{4,3,2,1,0:T(8,128)(2,1)}, bf16[8,2,32,64,128]{4,3,2,1,0:T(8,128)(2,1)S(1)}, u32[]{:S(2)}) %copy-start) | copy-done | bytes 8388632
  53.9 3.5 %collective-permute-start.7 = (bf16[256,128]{1,0:T(8,128)(2,1)S(1)}, bf16[256,128]{1,0:T(8,128)(2,1)S(1)}, u32[]{:S(2)}, u32[]{:S(2)}) collective-permute-start(bf16[256,128]{1,0:T(8,128)(2,1)S(1)} %get-tuple-element.53), channel_id=1, source_target_pairs={{0,8},{4,12},{8,0},{12,4},{1,9},{5,13},{9,1},{13,5},{2,10},{6,14},... | collective-permute-start | bytes 196616 | tf_op jit(solution)/shard_map/ppermute | solution.py:443
  58.0 3.5 %collective-permute-done.7.r2 = bf16[256,128]{1,0:T(8,128)(2,1)S(1)} collective-permute-done((bf16[256,128]{1,0:T(8,128)(2,1)S(1)}, bf16[256,128]{1,0:T(8,128)(2,1)S(1)}, u32[]{:S(2)}, u32[]{:S(2)}) %collective-permute-start.7) | collective-permute-done | bytes 65568 | tf_op jit(solution)/shard_map/ppermute | solution.py:443
  61.5 2.0 %collective-permute-done.8.r3 = bf16[256,128]{1,0:T(8,128)(2,1)S(1)} collective-permute-done((bf16[256,128]{1,0:T(8,128)(2,1)S(1)}, bf16[256,128]{1,0:T(8,128)(2,1)S(1)}, u32[]{:S(2)}, u32[]{:S(2)}) %collective-permute-start.8) | collective-permute-done | bytes 65568 | tf_op jit(solution)/shard_map/ppermute | solution.py:443
  63.5 1.5 y_inverse.2
  65.6 1.4 collective-permute-start.10
  68.8 1.7 cells.1
  73.1 21.9 %point.1 = (bf16[256,128]{1,0:T(8,128)(2,1)S(1)}, bf16[256,128]{1,0:T(8,128)(2,1)}, bf16[256,128]{1,0:T(8,128)(2,1)}, bf16[256,128]{1,0:T(8,128)(2,1)}, bf16[32,...) custom-call(s32[2]{0:T(128)S(1)} %pad_add_fusion.idx, bf16[256,128]{1,0:T(8,128)(2,1)S(1)} %copy-done.15, ...), custom_call_target="tpu_custom_call" | custom-call | bytes 24000000 | tf_op jit(solution)/shard_map/point/pallas_call | solution.py:429
  95.7 1.3 collective-permute-start.13
  98.0 2.5 %collective-permute-done.13.r2 = bf16[256,128]{1,0:T(8,128)(2,1)S(1)} collective-permute-done((bf16[256,128]{1,0:T(8,128)(2,1)}, bf16[256,128]{1,0:T(8,128)(2,1)S(1)}, u32[]{:S(2)}, u32[]{:S(2)}) %collective-permute-start.13) | collective-permute-done | bytes 65568 | tf_op jit(solution)/shard_map/ppermute | solution.py:443
  100.5 1.1 collective-permute-done.14.r3
  101.6 1.0 copy-done.9
  104.4 1.6 collective-permute-start.16
  106.0 2.8 %collective-permute-start.17 = (bf16[256,128]{1,0:T(8,128)(2,1)S(1)}, bf16[256,128]{1,0:T(8,128)(2,1)S(1)}, u32[]{:S(2)}, u32[]{:S(2)}) collective-permute-start(bf16[256,128]{1,0:T(8,128)(2,1)S(1)} %get-tuple-element.68), channel_id=1, source_target_pairs={{0,12},{4,8},{8,4},{12,0},{1,13},{5,9},{9,5},{13,1},{2,14},{6,10},... | collective-permute-start | bytes 196616 | tf_op jit(solution)/shard_map/ppermute | solution.py:443
  109.6 3.2 %collective-permute-done.25 = f32[72,128]{1,0:T(8,128)S(1)} collective-permute-done((f32[72,128]{1,0:T(8,128)S(1)}, f32[72,128]{1,0:T(8,128)S(1)}, u32[]{:S(2)}, u32[]{:S(2)}) %collective-permute-start.25) | collective-permute-done | bytes 36896 | tf_op jit(solution)/shard_map/ppermute | solution.py:450
  113.1 3.4 %copy-done.1 = bf16[8,2,32,64,128]{4,3,2,1,0:T(8,128)(2,1)S(1)} copy-done((bf16[8,2,32,64,128]{4,3,2,1,0:T(8,128)(2,1)S(1)}, bf16[8,2,32,64,128]{4,3,2,1,0:T(8,128)(2,1)}, u32[]{:S(2)}) %copy-start.1) | copy-done | bytes 8388632
  117.5 5.4 %mix_backward.1 = (bf16[32,2,64,128]{3,2,1,0:T(8,128)(2,1)S(1)}, bf16[256,128]{1,0:T(8,128)(2,1)S(1)}, bf16[256,128]{1,0:T(8,128)(2,1)}, bf16[256,128]{1,0:T(8,128)(2,1)}, bf16[256,128]{1,0:T(8,128)(2,1)}) custom-call(s32[2]{0:T(128)S(1)} %pad_add_fusion.idx, bf16[256,128]{1,0:T(8,128)(2,1)S(1)} %get-tuple-element.65.r0, ...), custom_call_target="tpu_custom_call" | custom-call | bytes 15000000 | tf_op jit(solution)/shard_map/mix_backward/pallas_call | solution.py:429
  123.5 1.8 %collective-permute-start.18 = (bf16[256,128]{1,0:T(8,128)(2,1)}, bf16[256,128]{1,0:T(8,128)(2,1)S(1)}, u32[]{:S(2)}, u32[]{:S(2)}) collective-permute-start(bf16[256,128]{1,0:T(8,128)(2,1)} %get-tuple-element.70), channel_id=1, source_target_pairs={{0,4},{4,0},{8,12},{12,8},{1,5},{5,1},{9,13},{13,9},{2,6},{6,2},{1... | collective-permute-start | bytes 196616 | tf_op jit(solution)/shard_map/ppermute | solution.py:443
  126.0 1.9 %collective-permute-start.20 = (bf16[256,128]{1,0:T(8,128)(2,1)}, bf16[256,128]{1,0:T(8,128)(2,1)}, u32[]{:S(2)}, u32[]{:S(2)}) collective-permute-start(bf16[256,128]{1,0:T(8,128)(2,1)} %get-tuple-element.72), channel_id=1, source_target_pairs={{0,12},{4,8},{8,4},{12,0},{1,13},{5,9},{9,5},{13,1},{2,14},{6,10},... | collective-permute-start | bytes 196616 | tf_op jit(solution)/shard_map/ppermute | solution.py:443
  130.1 33.8 %outer.1 = bf16[2,32,32,64,32]{4,3,2,1,0:T(8,128)(2,1)} custom-call(bf16[8,2,64,128]{3,2,1,0:T(8,128)(2,1)S(1)} %get-tuple-element.78.modes, bf16[32,2,64,128]{3,2,1,0:T(8,128)(2,1)S(1)} %get-tuple-element.79.pmodes), custom_call_target="tpu_custom_call" | custom-call | bytes 36000000 | tf_op jit(solution)/shard_map/outer/pallas_call | solution.py:522
  164.7 1.2 y_inverse.3
  166.0 1.3 collective-permute-start.22
  171.6 6.8 %finish.1 = bf16[2048,128]{1,0:T(8,128)(2,1)} custom-call(s32[2]{0:T(128)S(1)} %pad_add_fusion.idx, bf16[256,128]{1,0:T(8,128)(2,1)S(1)} %get-tuple-element.73.r0, bf16[256,128]{1,0:T(8,128)(2,1)S(1)} %collective-permute-done.21.r1, bf16[256,128]{1,0:T(8,128)(2,1)S(1)} %collective-permute-done.22.r2, bf16[256,128]{1,0:T(8,128)(2,1)S(1)} %collective-permute-done.23.r3, ...), custom_call_target="tpu_custom_call" | custom-call | bytes 6000000 | tf_op jit(solution)/shard_map/finish/pallas_call | solution.py:429
  (103 shorter events, 24.4 us)
Async XLA Ops:
  0.6 66.9 %copy-start.21 = (bf16[128,32]{0,1:T(8,128)(2,1)S(1)}, bf16[128,32]{0,1:T(8,128)(2,1)}, u32[]{:S(2)}) copy-start(bf16[128,32]{0,1:T(8,128)(2,1)} %param.18) | copy-start | bytes 24580
  3.0 68.6 %copy-start.3 = (bf16[4,1024,128]{2,1,0:T(8,128)(2,1)S(1)}, bf16[4,1024,128]{2,1,0:T(8,128)(2,1)}, u32[]{:S(2)}) copy-start(bf16[4,1024,128]{2,1,0:T(8,128)(2,1)} %constant.29.clone.zf) | copy-start | bytes 3145732
  3.0 68.6 %copy-start.4 = (bf16[4,128,1024]{2,1,0:T(8,128)(2,1)S(1)}, bf16[4,128,1024]{2,1,0:T(8,128)(2,1)}, u32[]{:S(2)}) copy-start(bf16[4,128,1024]{2,1,0:T(8,128)(2,1)} %constant.30.clone.zi) | copy-start | bytes 3145732
  4.0 3.2 %collective-permute-start = (bf16[256,128]{1,0:T(8,128)(2,1)S(1)}, bf16[256,128]{1,0:T(8,128)(2,1)S(1)}, u32[]{:S(2)}, u32[]{:S(2)}) collective-permute-start(bf16[256,128]{1,0:T(8,128)(2,1)S(1)} %get-tuple-element.44), channel_id=1, source_target_pairs={{0,1},{1,0},{2,3},{3,2},{4,5},{5,4},{6,7},{7,6},{8,9},{9,8},{10,11... | collective-permute-start | bytes 196616 | tf_op jit(solution)/shard_map/ppermute | solution.py:443
  4.6 5.3 %collective-permute-start.1 = (bf16[256,128]{1,0:T(8,128)(2,1)S(1)}, bf16[256,128]{1,0:T(8,128)(2,1)S(1)}, u32[]{:S(2)}, u32[]{:S(2)}) collective-permute-start(bf16[256,128]{1,0:T(8,128)(2,1)S(1)} %get-tuple-element.45), channel_id=1, source_target_pairs={{0,2},{1,3},{2,0},{3,1},{4,6},{5,7},{6,4},{7,5},{8,10},{9,11},{10,... | collective-permute-start | bytes 196616 | tf_op jit(solution)/shard_map/ppermute | solution.py:443
  7.1 4.0 %collective-permute-start.2 = (bf16[256,128]{1,0:T(8,128)(2,1)S(1)}, bf16[256,128]{1,0:T(8,128)(2,1)S(1)}, u32[]{:S(2)}, u32[]{:S(2)}) collective-permute-start(bf16[256,128]{1,0:T(8,128)(2,1)S(1)} %get-tuple-element.46), channel_id=1, source_target_pairs={{0,3},{1,2},{2,1},{3,0},{4,7},{5,6},{6,5},{7,4},{8,11},{9,10},{10,... | collective-permute-start | bytes 196616 | tf_op jit(solution)/shard_map/ppermute | solution.py:443
  12.2 100.8 %copy-start.13 = (bf16[4,32,256]{2,1,0:T(8,128)(2,1)S(1)}, bf16[4,32,256]{2,1,0:T(8,128)(2,1)}, u32[]{:S(2)}) copy-start(bf16[4,32,256]{2,1,0:T(8,128)(2,1)} %constant.36.clone.xd) | copy-start | bytes 196612
  13.1 30.9 %collective-permute-start.3 = (bf16[256,128]{1,0:T(8,128)(2,1)S(1)}, bf16[256,128]{1,0:T(8,128)(2,1)S(1)}, u32[]{:S(2)}, u32[]{:S(2)}) collective-permute-start(bf16[256,128]{1,0:T(8,128)(2,1)S(1)} %get-tuple-element.48), channel_id=1, source_target_pairs={{0,4},{4,0},{8,12},{12,8},{1,5},{5,1},{9,13},{13,9},{2,6},{6,2},{1... | collective-permute-start | bytes 196616 | tf_op jit(solution)/shard_map/ppermute | solution.py:443
  14.7 29.3 %collective-permute-start.4 = (bf16[256,128]{1,0:T(8,128)(2,1)S(1)}, bf16[256,128]{1,0:T(8,128)(2,1)S(1)}, u32[]{:S(2)}, u32[]{:S(2)}) collective-permute-start(bf16[256,128]{1,0:T(8,128)(2,1)S(1)} %get-tuple-element.49), channel_id=1, source_target_pairs={{0,8},{4,12},{8,0},{12,4},{1,9},{5,13},{9,1},{13,5},{2,10},{6,14},... | collective-permute-start | bytes 196616 | tf_op jit(solution)/shard_map/ppermute | solution.py:443
  17.3 26.7 %collective-permute-start.5 = (bf16[256,128]{1,0:T(8,128)(2,1)S(1)}, bf16[256,128]{1,0:T(8,128)(2,1)S(1)}, u32[]{:S(2)}, u32[]{:S(2)}) collective-permute-start(bf16[256,128]{1,0:T(8,128)(2,1)S(1)} %get-tuple-element.50), channel_id=1, source_target_pairs={{0,12},{4,8},{8,4},{12,0},{1,13},{5,9},{9,5},{13,1},{2,14},{6,10},... | collective-permute-start | bytes 196616 | tf_op jit(solution)/shard_map/ppermute | solution.py:443
  53.2 4.8 %collective-permute-start.6 = (bf16[256,128]{1,0:T(8,128)(2,1)S(1)}, bf16[256,128]{1,0:T(8,128)(2,1)S(1)}, u32[]{:S(2)}, u32[]{:S(2)}) collective-permute-start(bf16[256,128]{1,0:T(8,128)(2,1)S(1)} %get-tuple-element.52), channel_id=1, source_target_pairs={{0,4},{4,0},{8,12},{12,8},{1,5},{5,1},{9,13},{13,9},{2,6},{6,2},{1... | collective-permute-start | bytes 196616 | tf_op jit(solution)/shard_map/ppermute | solution.py:443
  53.9 7.6 %collective-permute-start.7 = (bf16[256,128]{1,0:T(8,128)(2,1)S(1)}, bf16[256,128]{1,0:T(8,128)(2,1)S(1)}, u32[]{:S(2)}, u32[]{:S(2)}) collective-permute-start(bf16[256,128]{1,0:T(8,128)(2,1)S(1)} %get-tuple-element.53), channel_id=1, source_target_pairs={{0,8},{4,12},{8,0},{12,4},{1,9},{5,13},{9,1},{13,5},{2,10},{6,14},... | collective-permute-start | bytes 196616 | tf_op jit(solution)/shard_map/ppermute | solution.py:443
  57.4 6.1 %collective-permute-start.8 = (bf16[256,128]{1,0:T(8,128)(2,1)S(1)}, bf16[256,128]{1,0:T(8,128)(2,1)S(1)}, u32[]{:S(2)}, u32[]{:S(2)}) collective-permute-start(bf16[256,128]{1,0:T(8,128)(2,1)S(1)} %get-tuple-element.54), channel_id=1, source_target_pairs={{0,12},{4,8},{8,4},{12,0},{1,13},{5,9},{9,5},{13,1},{2,14},{6,10},... | collective-permute-start | bytes 196616 | tf_op jit(solution)/shard_map/ppermute | solution.py:443
  65.6 4.9 %collective-permute-start.9 = (bf16[256,128]{1,0:T(8,128)(2,1)}, bf16[256,128]{1,0:T(8,128)(2,1)}, u32[]{:S(2)}, u32[]{:S(2)}) collective-permute-start(bf16[256,128]{1,0:T(8,128)(2,1)} %get-tuple-element.56), channel_id=1, source_target_pairs={{0,1},{1,0},{2,3},{3,2},{4,5},{5,4},{6,7},{7,6},{8,9},{9,8},{10,11... | collective-permute-start | bytes 196616 | tf_op jit(solution)/shard_map/ppermute | solution.py:443
  65.6 5.0 %collective-permute-start.10 = (bf16[256,128]{1,0:T(8,128)(2,1)}, bf16[256,128]{1,0:T(8,128)(2,1)}, u32[]{:S(2)}, u32[]{:S(2)}) collective-permute-start(bf16[256,128]{1,0:T(8,128)(2,1)} %get-tuple-element.57), channel_id=1, source_target_pairs={{0,2},{1,3},{2,0},{3,1},{4,6},{5,7},{6,4},{7,5},{8,10},{9,11},{10,... | collective-permute-start | bytes 196616 | tf_op jit(solution)/shard_map/ppermute | solution.py:443
  66.9 4.6 %collective-permute-start.11 = (bf16[256,128]{1,0:T(8,128)(2,1)}, bf16[256,128]{1,0:T(8,128)(2,1)}, u32[]{:S(2)}, u32[]{:S(2)}) collective-permute-start(bf16[256,128]{1,0:T(8,128)(2,1)} %get-tuple-element.58), channel_id=1, source_target_pairs={{0,3},{1,2},{2,1},{3,0},{4,7},{5,6},{6,5},{7,4},{8,11},{9,10},{10,... | collective-permute-start | bytes 196616 | tf_op jit(solution)/shard_map/ppermute | solution.py:443
  95.6 2.4 %collective-permute-start.12 = (bf16[256,128]{1,0:T(8,128)(2,1)}, bf16[256,128]{1,0:T(8,128)(2,1)S(1)}, u32[]{:S(2)}, u32[]{:S(2)}) collective-permute-start(bf16[256,128]{1,0:T(8,128)(2,1)} %get-tuple-element.62), channel_id=1, source_target_pairs={{0,1},{1,0},{2,3},{3,2},{4,5},{5,4},{6,7},{7,6},{8,9},{9,8},{10,11... | collective-permute-start | bytes 196616 | tf_op jit(solution)/shard_map/ppermute | solution.py:443
  95.7 4.8 %collective-permute-start.13 = (bf16[256,128]{1,0:T(8,128)(2,1)}, bf16[256,128]{1,0:T(8,128)(2,1)S(1)}, u32[]{:S(2)}, u32[]{:S(2)}) collective-permute-start(bf16[256,128]{1,0:T(8,128)(2,1)} %get-tuple-element.63), channel_id=1, source_target_pairs={{0,2},{1,3},{2,0},{3,1},{4,6},{5,7},{6,4},{7,5},{8,10},{9,11},{10,... | collective-permute-start | bytes 196616 | tf_op jit(solution)/shard_map/ppermute | solution.py:443
  97.0 4.6 %collective-permute-start.14 = (bf16[256,128]{1,0:T(8,128)(2,1)}, bf16[256,128]{1,0:T(8,128)(2,1)S(1)}, u32[]{:S(2)}, u32[]{:S(2)}) collective-permute-start(bf16[256,128]{1,0:T(8,128)(2,1)} %get-tuple-element.64), channel_id=1, source_target_pairs={{0,3},{1,2},{2,1},{3,0},{4,7},{5,6},{6,5},{7,4},{8,11},{9,10},{10,... | collective-permute-start | bytes 196616 | tf_op jit(solution)/shard_map/ppermute | solution.py:443
  97.6 11.2 %collective-permute-start.24 = (f32[72,128]{1,0:T(8,128)S(1)}, f32[72,128]{1,0:T(8,128)S(1)}, u32[]{:S(2)}, u32[]{:S(2)}) collective-permute-start(f32[72,128]{1,0:T(8,128)S(1)} %reshape.37), channel_id=1, source_target_pairs={{0,1},{1,0},{2,3},{3,2},{4,5},{5,4},{6,7},{7,6},{8,9},{9,8},{10,11... | collective-permute-start | bytes 110600 | tf_op jit(solution)/shard_map/ppermute | solution.py:450
  104.3 8.5 %collective-permute-start.15 = (bf16[256,128]{1,0:T(8,128)(2,1)S(1)}, bf16[256,128]{1,0:T(8,128)(2,1)S(1)}, u32[]{:S(2)}, u32[]{:S(2)}) collective-permute-start(bf16[256,128]{1,0:T(8,128)(2,1)S(1)} %get-tuple-element.66), channel_id=1, source_target_pairs={{0,4},{4,0},{8,12},{12,8},{1,5},{5,1},{9,13},{13,9},{2,6},{6,2},{1... | collective-permute-start | bytes 196616 | tf_op jit(solution)/shard_map/ppermute | solution.py:443
  104.4 8.7 %collective-permute-start.16 = (bf16[256,128]{1,0:T(8,128)(2,1)S(1)}, bf16[256,128]{1,0:T(8,128)(2,1)S(1)}, u32[]{:S(2)}, u32[]{:S(2)}) collective-permute-start(bf16[256,128]{1,0:T(8,128)(2,1)S(1)} %get-tuple-element.67), channel_id=1, source_target_pairs={{0,8},{4,12},{8,0},{12,4},{1,9},{5,13},{9,1},{13,5},{2,10},{6,14},... | collective-permute-start | bytes 196616 | tf_op jit(solution)/shard_map/ppermute | solution.py:443
  106.0 7.0 %collective-permute-start.17 = (bf16[256,128]{1,0:T(8,128)(2,1)S(1)}, bf16[256,128]{1,0:T(8,128)(2,1)S(1)}, u32[]{:S(2)}, u32[]{:S(2)}) collective-permute-start(bf16[256,128]{1,0:T(8,128)(2,1)S(1)} %get-tuple-element.68), channel_id=1, source_target_pairs={{0,12},{4,8},{8,4},{12,0},{1,13},{5,9},{9,5},{13,1},{2,14},{6,10},... | collective-permute-start | bytes 196616 | tf_op jit(solution)/shard_map/ppermute | solution.py:443
  108.8 4.0 %collective-permute-start.25 = (f32[72,128]{1,0:T(8,128)S(1)}, f32[72,128]{1,0:T(8,128)S(1)}, u32[]{:S(2)}, u32[]{:S(2)}) collective-permute-start(f32[72,128]{1,0:T(8,128)S(1)} %add.16), channel_id=1, source_target_pairs={{0,2},{2,0},{1,3},{3,1},{4,6},{6,4},{5,7},{7,5},{8,10},{10,8},{9,1... | collective-permute-start | bytes 110600 | tf_op jit(solution)/shard_map/ppermute | solution.py:450
  112.8 15.1 %collective-permute-start.26 = (f32[72,128]{1,0:T(8,128)S(1)}, f32[72,128]{1,0:T(8,128)S(1)}, u32[]{:S(2)}, u32[]{:S(2)}) collective-permute-start(f32[72,128]{1,0:T(8,128)S(1)} %add.17), channel_id=1, source_target_pairs={{0,4},{4,0},{8,12},{12,8},{1,5},{5,1},{9,13},{13,9},{2,6},{6,2},{1... | collective-permute-start | bytes 110600 | tf_op jit(solution)/shard_map/ppermute | solution.py:450
  123.5 41.2 %collective-permute-start.18 = (bf16[256,128]{1,0:T(8,128)(2,1)}, bf16[256,128]{1,0:T(8,128)(2,1)S(1)}, u32[]{:S(2)}, u32[]{:S(2)}) collective-permute-start(bf16[256,128]{1,0:T(8,128)(2,1)} %get-tuple-element.70), channel_id=1, source_target_pairs={{0,4},{4,0},{8,12},{12,8},{1,5},{5,1},{9,13},{13,9},{2,6},{6,2},{1... | collective-permute-start | bytes 196616 | tf_op jit(solution)/shard_map/ppermute | solution.py:443
  125.3 39.4 %collective-permute-start.19 = (bf16[256,128]{1,0:T(8,128)(2,1)}, bf16[256,128]{1,0:T(8,128)(2,1)}, u32[]{:S(2)}, u32[]{:S(2)}) collective-permute-start(bf16[256,128]{1,0:T(8,128)(2,1)} %get-tuple-element.71), channel_id=1, source_target_pairs={{0,8},{4,12},{8,0},{12,4},{1,9},{5,13},{9,1},{13,5},{2,10},{6,14},... | collective-permute-start | bytes 196616 | tf_op jit(solution)/shard_map/ppermute | solution.py:443
  126.0 38.7 %collective-permute-start.20 = (bf16[256,128]{1,0:T(8,128)(2,1)}, bf16[256,128]{1,0:T(8,128)(2,1)}, u32[]{:S(2)}, u32[]{:S(2)}) collective-permute-start(bf16[256,128]{1,0:T(8,128)(2,1)} %get-tuple-element.72), channel_id=1, source_target_pairs={{0,12},{4,8},{8,4},{12,0},{1,13},{5,9},{9,5},{13,1},{2,14},{6,10},... | collective-permute-start | bytes 196616 | tf_op jit(solution)/shard_map/ppermute | solution.py:443
  128.5 35.3 %collective-permute-start.27 = (f32[72,128]{1,0:T(8,128)}, f32[72,128]{1,0:T(8,128)}, u32[]{:S(2)}, u32[]{:S(2)}) collective-permute-start(f32[72,128]{1,0:T(8,128)} %add.18), channel_id=1, source_target_pairs={{0,8},{4,12},{8,0},{12,4},{1,9},{5,13},{9,1},{13,5},{2,10},{6,14},... | collective-permute-start | bytes 110600 | tf_op jit(solution)/shard_map/ppermute | solution.py:450
  165.9 4.2 %collective-permute-start.21 = (bf16[256,128]{1,0:T(8,128)(2,1)S(1)}, bf16[256,128]{1,0:T(8,128)(2,1)S(1)}, u32[]{:S(2)}, u32[]{:S(2)}) collective-permute-start(bf16[256,128]{1,0:T(8,128)(2,1)S(1)} %get-tuple-element.74), channel_id=1, source_target_pairs={{0,1},{1,0},{2,3},{3,2},{4,5},{5,4},{6,7},{7,6},{8,9},{9,8},{10,11... | collective-permute-start | bytes 196616 | tf_op jit(solution)/shard_map/ppermute | solution.py:443
  166.0 4.8 %collective-permute-start.22 = (bf16[256,128]{1,0:T(8,128)(2,1)S(1)}, bf16[256,128]{1,0:T(8,128)(2,1)S(1)}, u32[]{:S(2)}, u32[]{:S(2)}) collective-permute-start(bf16[256,128]{1,0:T(8,128)(2,1)S(1)} %get-tuple-element.75), channel_id=1, source_target_pairs={{0,2},{1,3},{2,0},{3,1},{4,6},{5,7},{6,4},{7,5},{8,10},{9,11},{10,... | collective-permute-start | bytes 196616 | tf_op jit(solution)/shard_map/ppermute | solution.py:443
  167.3 4.3 %collective-permute-start.23 = (bf16[256,128]{1,0:T(8,128)(2,1)S(1)}, bf16[256,128]{1,0:T(8,128)(2,1)S(1)}, u32[]{:S(2)}, u32[]{:S(2)}) collective-permute-start(bf16[256,128]{1,0:T(8,128)(2,1)S(1)} %get-tuple-element.76), channel_id=1, source_target_pairs={{0,3},{1,2},{2,1},{3,0},{4,7},{5,6},{6,5},{7,4},{8,11},{9,10},{10,... | collective-permute-start | bytes 196616 | tf_op jit(solution)/shard_map/ppermute | solution.py:443
  (20 other events, 314.2 us)
where the time goes:
time: 179 us; the launch traced here: 178 us
  Pallas kernels  107 us (60%)
  starting transfers between devices  28.6 us (16%)
  local copies, waits for them, and re-layouts  20.8 us (12%)
  waiting for transfers between devices  19.5 us (11%)
    pallas_call x10, Pallas kernels, call(): pl.pallas_call(kernel, out_shape=outs, in_specs=[SM] * smem + [VM] * (len...  46.9 us
    pallas_call x1, Pallas kernels, fast(): pl.pallas_call(outer_kernel, grid=(8,), out_shape=jax.ShapeDtypeStruct((2...  33.8 us
    ppermute x24, starting transfers between devices, exchange(): lax.ppermute(blocks[s], axes, pairs[s])  26.5 us
    pallas_call x1, Pallas kernels, fast(): pl.pallas_call(pack_kernel, grid=(8,), out_shape=jax.ShapeDtypeStruct((8,...  26.4 us
    unnamed x53, local copies, waits for them, and re-layouts  19.7 us
    ppermute x24, waiting for transfers between devices, exchange(): lax.ppermute(blocks[s], axes, pairs[s])  16.3 us
  transfers between devices with their start and end apart: 28, of which 13 were waited for; matrix products, arithmetic and copies ran while one was open for 3% of the time, Pallas kernels for 38%

commit v1 on v0

--- a/solution.py
+++ b/solution.py
@@ -214,18 +214,24 @@
 F32 = jnp.float32
 
 
-def z_forward_kernel(rows, yrows, zlen, idx, field, zf, o0, o1, o2, o3, wide):
-    wide[...] = field[...].astype(F32)
+def z_forward_kernel(rows, yrows, zlen, idx, field, zf, o0, o1, o2, o3, held, tab, wide, sem):
+    first = pltpu.make_async_copy(field, held, sem.at[0])
+    first.start()
+    second = pltpu.make_async_copy(zf, tab, sem.at[1])
+    second.start()
+    first.wait()
+    wide[...] = held[...].astype(F32)
     side = jnp.concatenate(
         [wide[pl.ds(y, rows, stride=yrows), :].astype(BF) for y in range(yrows)], axis=1
     )
-    table = jnp.concatenate([zf[idx[0] ^ s] for s in range(4)], axis=1)
+    second.wait()
+    table = jnp.concatenate([tab[idx[0] ^ s] for s in range(4)], axis=1)
     out = dot(side, table).astype(BF)
     for s, o in enumerate((o0, o1, o2, o3)):
         o[...] = out[:, s * 128 : (s + 1) * 128]
 
 
-def lane_kernel(near, far, idx, r0, r1, r2, r3, table, o0, o1, o2, o3):
+def lane_kernel(near, far, idx, r0, r1, r2, r3, table, after, o0, o1, o2, o3):
     side = jnp.concatenate([r0[...], r1[...], r2[...], r3[...]], axis=1)
     cols = []
     for t in range(4):
@@ -248,7 +254,7 @@
     return side, table
 
 
-def mix_forward_kernel(idx, r0, r1, r2, r3, xf, xi, weight, modes, o0, o1, o2, o3):
+def mix_forward_kernel(idx, r0, r1, r2, r3, xf, xi, early, late, modes, o0, o1, o2, o3):
     side, table = x_side(idx, (r0, r1, r2, r3), xf)
     got = dot(side, table).astype(BF)
     for g in range(8):
@@ -264,8 +270,9 @@
             real = jnp.zeros((64, 128), F32)
             imag = jnp.zeros((64, 128), F32)
             for g in range(8):
-                wr = weight[g, 0, o].astype(F32)
-                wi = weight[g, 1, o].astype(F32)
+                weight, at = (early, g) if g < EARLY else (late, g - EARLY)
+                wr = weight[at, 0, o].astype(F32)
+                wi = weight[at, 1, o].astype(F32)
                 mr = modes[g, 0].astype(F32)
                 mi = modes[g, 1].astype(F32)
                 real = real + wr * mr - wi * mi
@@ -283,7 +290,7 @@
     lax.fori_loop(0, 16, pair, 0)
 
 
-def mix_backward_kernel(idx, r0, r1, r2, r3, xr, xd, weight, pmodes, o0, o1, o2, o3):
+def mix_backward_kernel(idx, r0, r1, r2, r3, xr, xd, early, late, pmodes, o0, o1, o2, o3):
     side, table = x_side(idx, (r0, r1, r2, r3), xr)
     for d in range(4):
         got = dot(side, table[:, d * 256 : (d + 1) * 256]).astype(BF)
@@ -293,12 +300,13 @@
     left = jnp.concatenate([xd[idx[1] ^ s] for s in range(4)], axis=0)
     outs = (o0, o1, o2, o3)
 
-    def group(g, carry):
+    def group(weight, first, at, carry):
+        g = first + at
         real = jnp.zeros((64, 128), F32)
         imag = jnp.zeros((64, 128), F32)
         for o in range(32):
-            wr = weight[g, 0, o].astype(F32)
-            wi = weight[g, 1, o].astype(F32)
+            wr = weight[at, 0, o].astype(F32)
+            wi = weight[at, 1, o].astype(F32)
             pr = pmodes[o, 0].astype(F32)
             pi = pmodes[o, 1].astype(F32)
             real = real + wr * pr + wi * pi
@@ -312,82 +320,167 @@
             outs[s][pl.ds(pl.multiple_of(g * 32, 32), 32), :] = got[s * 32 : (s + 1) * 32]
         return carry
 
-    lax.fori_loop(0, 8, group, 0)
-
-
-def pack_kernel(weight, packed):
-    def step(o, carry):
+    lax.fori_loop(0, EARLY, functools.partial(group, early, 0), 0)
+    lax.fori_loop(0, 8 - EARLY, functools.partial(group, late, EARLY), 0)
+
+
+def pack_kernel(first, weight, after, packed, token, held, sem):
+    count, half = packed.shape[0], packed.shape[2] // 2
+
+    def copy(g, h):
+        part = pl.ds(h * half, half)
+        return pltpu.make_async_copy(
+            weight.at[:, pl.ds(4 * (first + g), 4), part], held.at[g, :, :, part], sem.at[g, h]
+        )
+
+    for g in range(count):
+        for h in range(2):
+            copy(g, h).start()
+    for g in range(count):
+        for h in range(2):
+            copy(g, h).wait()
+
+            def step(o, carry):
+                for p in range(2):
+                    packed[g, p, o] = jnp.concatenate(
+                        [held[g, p, k, o] for k in range(4)], axis=1
+                    )
+                return carry
+
+            lax.fori_loop(h * half, (h + 1) * half, step, 0, unroll=8)
+    token[...] = jnp.zeros_like(token)
+
+
+def outer_kernel(start, count, modes, pmodes, *rest):
+    grad, token, held, turned, sem = rest[-5:]
+    half = pmodes.shape[0] // 2
+    copies = []
+    for g in range(count):
         for p in range(2):
-            packed[0, p, o] = jnp.concatenate([weight[p, k, o] for k in range(4)], axis=1)
-        return carry
-
-    lax.fori_loop(0, 32, step, 0)
-
-
-def outer_kernel(modes, pmodes, grad):
-    def step(o, carry):
-        mr = modes[0, 0].astype(F32)
-        mi = modes[0, 1].astype(F32)
-        pr = pmodes[o, 0].astype(F32)
-        pi = pmodes[o, 1].astype(F32)
-        real = (mr * pr + mi * pi).astype(BF)
-        imag = (mr * pi - mi * pr).astype(BF)
-        for k in range(4):
-            grad[0, k, o] = real[:, k * 32 : (k + 1) * 32]
-            grad[1, k, o] = imag[:, k * 32 : (k + 1) * 32]
-        return carry
-
-    lax.fori_loop(0, 32, step, 0)
-
-
-def cells_kernel(yrows, field, cotangent, fx, cx, wide):
+            m = modes[start + g, p].astype(F32)
+            for k in range(4):
+                turned[k, p] = (pltpu.roll(m, (128 - 32 * k) % 128, 1) if k else m).astype(BF)
+        for h in range(2):
+
+            def step(o, carry):
+                pr, pi = pmodes[o, 0], pmodes[o, 1]
+                for k in range(4):
+                    mr, mi = turned[k, 0], turned[k, 1]
+                    held[g, 0, k, o] = (mr * pr + mi * pi)[:, :32]
+                    held[g, 1, k, o] = (mr * pi - mi * pr)[:, :32]
+                return carry
+
+            lax.fori_loop(h * half, (h + 1) * half, step, 0, unroll=4)
+            part = pl.ds(h * half, half)
+            copies.append(
+                pltpu.make_async_copy(
+                    held.at[g, :, :, part],
+                    grad.at[:, pl.ds(4 * (start + g), 4), part],
+                    sem.at[g, h],
+                )
+            )
+            copies[-1].start()
+    for copy in copies:
+        copy.wait()
+    token[...] = jnp.zeros_like(token)
+
+
+def gelu_pair(value):
+    square = value * value
+    half = 0.5 + 0.5 * jnp.tanh(value * (KAPPA + (KAPPA * CUBIC) * square))
+    tail = (1.0 - half) * value * (2.0 * KAPPA + (6.0 * KAPPA * CUBIC) * square)
+    return value * half, half + half * tail
+
+
+def turn(value):
+    return value.astype(F32).T.astype(BF)
+
+
+def spread(block, count):
+    rows, lanes = block.shape
+    wide = jnp.concatenate([block.astype(F32)] * count, axis=1)
+    tall = jnp.concatenate([wide] * count, axis=0)
+    at_row = lax.broadcasted_iota(jnp.int32, tall.shape, 0) // rows
+    at_lane = lax.broadcasted_iota(jnp.int32, tall.shape, 1) // lanes
+    return jnp.where(at_row == at_lane, tall, 0.0).astype(BF)
+
+
+def cells_kernel(field, cotangent, skip, lift_t, proj, fx, cx, dskip, dskip_t, dlift, dlift_t, dproj, wide):
     for src, dst in ((field, fx), (cotangent, cx)):
         wide[...] = src[...].astype(F32)
 
         def step(k, carry):
-            first = k * 2
-            dst[k] = jnp.concatenate(
-                [wide[pl.ds(first + j, 32, stride=64), :] for j in range(2)], axis=1
-            ).astype(BF)
+            parts = []
+            for sub in range(8):
+                first = 16 * k + 2 * sub
+                parts.append(
+                    jnp.concatenate(
+                        [wide[pl.ds(first + j, 32, stride=64), :] for j in range(2)], axis=1
+                    ).astype(BF)
+                )
+            dst[k] = jnp.concatenate(parts, axis=0)
             return carry
 
-        lax.fori_loop(0, 32, step, 0)
+        lax.fori_loop(0, 4, step, 0)
+    dskip[...] = spread(skip[...], 8)
+    dskip_t[...] = spread(turn(skip[...]), 8)
+    dlift[...] = spread(turn(lift_t[...]), 8)
+    dlift_t[...] = spread(lift_t[...], 2)
+    dproj[...] = spread(turn(proj[...]), 8)
+
+
+def inverse_z(idx, refs, zi, spectral):
+    side = jnp.concatenate([r[...] for r in refs], axis=1)
+    back = jnp.concatenate([zi[idx[0] ^ s] for s in range(4)], axis=0)
+    for y in range(4):
+        got = dot(side, back[:, y * 256 : (y + 1) * 256])
+        spectral[2 * y] = got[:, :128]
+        spectral[2 * y + 1] = got[:, 128:]
+
+
+def cell_rows(spectral, k):
+    parts = []
+    for sub in range(8):
+        rows = pl.ds(2 * k + sub // 4, 32, stride=8)
+        parts.append(
+            jnp.concatenate([spectral[2 * (sub % 4) + j, rows, :] for j in range(2)], axis=1)
+        )
+    return jnp.concatenate(parts, axis=0)
 
 
 def point_kernel(
-    idx, r0, r1, r2, r3, zi, zf, fx, cx, skip, lift, lift_t, proj_t,
-    o0, o1, o2, o3, pg, sums, spectral, wide,
+    idx, r0, r1, r2, r3, zi, zf, fx, cx, dskip, dlift, dlift_t, dproj,
+    o0, o1, o2, o3, pg, act, hid, lif, spectral, wide,
 ):
-    side = jnp.concatenate([r0[...], r1[...], r2[...], r3[...]], axis=1)
-    back = jnp.concatenate([zi[idx[0] ^ s] for s in range(4)], axis=0)
-    for y in range(8):
-        spectral[y] = dot(side, back[:, y * 128 : (y + 1) * 128])
-    sums[...] = jnp.zeros_like(sums)
+    inverse_z(idx, (r0, r1, r2, r3), zi, spectral)
 
     def step(k, carry):
-        x, part = k // 4, k % 4
-        rows = pl.ds(x, 32, stride=8)
         values, grads = fx[k], cx[k]
-        pre = jnp.concatenate([spectral[2 * part + j, rows, :] for j in range(2)], axis=1)
-        pre = pre + dot(skip[...], values)
-        lifted, slope_pre = gelu_slope(pre)
+        pre = cell_rows(spectral, k) + dot(dskip[...], values)
+        lifted, slope_pre = gelu_pair(pre)
         lifted = lifted.astype(BF)
-        hidden = dot(lift[...], lifted)
-        activated, slope_hid = gelu_slope(hidden)
-        activated = activated.astype(BF)
-        hidden_grad = (dot(proj_t[...], grads) * slope_hid).astype(BF)
-        grad_up = grads.astype(F32) + dot(lift_t[...], hidden_grad)
-        pre_grad = grad_up * slope_pre
-        pre_grad_b = pre_grad.astype(BF)
-        for j in range(2):
-            wide[2 * part + j, rows, :] = pre_grad[:, j * 128 : (j + 1) * 128]
-        pg[k] = pre_grad_b
-        tall = jnp.concatenate([activated, hidden_grad, pre_grad_b], axis=0)
-        low = jnp.concatenate([grads, lifted, values], axis=0)
-        sums[...] += dot_nt(tall, low)
+        lif[k] = lifted
+        hidden = dot(dlift[...], lifted)
+        backed = dot(dproj[...], grads)
+        up = []
+        for q in range(4):
+            part = slice(q * 256, (q + 1) * 256)
+            activated, slope_hid = gelu_pair(hidden[part])
+            hidden_grad = (backed[part] * slope_hid).astype(BF)
+            act[k, part] = activated.astype(BF)
+            hid[k, part] = hidden_grad
+            up.append(dot(dlift_t[...], hidden_grad))
+        pre_grad = (grads.astype(F32) + jnp.concatenate(up, axis=0)) * slope_pre
+        pg[k] = pre_grad.astype(BF)
+        for sub in range(8):
+            rows = pl.ds(2 * k + sub // 4, 32, stride=8)
+            for j in range(2):
+                wide[2 * (sub % 4) + j, rows, :] = pre_grad[
+                    sub * 32 : (sub + 1) * 32, j * 128 : (j + 1) * 128
+                ]
         return carry
 
-    lax.fori_loop(0, 32, step, 0)
+    lax.fori_loop(0, 4, step, 0, unroll=2)
     table = jnp.concatenate([zf[idx[0] ^ s] for s in range(4)], axis=1)
     side = jnp.concatenate([wide[y].astype(BF) for y in range(8)], axis=1)
     out = dot(side, table).astype(BF)
@@ -395,27 +488,45 @@
         o[...] = out[:, s * 128 : (s + 1) * 128]
 
 
-def finish_kernel(idx, r0, r1, r2, r3, zi, pg, skip_t, out, spectral, wide):
-    side = jnp.concatenate([r0[...], r1[...], r2[...], r3[...]], axis=1)
-    back = jnp.concatenate([zi[idx[0] ^ s] for s in range(4)], axis=0)
-    for y in range(8):
-        spectral[y] = dot(side, back[:, y * 128 : (y + 1) * 128])
-
+def sums_kernel(fx, cx, pg, act, hid, lif, sums):
     def step(k, carry):
-        x, part = k // 4, k % 4
-        rows = pl.ds(x, 32, stride=8)
-        got = jnp.concatenate([spectral[2 * part + j, rows, :] for j in range(2)], axis=1)
-        got = got + dot(skip_t[...], pg[k])
-        first = k * 2
-        wide[pl.ds(first, 32, stride=64), :] = got[:, :128]
-        wide[pl.ds(first + 1, 32, stride=64), :] = got[:, 128:]
+        proj, lift, skip = carry
+        for sub in range(8):
+            c = slice(sub * 32, (sub + 1) * 32)
+            h = slice(sub * 128, (sub + 1) * 128)
+            proj = proj + dot_nt(cx[k, c], act[k, h])
+            lift = lift + dot_nt(lif[k, c], hid[k, h])
+            skip = skip + dot_nt(pg[k, c], fx[k, c])
+        return proj, lift, skip
+
+    zero = jnp.zeros((32, 128), F32)
+    got = lax.fori_loop(0, 4, step, (zero, zero, jnp.zeros((32, 32), F32)))
+    sums[0:32] = got[0]
+    sums[32:64] = got[1]
+    sums[64:96] = jnp.concatenate([got[2]] * 4, axis=1)
+
+
+def finish_kernel(idx, r0, r1, r2, r3, zi, pg, dskip_t, out, spectral, wide):
+    inverse_z(idx, (r0, r1, r2, r3), zi, spectral)
+
+    def step(k, carry):
+        got = cell_rows(spectral, k) + dot(dskip_t[...], pg[k])
+        for sub in range(8):
+            first = 16 * k + 2 * sub
+            for j in range(2):
+                wide[pl.ds(first + j, 32, stride=64), :] = got[
+                    sub * 32 : (sub + 1) * 32, j * 128 : (j + 1) * 128
+                ]
         return carry
 
-    lax.fori_loop(0, 32, step, 0)
+    lax.fori_loop(0, 4, step, 0, unroll=2)
     out[...] = wide[...].astype(BF)
 
 
+EARLY = 3
 VM = pl.BlockSpec(memory_space=pltpu.VMEM)
+ANY = pl.BlockSpec(memory_space=pl.ANY)
+HBM = pl.BlockSpec(memory_space=pltpu.HBM)
 SM = pl.BlockSpec(memory_space=pltpu.SMEM)
 BLOCK = jax.ShapeDtypeStruct((256, 128), BF)
 MIB = 1024 * 1024
@@ -425,11 +536,14 @@
     return pl.CostEstimate(flops=0, bytes_accessed=int(us * 3.0e6), transcendentals=0)
 
 
-def call(kernel, ins, outs, scratch=(), name=None, mib=16, us=1.0, smem=1):
+def call(kernel, ins, outs, scratch=(), name=None, mib=8, us=1.0, smem=1, free=0, hbm=()):
+    specs = [SM] * smem + [VM] * (len(ins) - smem - free) + [ANY] * free
+    for at in hbm:
+        specs[at] = HBM
     return pl.pallas_call(
         kernel,
         out_shape=outs,
-        in_specs=[SM] * smem + [VM] * (len(ins) - smem),
+        in_specs=specs,
         out_specs=jax.tree.map(lambda _: VM, outs),
         scratch_shapes=list(scratch),
         compiler_params=pltpu.CompilerParams(vmem_limit_bytes=mib * MIB),
@@ -438,9 +552,50 @@
     )(*ins)
 
 
+TOKEN = jax.ShapeDtypeStruct((8, 128), F32)
+
+
+def pack(weight, first, count, after, us):
+    chans = weight.shape[1]
+    return pl.pallas_call(
+        functools.partial(pack_kernel, first),
+        out_shape=[jax.ShapeDtypeStruct((count, 2, chans, 64, 128), BF), TOKEN],
+        in_specs=[ANY, ANY],
+        out_specs=[VM, VM],
+        scratch_shapes=[
+            pltpu.VMEM((count, 2, 4, chans, 64, 32), BF),
+            pltpu.SemaphoreType.DMA((count, 2)),
+        ],
+        compiler_params=pltpu.CompilerParams(vmem_limit_bytes=36 * MIB),
+        cost_estimate=cost(us),
+        name="pack",
+    )(weight, after)
+
+
+def outer(modes, pmodes, first, count, so_far, after, us):
+    chans = pmodes.shape[0]
+    extra = [] if so_far is None else [so_far, after]
+    return pl.pallas_call(
+        functools.partial(outer_kernel, first, count),
+        out_shape=[jax.ShapeDtypeStruct((2, chans, chans, 64, 32), BF), TOKEN],
+        in_specs=[VM, VM] + [ANY] * len(extra),
+        out_specs=[ANY, VM],
+        scratch_shapes=[
+            pltpu.VMEM((count, 2, 4, chans, 64, 32), BF),
+            pltpu.VMEM((4, 2, 64, 128), BF),
+            pltpu.SemaphoreType.DMA((count, 2)),
+        ],
+        input_output_aliases={} if so_far is None else {2: 0},
+        compiler_params=pltpu.CompilerParams(vmem_limit_bytes=24 * MIB),
+        cost_estimate=cost(us),
+        name="outer",
+    )(modes, pmodes, *extra)
+
+
 def exchange(blocks, axes):
     pairs = [[(a, a ^ s) for a in range(4)] for s in range(4)]
-    return [blocks[0]] + [lax.ppermute(blocks[s], axes, pairs[s]) for s in (1, 2, 3)]
+    got = {s: lax.ppermute(blocks[s], axes, pairs[s]) for s in (2, 3, 1)}
+    return [blocks[0], got[1], got[2], got[3]]
 
 
 def sum_over(part, axes):
@@ -466,84 +621,80 @@
     wide = pltpu.VMEM((cells, zlen), F32)
     tall = pltpu.VMEM((yrows, rows, zlen), F32)
     weight = mode_weight.reshape(2, chans, chans, 64, 32)
-
-    packed = pl.pallas_call(
-        pack_kernel,
-        grid=(8,),
-        out_shape=jax.ShapeDtypeStruct((8, 2, chans, 64, 128), BF),
-        in_specs=[pl.BlockSpec((2, 4, chans, 64, 32), lambda g: (0, g, 0, 0, 0))],
-        out_specs=pl.BlockSpec((1, 2, chans, 64, 128), lambda g: (g, 0, 0, 0, 0)),
-        compiler_params=pltpu.CompilerParams(vmem_limit_bytes=20 * MIB),
-        cost_estimate=cost(12.0),
-        name="pack",
-    )(weight)
+    lift_t = lift_weight.T
+
+    def bf(*shape):
+        return jax.ShapeDtypeStruct(shape, BF)
+
+    def lanes(near, far, got, table, after, name):
+        return call(
+            functools.partial(lane_kernel, near, far),
+            (idx, *got, table, after), four, (), name, 4, 1.0, free=1,
+        )
 
     sent = call(
         functools.partial(z_forward_kernel, rows, yrows, zlen),
-        (idx, flat_field, zf), four, [wide], "z_forward", 8, 2.0,
+        (idx, flat_field, zf), four,
+        [
+            pltpu.VMEM((cells, zlen), BF),
+            pltpu.VMEM(zf.shape, BF),
+            wide,
+            pltpu.SemaphoreType.DMA((2,)),
+        ],
+        "z_forward", 8, 2.0, hbm=(1, 2),
     )
     got = exchange(sent, gyc)
-    fx, cx = call(
-        functools.partial(cells_kernel, yrows),
-        (flat_field, flat_cot),
-        [jax.ShapeDtypeStruct((32, chans, 256), BF)] * 2, [wide], "cells", 8, 2.0, 0,
-    )
-    sent = call(functools.partial(lane_kernel, 0, 1), (idx, *got, yf), four, (), "y_forward", 8, 1.0)
+    early, token = pack(weight, 0, EARLY, sent[0], 4.0)
+    sent = lanes(0, 1, got, yf, token, "y_forward")
     got = exchange(sent, "gx")
+    late, _ = pack(weight, EARLY, 8 - EARLY, sent[0], 8.0)
     modes, *sent = call(
-        mix_forward_kernel, (idx, *got, xf, xi, packed),
-        [jax.ShapeDtypeStruct((8, 2, 64, 128), BF)] + four, (), "mix_forward", 16, 5.0,
+        mix_forward_kernel, (idx, *got, xf, xi, early, late),
+        [bf(8, 2, 64, 128)] + four, (), "mix_forward", 12, 5.0,
     )
     got = exchange(sent, "gx")
-    sent = call(functools.partial(lane_kernel, 1, 0), (idx, *got, yi), four, (), "y_inverse", 8, 1.0)
+    fx, cx, dskip, dskip_t, dlift, dlift_t, dproj = call(
+        cells_kernel,
+        (flat_field, flat_cot, skip_weight, lift_t, proj_weight),
+        [bf(4, 256, 256)] * 2
+        + [bf(256, 256), bf(256, 256), bf(1024, 256), bf(64, 256), bf(1024, 256)],
+        [wide], "cells", 8, 3.0, 0,
+    )
+    sent = lanes(1, 0, got, yi, fx, "y_inverse")
     got = exchange(sent, gyc)
-    *sent, pg, sums = call(
+    *sent, pg, act, hid, lif = call(
         point_kernel,
-        (idx, *got, zi, zf, fx, cx, skip_weight, lift_weight, lift_weight.T, proj_weight.T),
-        four + [
-            jax.ShapeDtypeStruct((32, chans, 256), BF),
-            jax.ShapeDtypeStruct((288, 96), F32),
-        ],
+        (idx, *got, zi, zf, fx, cx, dskip, dlift, dlift_t, dproj),
+        four + [bf(4, 256, 256), bf(4, 1024, 256), bf(4, 1024, 256), bf(4, 256, 256)],
         [tall, tall], "point", 16, 8.0,
     )
     got = exchange(sent, gyc)
-    part = jnp.concatenate(
-        [sums[:128, :32], sums[128:256, 32:64], sums[256:, 64:]], axis=0
-    ).reshape(72, 128)
-    part = sum_over(part, (("col", 2), ("gy", 2), ("gx", 4))).reshape(288, 32)
-    proj_grad, lift_grad, skip_grad = part[:128].T, part[128:256], part[256:]
-    sent = call(functools.partial(lane_kernel, 0, 1), (idx, *got, yf), four, (), "y_forward", 8, 1.0)
+    part = call(
+        sums_kernel, (fx, cx, pg, act, hid, lif),
+        jax.ShapeDtypeStruct((96, 128), F32), (), "sums", 4, 2.5, 0,
+    )
+    sent = lanes(0, 1, got, yf, part, "y_forward")
     got = exchange(sent, "gx")
     pmodes, *sent = call(
-        mix_backward_kernel, (idx, *got, xr, xd, packed),
-        [jax.ShapeDtypeStruct((32, 2, 64, 128), BF)] + four, (), "mix_backward", 16, 5.0,
+        mix_backward_kernel, (idx, *got, xr, xd, early, late),
+        [bf(32, 2, 64, 128)] + four, (), "mix_backward", 12, 5.0,
     )
     got = exchange(sent, "gx")
-    mode_grad = pl.pallas_call(
-        outer_kernel,
-        grid=(8,),
-        out_shape=jax.ShapeDtypeStruct((2, chans, chans, 64, 32), BF),
-        in_specs=[
-            pl.BlockSpec((1, 2, 64, 128), lambda g: (g, 0, 0, 0)),
-            pl.BlockSpec((32, 2, 64, 128), lambda g: (0, 0, 0, 0)),
-        ],
-        out_specs=pl.BlockSpec((2, 4, chans, 64, 32), lambda g: (0, g, 0, 0, 0)),
-        compiler_params=pltpu.CompilerParams(vmem_limit_bytes=20 * MIB),
-        cost_estimate=cost(12.0),
-        name="outer",
-    )(modes, pmodes)
-    sent = call(functools.partial(lane_kernel, 1, 0), (idx, *got, yi), four, (), "y_inverse", 8, 1.0)
+    grad, token = outer(modes, pmodes, 0, 4, None, None, 6.0)
+    sent = lanes(1, 0, got, yi, token, "y_inverse")
     got = exchange(sent, gyc)
+    mode_grad, _ = outer(modes, pmodes, 4, 4, grad, sent[0], 6.0)
     field_grad = call(
-        finish_kernel, (idx, *got, zi, pg, skip_weight.T),
-        jax.ShapeDtypeStruct((cells, zlen), BF), [tall, wide], "finish", 8, 2.0,
-    )
+        finish_kernel, (idx, *got, zi, pg, dskip_t),
+        bf(cells, zlen), [tall, wide], "finish", 8, 2.0,
+    )
+    part = sum_over(part, (("col", 2), ("gy", 2), ("gx", 4)))
     return (
         field_grad.reshape(field.shape),
         mode_grad.reshape(mode_weight.shape),
-        skip_grad,
-        lift_grad,
-        proj_grad,
+        part[64:, :chans],
+        part[32:64].T,
+        part[:32],
     )
 
 

time: 179 us -> 103 us (0.58)
  Pallas kernels: 107 us -> 54.7 us
  local copies, waits for them, and re-layouts: 20.8 us -> 3.56 us
  waiting for transfers between devices: 19.5 us -> 13.1 us
    pallas_call x12 -> x15, Pallas kernels: 107 us -> 54.7 us  [the longest x11 27.6 us: call(): pl.pallas_call(kernel, out_shape=outs, in_specs=specs, out_specs=jax.tree...]
    unnamed x53 -> x30, local copies, waits for them, and re-layouts: 19.7 us -> 2.34 us
    ppermute x24, waiting for transfers between devices: 16.3 us -> 12.2 us  [exchange(): got = {s: lax.ppermute(blocks[s], axes, pairs[s]) for s in (2, 3, 1)}]
    ppermute x4, waiting for transfers between devices: 3.2 us -> 0.89 us  [sum_over(): part = part + lax.ppermute(part, axis, [(a, a ^ step) for a in range(size)])]
  transfers between devices with their start and end apart: 28 -> 28, of which waited for: 13 -> 7; matrix products, arithmetic and copies ran while one was open for 3% -> 1% of each run, Pallas kernels for 38% -> 36%
where the time goes in v1:
time: 103 us; the launch traced here: 102 us
  Pallas kernels  54.7 us (53%)
  starting transfers between devices  30 us (29%)
  waiting for transfers between devices  13.1 us (13%)
  local copies, waits for them, and re-layouts  3.56 us (3%)
  between operations  1.03 us (1%)
    pallas_call x11, Pallas kernels, call(): pl.pallas_call(kernel, out_shape=outs, in_specs=specs, out_specs=jax.tree...  27.6 us
    ppermute x24, starting transfers between devices, exchange(): got = {s: lax.ppermute(blocks[s], axes, pairs[s]) for s in (2, 3, 1)}  26.7 us
    pallas_call x2, Pallas kernels, pack(): pl.pallas_call(functools.partial(pack_kernel, first), out_shape=[jax.Shap...  13.6 us
    pallas_call x2, Pallas kernels, outer(): pl.pallas_call(functools.partial(outer_kernel, first, count), out_shape=[...  13.6 us
    ppermute x24, waiting for transfers between devices, exchange(): got = {s: lax.ppermute(blocks[s], axes, pairs[s]) for s in (2, 3, 1)}  12.2 us
    ppermute x4, starting transfers between devices, sum_over(): part = part + lax.ppermute(part, axis, [(a, a ^ step) for a in range(size)])  3.29 us
    unnamed x30, local copies, waits for them, and re-layouts  2.34 us
  transfers between devices with their start and end apart: 28, of which 7 were waited for; matrix products, arithmetic and copies ran while one was open for 1% of the time, Pallas kernels for 36%

profile of v1, /device:TPU:0, one launch (start us, length us, event | category | flops | bytes accessed | tf_op | source)
XLA Modules:
  0.0 102.5 jit_solution(13731215822772286925)
XLA Ops:
  0.7 1.2 %copy-done.1 = bf16[4,1024,128]{2,1,0:T(8,128)(2,1)S(1)} copy-done((bf16[4,1024,128]{2,1,0:T(8,128)(2,1)S(1)}, bf16[4,1024,128]{2,1,0:T(8,128)(2,1)}, u32[]{:S(2)}) %copy-start.1) | copy-done | bytes 1048600
  1.9 1.0 %copy-done.4 = bf16[32,8,8,128]{3,2,1,0:T(8,128)(2,1)S(1)} copy-done((bf16[32,8,8,128]{3,2,1,0:T(8,128)(2,1)S(1)}, bf16[32,8,8,128]{3,2,1,0:T(8,128)(2,1)}, u32[]{:S(2)}) %copy-start.4) | copy-done | bytes 524312
  3.0 1.4 %z_forward.1 = (bf16[256,128]{1,0:T(8,128)(2,1)S(1)}, bf16[256,128]{1,0:T(8,128)(2,1)S(1)}, bf16[256,128]{1,0:T(8,128)(2,1)S(1)}, bf16[256,128]{1,0:T(8,128)(2,1)S(1)}) custom-call(s32[2]{0:T(128)S(1)} %pad_add_fusion.idx, bf16[2048,128]{1,0:T(8,128)(2,1)S(1)} %bitcast.10, bf16[4,1024,128]{2,1,0:T(8,128)(2,1)S(1)} %copy-done.1), custom_call_target="tpu_custom_call" | custom-call | bytes 6000000 | tf_op jit(solution)/shard_map/z_forward/pallas_call | solution.py:543
  4.9 2.6 %collective-permute-start.1 = (bf16[256,128]{1,0:T(8,128)(2,1)S(1)}, bf16[256,128]{1,0:T(8,128)(2,1)S(1)}, u32[]{:S(2)}, u32[]{:S(2)}) collective-permute-start(bf16[256,128]{1,0:T(8,128)(2,1)S(1)} %get-tuple-element.58), channel_id=1, source_target_pairs={{0,2},{1,3},{2,0},{3,1},{4,6},{5,7},{6,4},{7,5},{8,10},{9,11},{10,... | collective-permute-start | bytes 196616 | tf_op jit(solution)/shard_map/ppermute | solution.py:597
  7.5 5.3 %pack.2 = (bf16[3,2,32,64,128]{4,3,2,1,0:T(8,128)(2,1)S(1)}, f32[8,128]{1,0:T(8,128)S(1)}) custom-call(bf16[2,32,32,64,32]{4,3,2,1,0:T(8,128)(2,1)} %bitcast.14, bf16[256,128]{1,0:T(8,128)(2,1)S(1)} %get-tuple-element.56.after.r0), custom_call_target="tpu_custom_call" | custom-call | bytes 12000000 | tf_op jit(solution)/shard_map/pack/pallas_call | solution.py:560
  13.7 1.9 %collective-permute-start.3 = (bf16[256,128]{1,0:T(8,128)(2,1)S(1)}, bf16[256,128]{1,0:T(8,128)(2,1)S(1)}, u32[]{:S(2)}, u32[]{:S(2)}) collective-permute-start(bf16[256,128]{1,0:T(8,128)(2,1)S(1)} %get-tuple-element.62), channel_id=1, source_target_pairs={{0,4},{4,0},{8,12},{12,8},{1,5},{5,1},{9,13},{13,9},{2,6},{6,2},{1... | collective-permute-start | bytes 196616 | tf_op jit(solution)/shard_map/ppermute | solution.py:597
  15.6 2.6 %collective-permute-start.4 = (bf16[256,128]{1,0:T(8,128)(2,1)S(1)}, bf16[256,128]{1,0:T(8,128)(2,1)S(1)}, u32[]{:S(2)}, u32[]{:S(2)}) collective-permute-start(bf16[256,128]{1,0:T(8,128)(2,1)S(1)} %get-tuple-element.63), channel_id=1, source_target_pairs={{0,8},{4,12},{8,0},{12,4},{1,9},{5,13},{9,1},{13,5},{2,10},{6,14},... | collective-permute-start | bytes 196616 | tf_op jit(solution)/shard_map/ppermute | solution.py:597
  18.2 8.3 %pack.3 = (bf16[5,2,32,64,128]{4,3,2,1,0:T(8,128)(2,1)S(1)}, f32[8,128]{1,0:T(8,128)}) custom-call(bf16[2,32,32,64,32]{4,3,2,1,0:T(8,128)(2,1)} %bitcast.15, bf16[256,128]{1,0:T(8,128)(2,1)S(1)} %get-tuple-element.61.after.r0), custom_call_target="tpu_custom_call" | custom-call | bytes 24000000 | tf_op jit(solution)/shard_map/pack/pallas_call | solution.py:560
  26.7 5.8 %mix_forward.1 = (bf16[8,2,64,128]{3,2,1,0:T(8,128)(2,1)S(1)}, bf16[256,128]{1,0:T(8,128)(2,1)S(1)}, bf16[256,128]{1,0:T(8,128)(2,1)S(1)}, bf16[256,128]{1,0:T(8,128)(2,1)S(1)}, bf16[256,128]{1,0:T(8,128)(2,1)S(1)}) custom-call(s32[2]{0:T(128)S(1)} %pad_add_fusion.idx, bf16[256,128]{1,0:T(8,128)(2,1)S(1)} %get-tuple-element.61.after.r0, ...), custom_call_target="tpu_custom_call" | custom-call | bytes 15000000 | tf_op jit(solution)/shard_map/mix_forward/pallas_call | solution.py:543
  33.4 3.5 %collective-permute-start.7 = (bf16[256,128]{1,0:T(8,128)(2,1)S(1)}, bf16[256,128]{1,0:T(8,128)(2,1)S(1)}, u32[]{:S(2)}, u32[]{:S(2)}) collective-permute-start(bf16[256,128]{1,0:T(8,128)(2,1)S(1)} %get-tuple-element.69), channel_id=1, source_target_pairs={{0,8},{4,12},{8,0},{12,4},{1,9},{5,13},{9,1},{13,5},{2,10},{6,14},... | collective-permute-start | bytes 196616 | tf_op jit(solution)/shard_map/ppermute | solution.py:597
  36.9 1.7 %cells.1 = (bf16[4,256,256]{2,1,0:T(8,128)(2,1)S(1)}, bf16[4,256,256]{2,1,0:T(8,128)(2,1)S(1)}, bf16[256,256]{1,0:T(8,128)(2,1)S(1)}, bf16[256,256]{1,0:T(8,128)...) custom-call(bf16[2048,128]{1,0:T(8,128)(2,1)S(1)} %bitcast.11, ...), custom_call_target="tpu_custom_call" | custom-call | bytes 9000000 | tf_op jit(solution)/shard_map/cells/pallas_call | solution.py:543
  38.6 2.5 %collective-permute-done.7.r2 = bf16[256,128]{1,0:T(8,128)(2,1)S(1)} collective-permute-done((bf16[256,128]{1,0:T(8,128)(2,1)S(1)}, bf16[256,128]{1,0:T(8,128)(2,1)S(1)}, u32[]{:S(2)}, u32[]{:S(2)}) %collective-permute-start.7) | collective-permute-done | bytes 65568 | tf_op jit(solution)/shard_map/ppermute | solution.py:597
  41.2 1.8 %collective-permute-done.8.r3 = bf16[256,128]{1,0:T(8,128)(2,1)S(1)} collective-permute-done((bf16[256,128]{1,0:T(8,128)(2,1)S(1)}, bf16[256,128]{1,0:T(8,128)(2,1)S(1)}, u32[]{:S(2)}, u32[]{:S(2)}) %collective-permute-start.8) | collective-permute-done | bytes 65568 | tf_op jit(solution)/shard_map/ppermute | solution.py:597
  43.9 1.5 %collective-permute-start.10 = (bf16[256,128]{1,0:T(8,128)(2,1)S(1)}, bf16[256,128]{1,0:T(8,128)(2,1)S(1)}, u32[]{:S(2)}, u32[]{:S(2)}) collective-permute-start(bf16[256,128]{1,0:T(8,128)(2,1)S(1)} %get-tuple-element.74), channel_id=1, source_target_pairs={{0,2},{1,3},{2,0},{3,1},{4,6},{5,7},{6,4},{7,5},{8,10},{9,11},{10,... | collective-permute-start | bytes 196616 | tf_op jit(solution)/shard_map/ppermute | solution.py:597
  45.7 2.6 %collective-permute-done.10.r2 = bf16[256,128]{1,0:T(8,128)(2,1)S(1)} collective-permute-done((bf16[256,128]{1,0:T(8,128)(2,1)S(1)}, bf16[256,128]{1,0:T(8,128)(2,1)S(1)}, u32[]{:S(2)}, u32[]{:S(2)}) %collective-permute-start.10) | collective-permute-done | bytes 65568 | tf_op jit(solution)/shard_map/ppermute | solution.py:597
  48.4 1.1 %collective-permute-done.11.r3 = bf16[256,128]{1,0:T(8,128)(2,1)S(1)} collective-permute-done((bf16[256,128]{1,0:T(8,128)(2,1)S(1)}, bf16[256,128]{1,0:T(8,128)(2,1)S(1)}, u32[]{:S(2)}, u32[]{:S(2)}) %collective-permute-start.11) | collective-permute-done | bytes 65568 | tf_op jit(solution)/shard_map/ppermute | solution.py:597
  49.5 5.8 %point.1 = (bf16[256,128]{1,0:T(8,128)(2,1)S(1)}, bf16[256,128]{1,0:T(8,128)(2,1)S(1)}, bf16[256,128]{1,0:T(8,128)(2,1)S(1)}, bf16[256,128]{1,0:T(8,128)(2,1)S(1...) custom-call(s32[2]{0:T(128)S(1)} %pad_add_fusion.idx, ...), custom_call_target="tpu_custom_call" | custom-call | bytes 24000000 | tf_op jit(solution)/shard_map/point/pallas_call | solution.py:543
  55.5 1.5 %collective-permute-start.13 = (bf16[256,128]{1,0:T(8,128)(2,1)S(1)}, bf16[256,128]{1,0:T(8,128)(2,1)S(1)}, u32[]{:S(2)}, u32[]{:S(2)}) collective-permute-start(bf16[256,128]{1,0:T(8,128)(2,1)S(1)} %get-tuple-element.83), channel_id=1, source_target_pairs={{0,2},{1,3},{2,0},{3,1},{4,6},{5,7},{6,4},{7,5},{8,10},{9,11},{10,... | collective-permute-start | bytes 196616 | tf_op jit(solution)/shard_map/ppermute | solution.py:597
  57.2 1.8 %sums.1.after = f32[96,128]{1,0:T(8,128)S(1)} custom-call(bf16[4,256,256]{2,1,0:T(8,128)(2,1)S(1)} %get-tuple-element.71.after.fx, bf16[4,256,256]{2,1,0:T(8,128)(2,1)S(1)} %get-tuple-element.76.cx, bf16[4,256,256]{2,1,0:T(8,128)(2,1)S(1)} %get-tuple-element.85.pg, bf16[4,1024,256]{2,1,0:T(8,128)(2,1)S(1)} %get-tuple-element.86.act, ...), custom_call_target="tpu_custom_call" | custom-call | bytes 7500000 | tf_op jit(solution)/shard_map/sums/pallas_call | solution.py:543
  60.4 1.5 %collective-permute-start.25 = (f32[96,128]{1,0:T(8,128)S(1)}, f32[96,128]{1,0:T(8,128)S(1)}, u32[]{:S(2)}, u32[]{:S(2)}) collective-permute-start(f32[96,128]{1,0:T(8,128)S(1)} %add.16), channel_id=1, source_target_pairs={{0,2},{2,0},{1,3},{3,1},{4,6},{6,4},{5,7},{7,5},{8,10},{10,8},{9,1... | collective-permute-start | bytes 147464 | tf_op jit(solution)/shard_map/ppermute | solution.py:605
  62.8 1.9 %collective-permute-start.16 = (bf16[256,128]{1,0:T(8,128)(2,1)S(1)}, bf16[256,128]{1,0:T(8,128)(2,1)S(1)}, u32[]{:S(2)}, u32[]{:S(2)}) collective-permute-start(bf16[256,128]{1,0:T(8,128)(2,1)S(1)} %get-tuple-element.91), channel_id=1, source_target_pairs={{0,8},{4,12},{8,0},{12,4},{1,9},{5,13},{9,1},{13,5},{2,10},{6,14},... | collective-permute-start | bytes 196616 | tf_op jit(solution)/shard_map/ppermute | solution.py:597
  64.7 2.5 %collective-permute-start.17 = (bf16[256,128]{1,0:T(8,128)(2,1)S(1)}, bf16[256,128]{1,0:T(8,128)(2,1)S(1)}, u32[]{:S(2)}, u32[]{:S(2)}) collective-permute-start(bf16[256,128]{1,0:T(8,128)(2,1)S(1)} %get-tuple-element.92), channel_id=1, source_target_pairs={{0,12},{4,8},{8,4},{12,0},{1,13},{5,9},{9,5},{13,1},{2,14},{6,10},... | collective-permute-start | bytes 196616 | tf_op jit(solution)/shard_map/ppermute | solution.py:597
  68.1 3.3 %collective-permute-done.16.r2 = bf16[256,128]{1,0:T(8,128)(2,1)S(1)} collective-permute-done((bf16[256,128]{1,0:T(8,128)(2,1)S(1)}, bf16[256,128]{1,0:T(8,128)(2,1)S(1)}, u32[]{:S(2)}, u32[]{:S(2)}) %collective-permute-start.16) | collective-permute-done | bytes 65568 | tf_op jit(solution)/shard_map/ppermute | solution.py:597
  71.4 4.8 %mix_backward.1 = (bf16[32,2,64,128]{3,2,1,0:T(8,128)(2,1)S(1)}, bf16[256,128]{1,0:T(8,128)(2,1)S(1)}, bf16[256,128]{1,0:T(8,128)(2,1)S(1)}, bf16[256,128]{1,0:T(8,128)(2,1)S(1)}, bf16[256,128]{1,0:T(8,128)(2,1)S(1)}) custom-call(s32[2]{0:T(128)S(1)} %pad_add_fusion.idx, bf16[256,128]{1,0:T(8,128)(2,1)S(1)} %get-tuple-element.89.r0, ...), custom_call_target="tpu_custom_call" | custom-call | bytes 15000000 | tf_op jit(solution)/shard_map/mix_backward/pallas_call | solution.py:543
  76.3 1.5 %collective-permute-start.18 = (bf16[256,128]{1,0:T(8,128)(2,1)S(1)}, bf16[256,128]{1,0:T(8,128)(2,1)S(1)}, u32[]{:S(2)}, u32[]{:S(2)}) collective-permute-start(bf16[256,128]{1,0:T(8,128)(2,1)S(1)} %get-tuple-element.94), channel_id=1, source_target_pairs={{0,4},{4,0},{8,12},{12,8},{1,5},{5,1},{9,13},{13,9},{2,6},{6,2},{1... | collective-permute-start | bytes 196616 | tf_op jit(solution)/shard_map/ppermute | solution.py:597
  77.8 1.2 %collective-permute-start.19 = (bf16[256,128]{1,0:T(8,128)(2,1)S(1)}, bf16[256,128]{1,0:T(8,128)(2,1)S(1)}, u32[]{:S(2)}, u32[]{:S(2)}) collective-permute-start(bf16[256,128]{1,0:T(8,128)(2,1)S(1)} %get-tuple-element.95), channel_id=1, source_target_pairs={{0,8},{4,12},{8,0},{12,4},{1,9},{5,13},{9,1},{13,5},{2,10},{6,14},... | collective-permute-start | bytes 196616 | tf_op jit(solution)/shard_map/ppermute | solution.py:597
  78.9 1.8 %collective-permute-start.20 = (bf16[256,128]{1,0:T(8,128)(2,1)S(1)}, bf16[256,128]{1,0:T(8,128)(2,1)S(1)}, u32[]{:S(2)}, u32[]{:S(2)}) collective-permute-start(bf16[256,128]{1,0:T(8,128)(2,1)S(1)} %get-tuple-element.96), channel_id=1, source_target_pairs={{0,12},{4,8},{8,4},{12,0},{1,13},{5,9},{9,5},{13,1},{2,14},{6,10},... | collective-permute-start | bytes 196616 | tf_op jit(solution)/shard_map/ppermute | solution.py:597
  80.7 1.3 %collective-permute-start.27 = (f32[96,128]{1,0:T(8,128)S(1)}, f32[96,128]{1,0:T(8,128)S(1)}, u32[]{:S(2)}, u32[]{:S(2)}) collective-permute-start(f32[96,128]{1,0:T(8,128)S(1)} %add.18), channel_id=1, source_target_pairs={{0,8},{4,12},{8,0},{12,4},{1,9},{5,13},{9,1},{13,5},{2,10},{6,14},... | collective-permute-start | bytes 147464 | tf_op jit(solution)/shard_map/ppermute | solution.py:605
  82.0 6.5 %outer.2 = (bf16[2,32,32,64,32]{4,3,2,1,0:T(8,128)(2,1)}, f32[8,128]{1,0:T(8,128)S(1)}) custom-call(bf16[8,2,64,128]{3,2,1,0:T(8,128)(2,1)S(1)} %get-tuple-element.97.modes, bf16[32,2,64,128]{3,2,1,0:T(8,128)(2,1)S(1)} %get-tuple-element.98.pmodes), custom_call_target="tpu_custom_call" | custom-call | bytes 18000000 | tf_op jit(solution)/shard_map/outer/pallas_call | solution.py:578
  90.1 1.2 %collective-permute-start.23 = (bf16[256,128]{1,0:T(8,128)(2,1)S(1)}, bf16[256,128]{1,0:T(8,128)(2,1)S(1)}, u32[]{:S(2)}, u32[]{:S(2)}) collective-permute-start(bf16[256,128]{1,0:T(8,128)(2,1)S(1)} %get-tuple-element.103), channel_id=1, source_target_pairs={{0,3},{1,2},{2,1},{3,0},{4,7},{5,6},{6,5},{7,4},{8,11},{9,10},{10,... | collective-permute-start | bytes 196616 | tf_op jit(solution)/shard_map/ppermute | solution.py:597
  92.5 7.1 %outer.3 = (bf16[2,32,32,64,32]{4,3,2,1,0:T(8,128)(2,1)}, f32[8,128]{1,0:T(8,128)}) custom-call(bf16[8,2,64,128]{3,2,1,0:T(8,128)(2,1)S(1)} %get-tuple-element.97.modes, bf16[32,2,64,128]{3,2,1,0:T(8,128)(2,1)S(1)} %get-tuple-element.98.pmodes, bf16[2,32,32,64,32]{4,3,2,1,0:T(8,128)(2,1)} %get-tuple-element.105.rest_0_, ...), custom_call_target="tpu_custom_call", output_to_operand_aliasing={{0}: (2, {})} | custom-call | bytes 18000000 | tf_op jit(solution)/shard_map/outer/pallas_call | solution.py:578
  99.6 2.8 %finish.1 = bf16[2048,128]{1,0:T(8,128)(2,1)} custom-call(s32[2]{0:T(128)S(1)} %pad_add_fusion.idx, bf16[256,128]{1,0:T(8,128)(2,1)S(1)} %get-tuple-element.100.r0.rest_1_, bf16[256,128]{1,0:T(8,128)(2,1)S(1)} %collective-permute-done.21.r1, bf16[256,128]{1,0:T(8,128)(2,1)S(1)} %collective-permute-done.22.r2, ...), custom_call_target="tpu_custom_call" | custom-call | bytes 6000000 | tf_op jit(solution)/shard_map/finish/pallas_call | solution.py:543
  (76 shorter events, 10.3 us)
Async XLA Ops:
  4.4 8.5 %collective-permute-start = (bf16[256,128]{1,0:T(8,128)(2,1)S(1)}, bf16[256,128]{1,0:T(8,128)(2,1)S(1)}, u32[]{:S(2)}, u32[]{:S(2)}) collective-permute-start(bf16[256,128]{1,0:T(8,128)(2,1)S(1)} %get-tuple-element.57), channel_id=1, source_target_pairs={{0,1},{1,0},{2,3},{3,2},{4,5},{5,4},{6,7},{7,6},{8,9},{9,8},{10,11... | collective-permute-start | bytes 196616 | tf_op jit(solution)/shard_map/ppermute | solution.py:597
  4.9 8.0 %collective-permute-start.1 = (bf16[256,128]{1,0:T(8,128)(2,1)S(1)}, bf16[256,128]{1,0:T(8,128)(2,1)S(1)}, u32[]{:S(2)}, u32[]{:S(2)}) collective-permute-start(bf16[256,128]{1,0:T(8,128)(2,1)S(1)} %get-tuple-element.58), channel_id=1, source_target_pairs={{0,2},{1,3},{2,0},{3,1},{4,6},{5,7},{6,4},{7,5},{8,10},{9,11},{10,... | collective-permute-start | bytes 196616 | tf_op jit(solution)/shard_map/ppermute | solution.py:597
  7.5 5.4 %collective-permute-start.2 = (bf16[256,128]{1,0:T(8,128)(2,1)S(1)}, bf16[256,128]{1,0:T(8,128)(2,1)S(1)}, u32[]{:S(2)}, u32[]{:S(2)}) collective-permute-start(bf16[256,128]{1,0:T(8,128)(2,1)S(1)} %get-tuple-element.59), channel_id=1, source_target_pairs={{0,3},{1,2},{2,1},{3,0},{4,7},{5,6},{6,5},{7,4},{8,11},{9,10},{10,... | collective-permute-start | bytes 196616 | tf_op jit(solution)/shard_map/ppermute | solution.py:597
  13.7 12.9 %collective-permute-start.3 = (bf16[256,128]{1,0:T(8,128)(2,1)S(1)}, bf16[256,128]{1,0:T(8,128)(2,1)S(1)}, u32[]{:S(2)}, u32[]{:S(2)}) collective-permute-start(bf16[256,128]{1,0:T(8,128)(2,1)S(1)} %get-tuple-element.62), channel_id=1, source_target_pairs={{0,4},{4,0},{8,12},{12,8},{1,5},{5,1},{9,13},{13,9},{2,6},{6,2},{1... | collective-permute-start | bytes 196616 | tf_op jit(solution)/shard_map/ppermute | solution.py:597
  15.6 11.0 %collective-permute-start.4 = (bf16[256,128]{1,0:T(8,128)(2,1)S(1)}, bf16[256,128]{1,0:T(8,128)(2,1)S(1)}, u32[]{:S(2)}, u32[]{:S(2)}) collective-permute-start(bf16[256,128]{1,0:T(8,128)(2,1)S(1)} %get-tuple-element.63), channel_id=1, source_target_pairs={{0,8},{4,12},{8,0},{12,4},{1,9},{5,13},{9,1},{13,5},{2,10},{6,14},... | collective-permute-start | bytes 196616 | tf_op jit(solution)/shard_map/ppermute | solution.py:597
  18.2 8.4 %collective-permute-start.5 = (bf16[256,128]{1,0:T(8,128)(2,1)S(1)}, bf16[256,128]{1,0:T(8,128)(2,1)S(1)}, u32[]{:S(2)}, u32[]{:S(2)}) collective-permute-start(bf16[256,128]{1,0:T(8,128)(2,1)S(1)} %get-tuple-element.64), channel_id=1, source_target_pairs={{0,12},{4,8},{8,4},{12,0},{1,13},{5,9},{9,5},{13,1},{2,14},{6,10},... | collective-permute-start | bytes 196616 | tf_op jit(solution)/shard_map/ppermute | solution.py:597
  26.6 22.8 %copy-start = (bf16[4,128,1024]{2,1,0:T(8,128)(2,1)S(1)}, bf16[4,128,1024]{2,1,0:T(8,128)(2,1)}, u32[]{:S(2)}) copy-start(bf16[4,128,1024]{2,1,0:T(8,128)(2,1)} %constant.30.clone.zi) | copy-start | bytes 3145732
  26.7 22.8 %copy-start.2 = (bf16[4,1024,128]{2,1,0:T(8,128)(2,1)S(1)}, bf16[4,1024,128]{2,1,0:T(8,128)(2,1)}, u32[]{:S(2)}) copy-start(bf16[4,1024,128]{2,1,0:T(8,128)(2,1)} %constant.29.clone.zf) | copy-start | bytes 3145732
  32.5 6.2 %collective-permute-start.6 = (bf16[256,128]{1,0:T(8,128)(2,1)S(1)}, bf16[256,128]{1,0:T(8,128)(2,1)S(1)}, u32[]{:S(2)}, u32[]{:S(2)}) collective-permute-start(bf16[256,128]{1,0:T(8,128)(2,1)S(1)} %get-tuple-element.68), channel_id=1, source_target_pairs={{0,4},{4,0},{8,12},{12,8},{1,5},{5,1},{9,13},{13,9},{2,6},{6,2},{1... | collective-permute-start | bytes 196616 | tf_op jit(solution)/shard_map/ppermute | solution.py:597
  33.4 7.8 %collective-permute-start.7 = (bf16[256,128]{1,0:T(8,128)(2,1)S(1)}, bf16[256,128]{1,0:T(8,128)(2,1)S(1)}, u32[]{:S(2)}, u32[]{:S(2)}) collective-permute-start(bf16[256,128]{1,0:T(8,128)(2,1)S(1)} %get-tuple-element.69), channel_id=1, source_target_pairs={{0,8},{4,12},{8,0},{12,4},{1,9},{5,13},{9,1},{13,5},{2,10},{6,14},... | collective-permute-start | bytes 196616 | tf_op jit(solution)/shard_map/ppermute | solution.py:597
  36.9 6.1 %collective-permute-start.8 = (bf16[256,128]{1,0:T(8,128)(2,1)S(1)}, bf16[256,128]{1,0:T(8,128)(2,1)S(1)}, u32[]{:S(2)}, u32[]{:S(2)}) collective-permute-start(bf16[256,128]{1,0:T(8,128)(2,1)S(1)} %get-tuple-element.70), channel_id=1, source_target_pairs={{0,12},{4,8},{8,4},{12,0},{1,13},{5,9},{9,5},{13,1},{2,14},{6,10},... | collective-permute-start | bytes 196616 | tf_op jit(solution)/shard_map/ppermute | solution.py:597
  43.8 1.9 %collective-permute-start.9 = (bf16[256,128]{1,0:T(8,128)(2,1)S(1)}, bf16[256,128]{1,0:T(8,128)(2,1)S(1)}, u32[]{:S(2)}, u32[]{:S(2)}) collective-permute-start(bf16[256,128]{1,0:T(8,128)(2,1)S(1)} %get-tuple-element.73), channel_id=1, source_target_pairs={{0,1},{1,0},{2,3},{3,2},{4,5},{5,4},{6,7},{7,6},{8,9},{9,8},{10,11... | collective-permute-start | bytes 196616 | tf_op jit(solution)/shard_map/ppermute | solution.py:597
  43.9 4.5 %collective-permute-start.10 = (bf16[256,128]{1,0:T(8,128)(2,1)S(1)}, bf16[256,128]{1,0:T(8,128)(2,1)S(1)}, u32[]{:S(2)}, u32[]{:S(2)}) collective-permute-start(bf16[256,128]{1,0:T(8,128)(2,1)S(1)} %get-tuple-element.74), channel_id=1, source_target_pairs={{0,2},{1,3},{2,0},{3,1},{4,6},{5,7},{6,4},{7,5},{8,10},{9,11},{10,... | collective-permute-start | bytes 196616 | tf_op jit(solution)/shard_map/ppermute | solution.py:597
  45.4 4.0 %collective-permute-start.11 = (bf16[256,128]{1,0:T(8,128)(2,1)S(1)}, bf16[256,128]{1,0:T(8,128)(2,1)S(1)}, u32[]{:S(2)}, u32[]{:S(2)}) collective-permute-start(bf16[256,128]{1,0:T(8,128)(2,1)S(1)} %get-tuple-element.75), channel_id=1, source_target_pairs={{0,3},{1,2},{2,1},{3,0},{4,7},{5,6},{6,5},{7,4},{8,11},{9,10},{10,... | collective-permute-start | bytes 196616 | tf_op jit(solution)/shard_map/ppermute | solution.py:597
  49.5 21.9 %copy-start.7 = (bf16[4,2,32,1024]{3,2,1,0:T(8,128)(2,1)S(1)}, bf16[4,2,32,1024]{3,2,1,0:T(8,128)(2,1)}, u32[]{:S(2)}) copy-start(bf16[4,2,32,1024]{3,2,1,0:T(8,128)(2,1)} %constant.34.clone.xr) | copy-start | bytes 1572868
  49.5 21.9 %copy-start.10 = (bf16[4,32,256]{2,1,0:T(8,128)(2,1)S(1)}, bf16[4,32,256]{2,1,0:T(8,128)(2,1)}, u32[]{:S(2)}) copy-start(bf16[4,32,256]{2,1,0:T(8,128)(2,1)} %constant.36.clone.xd) | copy-start | bytes 196612
  55.3 6.6 %collective-permute-start.12 = (bf16[256,128]{1,0:T(8,128)(2,1)S(1)}, bf16[256,128]{1,0:T(8,128)(2,1)S(1)}, u32[]{:S(2)}, u32[]{:S(2)}) collective-permute-start(bf16[256,128]{1,0:T(8,128)(2,1)S(1)} %get-tuple-element.82), channel_id=1, source_target_pairs={{0,1},{1,0},{2,3},{3,2},{4,5},{5,4},{6,7},{7,6},{8,9},{9,8},{10,11... | collective-permute-start | bytes 196616 | tf_op jit(solution)/shard_map/ppermute | solution.py:597
  55.5 6.4 %collective-permute-start.13 = (bf16[256,128]{1,0:T(8,128)(2,1)S(1)}, bf16[256,128]{1,0:T(8,128)(2,1)S(1)}, u32[]{:S(2)}, u32[]{:S(2)}) collective-permute-start(bf16[256,128]{1,0:T(8,128)(2,1)S(1)} %get-tuple-element.83), channel_id=1, source_target_pairs={{0,2},{1,3},{2,0},{3,1},{4,6},{5,7},{6,4},{7,5},{8,10},{9,11},{10,... | collective-permute-start | bytes 196616 | tf_op jit(solution)/shard_map/ppermute | solution.py:597
  56.9 5.0 %collective-permute-start.14 = (bf16[256,128]{1,0:T(8,128)(2,1)S(1)}, bf16[256,128]{1,0:T(8,128)(2,1)S(1)}, u32[]{:S(2)}, u32[]{:S(2)}) collective-permute-start(bf16[256,128]{1,0:T(8,128)(2,1)S(1)} %get-tuple-element.84), channel_id=1, source_target_pairs={{0,3},{1,2},{2,1},{3,0},{4,7},{5,6},{6,5},{7,4},{8,11},{9,10},{10,... | collective-permute-start | bytes 196616 | tf_op jit(solution)/shard_map/ppermute | solution.py:597
  59.0 1.4 %collective-permute-start.24 = (f32[96,128]{1,0:T(8,128)S(1)}, f32[96,128]{1,0:T(8,128)S(1)}, u32[]{:S(2)}, u32[]{:S(2)}) collective-permute-start(f32[96,128]{1,0:T(8,128)S(1)} %sums.1.after), channel_id=1, source_target_pairs={{0,1},{1,0},{2,3},{3,2},{4,5},{5,4},{6,7},{7,6},{8,9},{9,8},{10,11... | collective-permute-start | bytes 147464 | tf_op jit(solution)/shard_map/ppermute | solution.py:605
  60.4 6.8 %collective-permute-start.25 = (f32[96,128]{1,0:T(8,128)S(1)}, f32[96,128]{1,0:T(8,128)S(1)}, u32[]{:S(2)}, u32[]{:S(2)}) collective-permute-start(f32[96,128]{1,0:T(8,128)S(1)} %add.16), channel_id=1, source_target_pairs={{0,2},{2,0},{1,3},{3,1},{4,6},{6,4},{5,7},{7,5},{8,10},{10,8},{9,1... | collective-permute-start | bytes 147464 | tf_op jit(solution)/shard_map/ppermute | solution.py:605
  62.8 5.3 %collective-permute-start.15 = (bf16[256,128]{1,0:T(8,128)(2,1)S(1)}, bf16[256,128]{1,0:T(8,128)(2,1)S(1)}, u32[]{:S(2)}, u32[]{:S(2)}) collective-permute-start(bf16[256,128]{1,0:T(8,128)(2,1)S(1)} %get-tuple-element.90), channel_id=1, source_target_pairs={{0,4},{4,0},{8,12},{12,8},{1,5},{5,1},{9,13},{13,9},{2,6},{6,2},{1... | collective-permute-start | bytes 196616 | tf_op jit(solution)/shard_map/ppermute | solution.py:597
  62.8 8.6 %collective-permute-start.16 = (bf16[256,128]{1,0:T(8,128)(2,1)S(1)}, bf16[256,128]{1,0:T(8,128)(2,1)S(1)}, u32[]{:S(2)}, u32[]{:S(2)}) collective-permute-start(bf16[256,128]{1,0:T(8,128)(2,1)S(1)} %get-tuple-element.91), channel_id=1, source_target_pairs={{0,8},{4,12},{8,0},{12,4},{1,9},{5,13},{9,1},{13,5},{2,10},{6,14},... | collective-permute-start | bytes 196616 | tf_op jit(solution)/shard_map/ppermute | solution.py:597
  64.7 6.7 %collective-permute-start.17 = (bf16[256,128]{1,0:T(8,128)(2,1)S(1)}, bf16[256,128]{1,0:T(8,128)(2,1)S(1)}, u32[]{:S(2)}, u32[]{:S(2)}) collective-permute-start(bf16[256,128]{1,0:T(8,128)(2,1)S(1)} %get-tuple-element.92), channel_id=1, source_target_pairs={{0,12},{4,8},{8,4},{12,0},{1,13},{5,9},{9,5},{13,1},{2,14},{6,10},... | collective-permute-start | bytes 196616 | tf_op jit(solution)/shard_map/ppermute | solution.py:597
  67.2 13.5 %collective-permute-start.26 = (f32[96,128]{1,0:T(8,128)S(1)}, f32[96,128]{1,0:T(8,128)S(1)}, u32[]{:S(2)}, u32[]{:S(2)}) collective-permute-start(f32[96,128]{1,0:T(8,128)S(1)} %add.17), channel_id=1, source_target_pairs={{0,4},{4,0},{8,12},{12,8},{1,5},{5,1},{9,13},{13,9},{2,6},{6,2},{1... | collective-permute-start | bytes 147464 | tf_op jit(solution)/shard_map/ppermute | solution.py:605
  76.3 12.2 %collective-permute-start.18 = (bf16[256,128]{1,0:T(8,128)(2,1)S(1)}, bf16[256,128]{1,0:T(8,128)(2,1)S(1)}, u32[]{:S(2)}, u32[]{:S(2)}) collective-permute-start(bf16[256,128]{1,0:T(8,128)(2,1)S(1)} %get-tuple-element.94), channel_id=1, source_target_pairs={{0,4},{4,0},{8,12},{12,8},{1,5},{5,1},{9,13},{13,9},{2,6},{6,2},{1... | collective-permute-start | bytes 196616 | tf_op jit(solution)/shard_map/ppermute | solution.py:597
  77.8 10.7 %collective-permute-start.19 = (bf16[256,128]{1,0:T(8,128)(2,1)S(1)}, bf16[256,128]{1,0:T(8,128)(2,1)S(1)}, u32[]{:S(2)}, u32[]{:S(2)}) collective-permute-start(bf16[256,128]{1,0:T(8,128)(2,1)S(1)} %get-tuple-element.95), channel_id=1, source_target_pairs={{0,8},{4,12},{8,0},{12,4},{1,9},{5,13},{9,1},{13,5},{2,10},{6,14},... | collective-permute-start | bytes 196616 | tf_op jit(solution)/shard_map/ppermute | solution.py:597
  78.9 9.6 %collective-permute-start.20 = (bf16[256,128]{1,0:T(8,128)(2,1)S(1)}, bf16[256,128]{1,0:T(8,128)(2,1)S(1)}, u32[]{:S(2)}, u32[]{:S(2)}) collective-permute-start(bf16[256,128]{1,0:T(8,128)(2,1)S(1)} %get-tuple-element.96), channel_id=1, source_target_pairs={{0,12},{4,8},{8,4},{12,0},{1,13},{5,9},{9,5},{13,1},{2,14},{6,10},... | collective-permute-start | bytes 196616 | tf_op jit(solution)/shard_map/ppermute | solution.py:597
  80.7 10.6 %collective-permute-start.27 = (f32[96,128]{1,0:T(8,128)S(1)}, f32[96,128]{1,0:T(8,128)S(1)}, u32[]{:S(2)}, u32[]{:S(2)}) collective-permute-start(f32[96,128]{1,0:T(8,128)S(1)} %add.18), channel_id=1, source_target_pairs={{0,8},{4,12},{8,0},{12,4},{1,9},{5,13},{9,1},{13,5},{2,10},{6,14},... | collective-permute-start | bytes 147464 | tf_op jit(solution)/shard_map/ppermute | solution.py:605
  89.4 10.3 %collective-permute-start.21 = (bf16[256,128]{1,0:T(8,128)(2,1)S(1)}, bf16[256,128]{1,0:T(8,128)(2,1)S(1)}, u32[]{:S(2)}, u32[]{:S(2)}) collective-permute-start(bf16[256,128]{1,0:T(8,128)(2,1)S(1)} %get-tuple-element.101), channel_id=1, source_target_pairs={{0,1},{1,0},{2,3},{3,2},{4,5},{5,4},{6,7},{7,6},{8,9},{9,8},{10,11... | collective-permute-start | bytes 196616 | tf_op jit(solution)/shard_map/ppermute | solution.py:597
  89.4 10.2 %collective-permute-start.22 = (bf16[256,128]{1,0:T(8,128)(2,1)S(1)}, bf16[256,128]{1,0:T(8,128)(2,1)S(1)}, u32[]{:S(2)}, u32[]{:S(2)}) collective-permute-start(bf16[256,128]{1,0:T(8,128)(2,1)S(1)} %get-tuple-element.102), channel_id=1, source_target_pairs={{0,2},{1,3},{2,0},{3,1},{4,6},{5,7},{6,4},{7,5},{8,10},{9,11},{10,... | collective-permute-start | bytes 196616 | tf_op jit(solution)/shard_map/ppermute | solution.py:597
  90.1 9.6 %collective-permute-start.23 = (bf16[256,128]{1,0:T(8,128)(2,1)S(1)}, bf16[256,128]{1,0:T(8,128)(2,1)S(1)}, u32[]{:S(2)}, u32[]{:S(2)}) collective-permute-start(bf16[256,128]{1,0:T(8,128)(2,1)S(1)} %get-tuple-element.103), channel_id=1, source_target_pairs={{0,3},{1,2},{2,1},{3,0},{4,7},{5,6},{6,5},{7,4},{8,11},{9,10},{10,... | collective-permute-start | bytes 196616 | tf_op jit(solution)/shard_map/ppermute | solution.py:597
  (11 other events, 92.5 us)

commit v2 on v1

--- a/solution.py
+++ b/solution.py
@@ -212,6 +212,7 @@
 
 BF = jnp.bfloat16
 F32 = jnp.float32
+STEPS = (0, 2, 3, 1)
 
 
 def z_forward_kernel(rows, yrows, zlen, idx, field, zf, o0, o1, o2, o3, held, tab, wide, sem):
@@ -225,20 +226,16 @@
         [wide[pl.ds(y, rows, stride=yrows), :].astype(BF) for y in range(yrows)], axis=1
     )
     second.wait()
-    table = jnp.concatenate([tab[idx[0] ^ s] for s in range(4)], axis=1)
+    table = jnp.concatenate([tab[idx[0] ^ STEPS[s]] for s in range(4)], axis=1)
     out = dot(side, table).astype(BF)
     for s, o in enumerate((o0, o1, o2, o3)):
         o[...] = out[:, s * 128 : (s + 1) * 128]
 
 
-def lane_kernel(near, far, idx, r0, r1, r2, r3, table, after, o0, o1, o2, o3):
+def lane_kernel(idx, r0, r1, r2, r3, table, after, o0, o1, o2, o3):
     side = jnp.concatenate([r0[...], r1[...], r2[...], r3[...]], axis=1)
-    cols = []
-    for t in range(4):
-        cols.append(
-            jnp.concatenate([table[idx[near] ^ s, idx[far] ^ t] for s in range(4)], axis=0)
-        )
-    out = dot(side, jnp.concatenate(cols, axis=1)).astype(BF)
+    known = table[...] if len(table.shape) == 2 else lane_table(idx, 0, 1, table)
+    out = dot(side, known).astype(BF)
     for t, o in enumerate((o0, o1, o2, o3)):
         o[...] = out[:, t * 128 : (t + 1) * 128]
 
@@ -250,33 +247,49 @@
         turned = block.astype(F32).T.astype(BF)
         parts.append(jnp.concatenate([turned[:64, :], turned[64:, :]], axis=1))
     side = jnp.concatenate(parts, axis=0)
-    table = jnp.concatenate([tab[idx[1] ^ s, p] for p in range(2) for s in range(4)], axis=0)
+    table = jnp.concatenate([tab[idx[1] ^ STEPS[s], p] for p in range(2) for s in range(4)], axis=0)
     return side, table
 
 
-def mix_forward_kernel(idx, r0, r1, r2, r3, xf, xi, early, late, modes, o0, o1, o2, o3):
+def add_products(total, weight, modes, o, first):
+    real, imag = total
+    for g in range(weight.shape[0]):
+        wr, wi = weight[g, 0, o].astype(F32), weight[g, 1, o].astype(F32)
+        mr, mi = modes[first + g, 0].astype(F32), modes[first + g, 1].astype(F32)
+        real = real + wr * mr - wi * mi
+        imag = imag + wr * mi + wi * mr
+    return real, imag
+
+
+def mix_forward_kernel(
+    idx, r0, r1, r2, r3, xf, xi, early, late, weight, modes, o0, o1, o2, o3, last,
+    total, held, sem,
+):
+    known = early.shape[0] + late.shape[0]
+    copies = pack_copies(known, weight, held, sem)
     side, table = x_side(idx, (r0, r1, r2, r3), xf)
     got = dot(side, table).astype(BF)
     for g in range(8):
-        modes[g, 0] = got[g * 64 : (g + 1) * 64, :128]
-        modes[g, 1] = got[g * 64 : (g + 1) * 64, 128:]
-    left = jnp.concatenate([xi[idx[1] ^ s] for s in range(4)], axis=0).astype(BF)
+        for p in range(2):
+            part = got[g * 64 : (g + 1) * 64, p * 128 : (p + 1) * 128]
+            modes[g, p] = part
+    left = jnp.concatenate([xi[idx[1] ^ STEPS[s]] for s in range(4)], axis=0).astype(BF)
     outs = (o0, o1, o2, o3)
+    zero = jnp.zeros((64, 128), F32)
+
+    def begin(o, carry):
+        got = add_products((zero, zero), early, modes, o, 0)
+        total[o, 0], total[o, 1] = add_products(got, late, modes, o, early.shape[0])
+        return carry
+
+    lax.fori_loop(0, 32, begin, 0, unroll=2)
+    pack_finish(copies, held, last)
 
     def pair(k, carry):
         rows = []
         for j in range(2):
             o = 2 * k + j
-            real = jnp.zeros((64, 128), F32)
-            imag = jnp.zeros((64, 128), F32)
-            for g in range(8):
-                weight, at = (early, g) if g < EARLY else (late, g - EARLY)
-                wr = weight[at, 0, o].astype(F32)
-                wi = weight[at, 1, o].astype(F32)
-                mr = modes[g, 0].astype(F32)
-                mi = modes[g, 1].astype(F32)
-                real = real + wr * mr - wi * mi
-                imag = imag + wr * mi + wi * mr
+            real, imag = add_products((total[o, 0], total[o, 1]), last, modes, o, known)
             rows.append(jnp.concatenate([real.astype(BF), (-imag).astype(BF)], axis=1))
             rows.append(jnp.concatenate([imag.astype(BF), real.astype(BF)], axis=1))
         got = dot_nt(left, jnp.concatenate(rows, axis=0))
@@ -287,17 +300,20 @@
             outs[s][pl.ds(pl.multiple_of(k * 16, 16), 16), :] = both.astype(BF)
         return carry
 
-    lax.fori_loop(0, 16, pair, 0)
-
-
-def mix_backward_kernel(idx, r0, r1, r2, r3, xr, xd, early, late, pmodes, o0, o1, o2, o3):
+    lax.fori_loop(0, 16, pair, 0, unroll=2)
+
+
+def mix_backward_kernel(
+    idx, r0, r1, r2, r3, xr, xd, early, late, last, pmodes, o0, o1, o2, o3
+):
     side, table = x_side(idx, (r0, r1, r2, r3), xr)
     for d in range(4):
         got = dot(side, table[:, d * 256 : (d + 1) * 256]).astype(BF)
         for g in range(8):
-            pmodes[4 * g + d, 0] = got[g * 64 : (g + 1) * 64, :128]
-            pmodes[4 * g + d, 1] = got[g * 64 : (g + 1) * 64, 128:]
-    left = jnp.concatenate([xd[idx[1] ^ s] for s in range(4)], axis=0)
+            for p in range(2):
+                part = got[g * 64 : (g + 1) * 64, p * 128 : (p + 1) * 128]
+                pmodes[4 * g + d, p] = part
+    left = jnp.concatenate([xd[idx[1] ^ STEPS[s]] for s in range(4)], axis=0)
     outs = (o0, o1, o2, o3)
 
     def group(weight, first, at, carry):
@@ -305,10 +321,8 @@
         real = jnp.zeros((64, 128), F32)
         imag = jnp.zeros((64, 128), F32)
         for o in range(32):
-            wr = weight[at, 0, o].astype(F32)
-            wi = weight[at, 1, o].astype(F32)
-            pr = pmodes[o, 0].astype(F32)
-            pi = pmodes[o, 1].astype(F32)
+            wr, wi = weight[at, 0, o].astype(F32), weight[at, 1, o].astype(F32)
+            pr, pi = pmodes[o, 0].astype(F32), pmodes[o, 1].astype(F32)
             real = real + wr * pr + wi * pi
             imag = imag + wr * pi - wi * pr
         rows = [
@@ -320,25 +334,34 @@
             outs[s][pl.ds(pl.multiple_of(g * 32, 32), 32), :] = got[s * 32 : (s + 1) * 32]
         return carry
 
-    lax.fori_loop(0, EARLY, functools.partial(group, early, 0), 0)
-    lax.fori_loop(0, 8 - EARLY, functools.partial(group, late, EARLY), 0)
-
-
-def pack_kernel(first, weight, after, packed, token, held, sem):
-    count, half = packed.shape[0], packed.shape[2] // 2
-
-    def copy(g, h):
-        part = pl.ds(h * half, half)
-        return pltpu.make_async_copy(
-            weight.at[:, pl.ds(4 * (first + g), 4), part], held.at[g, :, :, part], sem.at[g, h]
-        )
-
-    for g in range(count):
-        for h in range(2):
-            copy(g, h).start()
-    for g in range(count):
-        for h in range(2):
-            copy(g, h).wait()
+    first = 0
+    for weight in (early, late, last):
+        lax.fori_loop(0, weight.shape[0], functools.partial(group, weight, first), 0)
+        first += weight.shape[0]
+
+
+def pack_copies(first, weight, held, sem):
+    span = held.shape[3] // 4
+    copies = []
+    for g in range(held.shape[0]):
+        for h in range(4):
+            part = pl.ds(h * span, span)
+            copies.append(
+                pltpu.make_async_copy(
+                    weight.at[:, pl.ds(4 * (first + g), 4), part],
+                    held.at[g, :, :, part],
+                    sem.at[g, h],
+                )
+            )
+            copies[-1].start()
+    return copies
+
+
+def pack_finish(copies, held, packed):
+    span = held.shape[3] // 4
+    for g in range(held.shape[0]):
+        for h in range(4):
+            copies[4 * g + h].wait()
 
             def step(o, carry):
                 for p in range(2):
@@ -347,20 +370,23 @@
                     )
                 return carry
 
-            lax.fori_loop(h * half, (h + 1) * half, step, 0, unroll=8)
+            lax.fori_loop(h * span, (h + 1) * span, step, 0, unroll=8)
+
+
+def pack_kernel(first, weight, after, packed, token, held, sem):
+    pack_finish(pack_copies(first, weight, held, sem), held, packed)
     token[...] = jnp.zeros_like(token)
 
 
-def outer_kernel(start, count, modes, pmodes, *rest):
-    grad, token, held, turned, sem = rest[-5:]
-    half = pmodes.shape[0] // 2
+def outer_start(start, modes, pmodes, grad, held, turned, sem):
+    span = pmodes.shape[0] // 4
     copies = []
-    for g in range(count):
+    for g in range(held.shape[0]):
         for p in range(2):
             m = modes[start + g, p].astype(F32)
             for k in range(4):
                 turned[k, p] = (pltpu.roll(m, (128 - 32 * k) % 128, 1) if k else m).astype(BF)
-        for h in range(2):
+        for h in range(4):
 
             def step(o, carry):
                 pr, pi = pmodes[o, 0], pmodes[o, 1]
@@ -370,8 +396,8 @@
                     held[g, 1, k, o] = (mr * pi - mi * pr)[:, :32]
                 return carry
 
-            lax.fori_loop(h * half, (h + 1) * half, step, 0, unroll=4)
-            part = pl.ds(h * half, half)
+            lax.fori_loop(h * span, (h + 1) * span, step, 0, unroll=8)
+            part = pl.ds(h * span, span)
             copies.append(
                 pltpu.make_async_copy(
                     held.at[g, :, :, part],
@@ -380,7 +406,20 @@
                 )
             )
             copies[-1].start()
-    for copy in copies:
+    return copies
+
+
+def outer_scratch(count, chans):
+    return [
+        pltpu.VMEM((count, 2, 4, chans, 64, 32), BF),
+        pltpu.VMEM((4, 2, 64, 128), BF),
+        pltpu.SemaphoreType.DMA((count, 4)),
+    ]
+
+
+def outer_kernel(start, modes, pmodes, *rest):
+    grad, token, held, turned, sem = rest[-5:]
+    for copy in outer_start(start, modes, pmodes, grad, held, turned, sem):
         copy.wait()
     token[...] = jnp.zeros_like(token)
 
@@ -405,7 +444,22 @@
     return jnp.where(at_row == at_lane, tall, 0.0).astype(BF)
 
 
-def cells_kernel(field, cotangent, skip, lift_t, proj, fx, cx, dskip, dskip_t, dlift, dlift_t, dproj, wide):
+def by_step(idx, at, table, axis):
+    return jnp.concatenate([table[idx[at] ^ STEPS[s]] for s in range(4)], axis=axis)
+
+
+def lane_table(idx, near, far, table):
+    cols = []
+    for t in range(4):
+        rows = [table[idx[near] ^ STEPS[s], idx[far] ^ STEPS[t]] for s in range(4)]
+        cols.append(jnp.concatenate(rows, axis=0))
+    return jnp.concatenate(cols, axis=1)
+
+
+def cells_kernel(
+    idx, field, cotangent, skip, lift_t, proj, zf, zi, yf, yi,
+    fx, cx, skipped, backed, dskip_t, dlift, dlift_t, zfp, zip_, yfp, yip, wide,
+):
     for src, dst in ((field, fx), (cotangent, cx)):
         wide[...] = src[...].astype(F32)
 
@@ -422,16 +476,22 @@
             return carry
 
         lax.fori_loop(0, 4, step, 0)
-    dskip[...] = spread(skip[...], 8)
+    dskip = spread(skip[...], 8)
+    dproj = spread(turn(proj[...]), 8)
+    for k in range(4):
+        skipped[k] = dot(dskip, fx[k])
+        backed[k] = dot(dproj, cx[k])
+    zfp[...] = by_step(idx, 0, zf, 1)
+    zip_[...] = by_step(idx, 0, zi, 0)
+    yfp[...] = lane_table(idx, 0, 1, yf)
+    yip[...] = lane_table(idx, 1, 0, yi)
     dskip_t[...] = spread(turn(skip[...]), 8)
     dlift[...] = spread(turn(lift_t[...]), 8)
     dlift_t[...] = spread(lift_t[...], 2)
-    dproj[...] = spread(turn(proj[...]), 8)
-
-
-def inverse_z(idx, refs, zi, spectral):
+
+
+def inverse_z(refs, back, spectral):
     side = jnp.concatenate([r[...] for r in refs], axis=1)
-    back = jnp.concatenate([zi[idx[0] ^ s] for s in range(4)], axis=0)
     for y in range(4):
         got = dot(side, back[:, y * 256 : (y + 1) * 256])
         spectral[2 * y] = got[:, :128]
@@ -449,24 +509,23 @@
 
 
 def point_kernel(
-    idx, r0, r1, r2, r3, zi, zf, fx, cx, dskip, dlift, dlift_t, dproj,
+    r0, r1, r2, r3, back, table, cx, skipped, backed, dlift, dlift_t,
     o0, o1, o2, o3, pg, act, hid, lif, spectral, wide,
 ):
-    inverse_z(idx, (r0, r1, r2, r3), zi, spectral)
+    inverse_z((r0, r1, r2, r3), back, spectral)
 
     def step(k, carry):
-        values, grads = fx[k], cx[k]
-        pre = cell_rows(spectral, k) + dot(dskip[...], values)
+        grads = cx[k]
+        pre = cell_rows(spectral, k) + skipped[k]
         lifted, slope_pre = gelu_pair(pre)
         lifted = lifted.astype(BF)
         lif[k] = lifted
         hidden = dot(dlift[...], lifted)
-        backed = dot(dproj[...], grads)
         up = []
         for q in range(4):
             part = slice(q * 256, (q + 1) * 256)
             activated, slope_hid = gelu_pair(hidden[part])
-            hidden_grad = (backed[part] * slope_hid).astype(BF)
+            hidden_grad = (backed[k, part] * slope_hid).astype(BF)
             act[k, part] = activated.astype(BF)
             hid[k, part] = hidden_grad
             up.append(dot(dlift_t[...], hidden_grad))
@@ -481,9 +540,8 @@
         return carry
 
     lax.fori_loop(0, 4, step, 0, unroll=2)
-    table = jnp.concatenate([zf[idx[0] ^ s] for s in range(4)], axis=1)
     side = jnp.concatenate([wide[y].astype(BF) for y in range(8)], axis=1)
-    out = dot(side, table).astype(BF)
+    out = dot(side, table[...]).astype(BF)
     for s, o in enumerate((o0, o1, o2, o3)):
         o[...] = out[:, s * 128 : (s + 1) * 128]
 
@@ -506,8 +564,14 @@
     sums[64:96] = jnp.concatenate([got[2]] * 4, axis=1)
 
 
-def finish_kernel(idx, r0, r1, r2, r3, zi, pg, dskip_t, out, spectral, wide):
-    inverse_z(idx, (r0, r1, r2, r3), zi, spectral)
+def finish_kernel(
+    r0, r1, r2, r3, back, pg, dskip_t, part, other, out, proj, lift, skip, spectral, wide
+):
+    sums = part[...] + other[...]
+    proj[...] = sums[:32]
+    lift[...] = sums[32:64]
+    skip[...] = sums[64:, :32]
+    inverse_z((r0, r1, r2, r3), back, spectral)
 
     def step(k, carry):
         got = cell_rows(spectral, k) + dot(dskip_t[...], pg[k])
@@ -523,7 +587,8 @@
     out[...] = wide[...].astype(BF)
 
 
-EARLY = 3
+PACK = (2, 3, 3)
+OUTER = (4, 4)
 VM = pl.BlockSpec(memory_space=pltpu.VMEM)
 ANY = pl.BlockSpec(memory_space=pl.ANY)
 HBM = pl.BlockSpec(memory_space=pltpu.HBM)
@@ -536,16 +601,16 @@
     return pl.CostEstimate(flops=0, bytes_accessed=int(us * 3.0e6), transcendentals=0)
 
 
-def call(kernel, ins, outs, scratch=(), name=None, mib=8, us=1.0, smem=1, free=0, hbm=()):
-    specs = [SM] * smem + [VM] * (len(ins) - smem - free) + [ANY] * free
-    for at in hbm:
-        specs[at] = HBM
+def call(
+    kernel, ins, outs, scratch=(), name=None, mib=8, us=1.0, smem=1, free=0, far_out=(), alias={}
+):
     return pl.pallas_call(
         kernel,
         out_shape=outs,
-        in_specs=specs,
-        out_specs=jax.tree.map(lambda _: VM, outs),
+        in_specs=[SM] * smem + [VM] * (len(ins) - smem - free) + [ANY] * free,
+        out_specs=[ANY if at in far_out else VM for at in range(len(outs))],
         scratch_shapes=list(scratch),
+        input_output_aliases=alias,
         compiler_params=pltpu.CompilerParams(vmem_limit_bytes=mib * MIB),
         cost_estimate=cost(us),
         name=name,
@@ -564,7 +629,7 @@
         out_specs=[VM, VM],
         scratch_shapes=[
             pltpu.VMEM((count, 2, 4, chans, 64, 32), BF),
-            pltpu.SemaphoreType.DMA((count, 2)),
+            pltpu.SemaphoreType.DMA((count, 4)),
         ],
         compiler_params=pltpu.CompilerParams(vmem_limit_bytes=36 * MIB),
         cost_estimate=cost(us),
@@ -572,39 +637,17 @@
     )(weight, after)
 
 
-def outer(modes, pmodes, first, count, so_far, after, us):
-    chans = pmodes.shape[0]
-    extra = [] if so_far is None else [so_far, after]
-    return pl.pallas_call(
-        functools.partial(outer_kernel, first, count),
-        out_shape=[jax.ShapeDtypeStruct((2, chans, chans, 64, 32), BF), TOKEN],
-        in_specs=[VM, VM] + [ANY] * len(extra),
-        out_specs=[ANY, VM],
-        scratch_shapes=[
-            pltpu.VMEM((count, 2, 4, chans, 64, 32), BF),
-            pltpu.VMEM((4, 2, 64, 128), BF),
-            pltpu.SemaphoreType.DMA((count, 2)),
-        ],
-        input_output_aliases={} if so_far is None else {2: 0},
-        compiler_params=pltpu.CompilerParams(vmem_limit_bytes=24 * MIB),
-        cost_estimate=cost(us),
-        name="outer",
-    )(modes, pmodes, *extra)
-
-
 def exchange(blocks, axes):
-    pairs = [[(a, a ^ s) for a in range(4)] for s in range(4)]
-    got = {s: lax.ppermute(blocks[s], axes, pairs[s]) for s in (2, 3, 1)}
-    return [blocks[0], got[1], got[2], got[3]]
-
-
-def sum_over(part, axes):
-    for axis, size in axes:
-        step = 1
-        while step < size:
-            part = part + lax.ppermute(part, axis, [(a, a ^ step) for a in range(size)])
-            step *= 2
-    return part
+    got = [
+        lax.ppermute(block, axes, [(a, a ^ step) for a in range(4)])
+        for block, step in zip(blocks[1:], STEPS[1:])
+    ]
+    return [blocks[0]] + got
+
+
+def swap(part, axis, step):
+    size = lax.axis_size(axis)
+    return lax.ppermute(part, axis, [(a, a ^ step) for a in range(size)])
 
 
 def fast(field, cotangent, mode_weight, skip_weight, lift_weight, proj_weight):
@@ -626,11 +669,8 @@
     def bf(*shape):
         return jax.ShapeDtypeStruct(shape, BF)
 
-    def lanes(near, far, got, table, after, name):
-        return call(
-            functools.partial(lane_kernel, near, far),
-            (idx, *got, table, after), four, (), name, 4, 1.0, free=1,
-        )
+    def lanes(got, table, after, name):
+        return call(lane_kernel, (idx, *got, table, after), four, (), name, 4, 1.0, free=1)
 
     sent = call(
         functools.partial(z_forward_kernel, rows, yrows, zlen),
@@ -641,60 +681,82 @@
             wide,
             pltpu.SemaphoreType.DMA((2,)),
         ],
-        "z_forward", 8, 2.0, hbm=(1, 2),
+        "z_forward", 8, 2.0, free=2,
     )
     got = exchange(sent, gyc)
-    early, token = pack(weight, 0, EARLY, sent[0], 4.0)
-    sent = lanes(0, 1, got, yf, token, "y_forward")
+    one, two, three = PACK
+    early, token = pack(weight, 0, one, sent[0], 3.0)
+    sent = lanes(got, yf, token, "y_forward")
     got = exchange(sent, "gx")
-    late, _ = pack(weight, EARLY, 8 - EARLY, sent[0], 8.0)
-    modes, *sent = call(
-        mix_forward_kernel, (idx, *got, xf, xi, early, late),
-        [bf(8, 2, 64, 128)] + four, (), "mix_forward", 12, 5.0,
+    late, _ = pack(weight, one, two, sent[0], 5.0)
+    modes, *sent, last = call(
+        mix_forward_kernel, (idx, *got, xf, xi, early, late, weight),
+        [bf(8, 2, 64, 128)] + four + [bf(three, 2, chans, 64, 128)],
+        [
+            pltpu.VMEM((chans, 2, 64, 128), F32),
+            pltpu.VMEM((three, 2, 4, chans, 64, 32), BF),
+            pltpu.SemaphoreType.DMA((three, 4)),
+        ],
+        "mix_forward", 36, 8.0, free=1,
     )
     got = exchange(sent, "gx")
-    fx, cx, dskip, dskip_t, dlift, dlift_t, dproj = call(
+    fx, cx, skipped, backed, dskip_t, dlift, dlift_t, zfp, zip_, yfp, yip = call(
         cells_kernel,
-        (flat_field, flat_cot, skip_weight, lift_t, proj_weight),
+        (idx, flat_field, flat_cot, skip_weight, lift_t, proj_weight, zf, zi, yf, yi),
         [bf(4, 256, 256)] * 2
-        + [bf(256, 256), bf(256, 256), bf(1024, 256), bf(64, 256), bf(1024, 256)],
-        [wide], "cells", 8, 3.0, 0,
-    )
-    sent = lanes(1, 0, got, yi, fx, "y_inverse")
+        + [jax.ShapeDtypeStruct((4, 256, 256), F32), jax.ShapeDtypeStruct((4, 1024, 256), F32)]
+        + [bf(256, 256), bf(1024, 256), bf(64, 256)]
+        + [bf(1024, 512), bf(512, 1024), bf(512, 512), bf(512, 512)],
+        [wide], "cells", 8, 3.0,
+    )
+    sent = lanes(got, yip, fx, "y_inverse")
     got = exchange(sent, gyc)
     *sent, pg, act, hid, lif = call(
         point_kernel,
-        (idx, *got, zi, zf, fx, cx, dskip, dlift, dlift_t, dproj),
+        (*got, zip_, zfp, cx, skipped, backed, dlift, dlift_t),
         four + [bf(4, 256, 256), bf(4, 1024, 256), bf(4, 1024, 256), bf(4, 256, 256)],
-        [tall, tall], "point", 16, 8.0,
+        [tall, tall], "point", 8, 6.0, 0,
     )
     got = exchange(sent, gyc)
-    part = call(
+    (part,) = call(
         sums_kernel, (fx, cx, pg, act, hid, lif),
-        jax.ShapeDtypeStruct((96, 128), F32), (), "sums", 4, 2.5, 0,
-    )
-    sent = lanes(0, 1, got, yf, part, "y_forward")
+        [jax.ShapeDtypeStruct((96, 128), F32)], (), "sums", 4, 2.5, 0,
+    )
+    sent = lanes(got, yfp, part, "y_forward")
     got = exchange(sent, "gx")
+    for axis in ("col", "gy", "gx"):
+        part = part + swap(part, axis, 1)
+    other = swap(part, "gx", 2)
+    grads = bf(2, chans, chans, 64, 32)
+    begin, end = OUTER
     pmodes, *sent = call(
-        mix_backward_kernel, (idx, *got, xr, xd, early, late),
+        mix_backward_kernel, (idx, *got, xr, xd, early, late, last),
         [bf(32, 2, 64, 128)] + four, (), "mix_backward", 12, 5.0,
     )
     got = exchange(sent, "gx")
-    grad, token = outer(modes, pmodes, 0, 4, None, None, 6.0)
-    sent = lanes(1, 0, got, yi, token, "y_inverse")
+    grad, token = call(
+        functools.partial(outer_kernel, 0), (modes, pmodes), [grads, TOKEN],
+        outer_scratch(begin, chans), "outer", 20, 5.0, 0, far_out=(0,),
+    )
+    sent = lanes(got, yip, token, "y_inverse")
     got = exchange(sent, gyc)
-    mode_grad, _ = outer(modes, pmodes, 4, 4, grad, sent[0], 6.0)
-    field_grad = call(
-        finish_kernel, (idx, *got, zi, pg, dskip_t),
-        bf(cells, zlen), [tall, wide], "finish", 8, 2.0,
-    )
-    part = sum_over(part, (("col", 2), ("gy", 2), ("gx", 4)))
+    mode_grad, _ = call(
+        functools.partial(outer_kernel, begin), (modes, pmodes, sent[0], grad),
+        [grads, TOKEN], outer_scratch(end, chans), "outer", 20, 4.0, 0, free=2,
+        far_out=(0,), alias={3: 0},
+    )
+    field_grad, proj_grad, lift_grad, skip_grad = call(
+        finish_kernel, (*got, zip_, pg, dskip_t, part, other),
+        [bf(cells, zlen)]
+        + [jax.ShapeDtypeStruct((chans, n), F32) for n in (128, 128, 32)],
+        [tall, wide], "finish", 8, 3.0, 0,
+    )
     return (
         field_grad.reshape(field.shape),
         mode_grad.reshape(mode_weight.shape),
-        part[64:, :chans],
-        part[32:64].T,
-        part[:32],
+        skip_grad,
+        lift_grad.T,
+        proj_grad,
     )
 
 

time: 103 us -> 97 us (0.942)
  waiting for transfers between devices: 13.1 us -> 10.9 us
  Pallas kernels: 54.7 us -> 52.6 us
  local copies, waits for them, and re-layouts: 3.56 us -> 2.34 us
    pallas_call x2, Pallas kernels: 13.6 us -> 9.31 us  [pack(): pl.pallas_call(functools.partial(pack_kernel, first), out_shape=[jax.Shap...]
    ppermute x28, waiting for transfers between devices: 13.1 us -> 10.9 us  [the longest x24 9.67 us: exchange(): lax.ppermute(block, axes, [(a, a ^ step) for a in range(4)])]
    pallas_call x13, Pallas kernels: 41.1 us -> 43.2 us  [call(): pl.pallas_call(kernel, out_shape=outs, in_specs=[SM] * smem + [VM] * (len...]
    slice x2 -> x0, local copies, waits for them, and re-layouts: 1.22 us -> none  [the longest x1 0.61 us: fast(): part[:32]]
  transfers between devices with their start and end apart: 28 -> 28, of which waited for: 7 -> 11; matrix products, arithmetic and copies ran while one was open for 1% -> 0% of each run, Pallas kernels for 36% -> 34%
where the time goes in v2:
time: 97 us; the launch traced here: 96.8 us
  Pallas kernels  52.6 us (54%)
  starting transfers between devices  29.9 us (31%)
  waiting for transfers between devices  10.9 us (11%)
  local copies, waits for them, and re-layouts  2.34 us (2%)
  between operations  1 us (1%)
    pallas_call x13, Pallas kernels, call(): pl.pallas_call(kernel, out_shape=outs, in_specs=[SM] * smem + [VM] * (len...  43.2 us
    ppermute x24, starting transfers between devices, exchange(): lax.ppermute(block, axes, [(a, a ^ step) for a in range(4)])  25.7 us
    ppermute x24, waiting for transfers between devices, exchange(): lax.ppermute(block, axes, [(a, a ^ step) for a in range(4)])  9.67 us
    pallas_call x2, Pallas kernels, pack(): pl.pallas_call(functools.partial(pack_kernel, first), out_shape=[jax.Shap...  9.31 us
    ppermute x4, starting transfers between devices, swap(): return lax.ppermute(part, axis, [(a, a ^ step) for a in range(size)])  4.16 us
    unnamed x30, local copies, waits for them, and re-layouts  2.34 us
  transfers between devices with their start and end apart: 28, of which 11 were waited for; matrix products, arithmetic and copies ran while one was open for 0% of the time, Pallas kernels for 34%

profile of v2, /device:TPU:0, one launch (start us, length us, event | category | flops | bytes accessed | tf_op | source)
XLA Modules:
  0.0 96.8 jit_solution(2019686325678002861)
XLA Ops:
  0.7 1.2 %copy-done = bf16[4,1024,128]{2,1,0:T(8,128)(2,1)S(1)} copy-done((bf16[4,1024,128]{2,1,0:T(8,128)(2,1)S(1)}, bf16[4,1024,128]{2,1,0:T(8,128)(2,1)}, u32[]{:S(2)}) %copy-start) | copy-done | bytes 1048600
  3.0 1.4 %z_forward.1 = (bf16[256,128]{1,0:T(8,128)(2,1)S(1)}, bf16[256,128]{1,0:T(8,128)(2,1)S(1)}, bf16[256,128]{1,0:T(8,128)(2,1)S(1)}, bf16[256,128]{1,0:T(8,128)(2,1)S(1)}) custom-call(s32[2]{0:T(128)S(1)} %pad_add_fusion.idx, bf16[2048,128]{1,0:T(8,128)(2,1)S(1)} %bitcast.9, bf16[4,1024,128]{2,1,0:T(8,128)(2,1)S(1)} %copy-done), custom_call_target="tpu_custom_call" | custom-call | bytes 6000000 | tf_op jit(solution)/shard_map/z_forward/pallas_call | solution.py:607
  4.4 3.0 %collective-permute-start = (bf16[256,128]{1,0:T(8,128)(2,1)S(1)}, bf16[256,128]{1,0:T(8,128)(2,1)S(1)}, u32[]{:S(2)}, u32[]{:S(2)}) collective-permute-start(bf16[256,128]{1,0:T(8,128)(2,1)S(1)} %get-tuple-element.66), channel_id=1, source_target_pairs={{0,2},{1,3},{2,0},{3,1},{4,6},{5,7},{6,4},{7,5},{8,10},{9,11},{10,... | collective-permute-start | bytes 196616 | tf_op jit(solution)/shard_map/ppermute | solution.py:642
  7.6 3.8 %pack.2 = (bf16[2,2,32,64,128]{4,3,2,1,0:T(8,128)(2,1)S(1)}, f32[8,128]{1,0:T(8,128)S(1)}) custom-call(bf16[2,32,32,64,32]{4,3,2,1,0:T(8,128)(2,1)} %bitcast.13, bf16[256,128]{1,0:T(8,128)(2,1)S(1)} %get-tuple-element.65.after.r0), custom_call_target="tpu_custom_call" | custom-call | bytes 9000000 | tf_op jit(solution)/shard_map/pack/pallas_call | solution.py:625
  12.4 3.0 %collective-permute-start.3 = (bf16[256,128]{1,0:T(8,128)(2,1)S(1)}, bf16[256,128]{1,0:T(8,128)(2,1)S(1)}, u32[]{:S(2)}, u32[]{:S(2)}) collective-permute-start(bf16[256,128]{1,0:T(8,128)(2,1)S(1)} %get-tuple-element.71), channel_id=1, source_target_pairs={{0,8},{4,12},{8,0},{12,4},{1,9},{5,13},{9,1},{13,5},{2,10},{6,14},... | collective-permute-start | bytes 196616 | tf_op jit(solution)/shard_map/ppermute | solution.py:642
  15.4 1.3 %collective-permute-start.4 = (bf16[256,128]{1,0:T(8,128)(2,1)S(1)}, bf16[256,128]{1,0:T(8,128)(2,1)S(1)}, u32[]{:S(2)}, u32[]{:S(2)}) collective-permute-start(bf16[256,128]{1,0:T(8,128)(2,1)S(1)} %get-tuple-element.72), channel_id=1, source_target_pairs={{0,12},{4,8},{8,4},{12,0},{1,13},{5,9},{9,5},{13,1},{2,14},{6,10},... | collective-permute-start | bytes 196616 | tf_op jit(solution)/shard_map/ppermute | solution.py:642
  17.0 5.5 %pack.3 = (bf16[3,2,32,64,128]{4,3,2,1,0:T(8,128)(2,1)S(1)}, f32[8,128]{1,0:T(8,128)}) custom-call(bf16[2,32,32,64,32]{4,3,2,1,0:T(8,128)(2,1)} %bitcast.14, bf16[256,128]{1,0:T(8,128)(2,1)S(1)} %get-tuple-element.70.after.r0), custom_call_target="tpu_custom_call" | custom-call | bytes 15000000 | tf_op jit(solution)/shard_map/pack/pallas_call | solution.py:625
  22.6 8.4 %mix_forward.1 = (bf16[8,2,64,128]{3,2,1,0:T(8,128)(2,1)S(1)}, bf16[256,128]{1,0:T(8,128)(2,1)S(1)}, bf16[256,128]{1,0:T(8,128)(2,1)S(1)}, bf16[256,128]{1,0:T(8...) custom-call(s32[2]{0:T(128)S(1)} %pad_add_fusion.idx, ...), custom_call_target="tpu_custom_call" | custom-call | bytes 24000000 | tf_op jit(solution)/shard_map/mix_forward/pallas_call | solution.py:607
  31.0 2.9 %collective-permute-start.6 = (bf16[256,128]{1,0:T(8,128)(2,1)S(1)}, bf16[256,128]{1,0:T(8,128)(2,1)S(1)}, u32[]{:S(2)}, u32[]{:S(2)}) collective-permute-start(bf16[256,128]{1,0:T(8,128)(2,1)S(1)} %get-tuple-element.77), channel_id=1, source_target_pairs={{0,8},{4,12},{8,0},{12,4},{1,9},{5,13},{9,1},{13,5},{2,10},{6,14},... | collective-permute-start | bytes 196616 | tf_op jit(solution)/shard_map/ppermute | solution.py:642
  33.9 1.3 %collective-permute-start.7 = (bf16[256,128]{1,0:T(8,128)(2,1)S(1)}, bf16[256,128]{1,0:T(8,128)(2,1)S(1)}, u32[]{:S(2)}, u32[]{:S(2)}) collective-permute-start(bf16[256,128]{1,0:T(8,128)(2,1)S(1)} %get-tuple-element.78), channel_id=1, source_target_pairs={{0,12},{4,8},{8,4},{12,0},{1,13},{5,9},{9,5},{13,1},{2,14},{6,10},... | collective-permute-start | bytes 196616 | tf_op jit(solution)/shard_map/ppermute | solution.py:642
  35.3 3.1 %cells.1 = (bf16[4,256,256]{2,1,0:T(8,128)(2,1)S(1)}, bf16[4,256,256]{2,1,0:T(8,128)(2,1)S(1)}, f32[4,256,256]{2,1,0:T(8,128)S(1)}, f32[4,1024,256]{2,1,0:T(8,12...) custom-call(s32[2]{0:T(128)S(1)} %pad_add_fusion.idx, ...), custom_call_target="tpu_custom_call" | custom-call | bytes 9000000 | tf_op jit(solution)/shard_map/cells/pallas_call | solution.py:607
  38.5 1.6 %collective-permute-done.7.r2 = bf16[256,128]{1,0:T(8,128)(2,1)S(1)} collective-permute-done((bf16[256,128]{1,0:T(8,128)(2,1)S(1)}, bf16[256,128]{1,0:T(8,128)(2,1)S(1)}, u32[]{:S(2)}, u32[]{:S(2)}) %collective-permute-start.7) | collective-permute-done | bytes 65568 | tf_op jit(solution)/shard_map/ppermute | solution.py:642
  41.1 1.6 %collective-permute-start.9 = (bf16[256,128]{1,0:T(8,128)(2,1)S(1)}, bf16[256,128]{1,0:T(8,128)(2,1)S(1)}, u32[]{:S(2)}, u32[]{:S(2)}) collective-permute-start(bf16[256,128]{1,0:T(8,128)(2,1)S(1)} %get-tuple-element.83), channel_id=1, source_target_pairs={{0,2},{1,3},{2,0},{3,1},{4,6},{5,7},{6,4},{7,5},{8,10},{9,11},{10,... | collective-permute-start | bytes 196616 | tf_op jit(solution)/shard_map/ppermute | solution.py:642
  43.3 2.1 %collective-permute-done.9.r1 = bf16[256,128]{1,0:T(8,128)(2,1)S(1)} collective-permute-done((bf16[256,128]{1,0:T(8,128)(2,1)S(1)}, bf16[256,128]{1,0:T(8,128)(2,1)S(1)}, u32[]{:S(2)}, u32[]{:S(2)}) %collective-permute-start.9) | collective-permute-done | bytes 65568 | tf_op jit(solution)/shard_map/ppermute | solution.py:642
  45.4 1.4 %collective-permute-done.10.r2 = bf16[256,128]{1,0:T(8,128)(2,1)S(1)} collective-permute-done((bf16[256,128]{1,0:T(8,128)(2,1)S(1)}, bf16[256,128]{1,0:T(8,128)(2,1)S(1)}, u32[]{:S(2)}, u32[]{:S(2)}) %collective-permute-start.10) | collective-permute-done | bytes 65568 | tf_op jit(solution)/shard_map/ppermute | solution.py:642
  46.8 4.8 %point.1 = (bf16[256,128]{1,0:T(8,128)(2,1)S(1)}, bf16[256,128]{1,0:T(8,128)(2,1)S(1)}, bf16[256,128]{1,0:T(8,128)(2,1)S(1)}, bf16[256,128]{1,0:T(8,128)(2,1)S(1...) custom-call(bf16[256,128]{1,0:T(8,128)(2,1)S(1)} %get-tuple-element., ...), custom_call_target="tpu_custom_call" | custom-call | bytes 18000000 | tf_op jit(solution)/shard_map/point/pallas_call | solution.py:607
  53.8 1.9 %sums.1.after = f32[96,128]{1,0:T(8,128)S(1)} custom-call(bf16[4,256,256]{2,1,0:T(8,128)(2,1)S(1)} %get-tuple-element.81.after.fx, bf16[4,256,256]{2,1,0:T(8,128)(2,1)S(1)} %get-tuple-element.88.cx, bf16[4,256,256]{2,1,0:T(8,128)(2,1)S(1)} %get-tuple-element.98.pg, bf16[4,1024,256]{2,1,0:T(8,128)(2,1)S(1)} %get-tuple-element.99.act, ...), custom_call_target="tpu_custom_call" | custom-call | bytes 7500000 | tf_op jit(solution)/shard_map/sums/pallas_call | solution.py:607
  57.7 1.4 %collective-permute-start.15 = (bf16[256,128]{1,0:T(8,128)(2,1)S(1)}, bf16[256,128]{1,0:T(8,128)(2,1)S(1)}, u32[]{:S(2)}, u32[]{:S(2)}) collective-permute-start(bf16[256,128]{1,0:T(8,128)(2,1)S(1)} %get-tuple-element.103), channel_id=1, source_target_pairs={{0,8},{4,12},{8,0},{12,4},{1,9},{5,13},{9,1},{13,5},{2,10},{6,14},... | collective-permute-start | bytes 196616 | tf_op jit(solution)/shard_map/ppermute | solution.py:642
  59.0 1.3 %collective-permute-start.16 = (bf16[256,128]{1,0:T(8,128)(2,1)S(1)}, bf16[256,128]{1,0:T(8,128)(2,1)S(1)}, u32[]{:S(2)}, u32[]{:S(2)}) collective-permute-start(bf16[256,128]{1,0:T(8,128)(2,1)S(1)} %get-tuple-element.104), channel_id=1, source_target_pairs={{0,12},{4,8},{8,4},{12,0},{1,13},{5,9},{9,5},{13,1},{2,14},{6,10},... | collective-permute-start | bytes 196616 | tf_op jit(solution)/shard_map/ppermute | solution.py:642
  61.2 1.2 %collective-permute-done.24 = f32[96,128]{1,0:T(8,128)S(1)} collective-permute-done((f32[96,128]{1,0:T(8,128)S(1)}, f32[96,128]{1,0:T(8,128)S(1)}, u32[]{:S(2)}, u32[]{:S(2)}) %collective-permute-start.24) | collective-permute-done | bytes 49184 | tf_op jit(solution)/shard_map/ppermute | solution.py:650
  62.5 1.3 %collective-permute-start.25 = (f32[96,128]{1,0:T(8,128)S(1)}, f32[96,128]{1,0:T(8,128)S(1)}, u32[]{:S(2)}, u32[]{:S(2)}) collective-permute-start(f32[96,128]{1,0:T(8,128)S(1)} %add.13), channel_id=1, source_target_pairs={{0,2},{2,0},{1,3},{3,1},{4,6},{6,4},{5,7},{7,5},{8,10},{10,8},{9,1... | collective-permute-start | bytes 147464 | tf_op jit(solution)/shard_map/ppermute | solution.py:650
  63.7 1.9 %collective-permute-done.15.r1 = bf16[256,128]{1,0:T(8,128)(2,1)S(1)} collective-permute-done((bf16[256,128]{1,0:T(8,128)(2,1)S(1)}, bf16[256,128]{1,0:T(8,128)(2,1)S(1)}, u32[]{:S(2)}, u32[]{:S(2)}) %collective-permute-start.15) | collective-permute-done | bytes 65568 | tf_op jit(solution)/shard_map/ppermute | solution.py:642
  65.6 1.2 %collective-permute-done.17.r3 = bf16[256,128]{1,0:T(8,128)(2,1)S(1)} collective-permute-done((bf16[256,128]{1,0:T(8,128)(2,1)S(1)}, bf16[256,128]{1,0:T(8,128)(2,1)S(1)}, u32[]{:S(2)}, u32[]{:S(2)}) %collective-permute-start.17) | collective-permute-done | bytes 65568 | tf_op jit(solution)/shard_map/ppermute | solution.py:642
  66.9 4.7 %mix_backward.1 = (bf16[32,2,64,128]{3,2,1,0:T(8,128)(2,1)S(1)}, bf16[256,128]{1,0:T(8,128)(2,1)S(1)}, bf16[256,128]{1,0:T(8,128)(2,1)S(1)}, bf16[256,128]{1,0:T(8,128)(2,1)S(1)}, bf16[256,128]{1,0:T(8,128)(2,1)S(1)}) custom-call(s32[2]{0:T(128)S(1)} %pad_add_fusion.idx, bf16[256,128]{1,0:T(8,128)(2,1)S(1)} %get-tuple-element.102.r0, ...), custom_call_target="tpu_custom_call" | custom-call | bytes 15000000 | tf_op jit(solution)/shard_map/mix_backward/pallas_call | solution.py:607
  71.6 1.6 %collective-permute-start.18 = (bf16[256,128]{1,0:T(8,128)(2,1)S(1)}, bf16[256,128]{1,0:T(8,128)(2,1)S(1)}, u32[]{:S(2)}, u32[]{:S(2)}) collective-permute-start(bf16[256,128]{1,0:T(8,128)(2,1)S(1)} %get-tuple-element.108), channel_id=1, source_target_pairs={{0,8},{4,12},{8,0},{12,4},{1,9},{5,13},{9,1},{13,5},{2,10},{6,14},... | collective-permute-start | bytes 196616 | tf_op jit(solution)/shard_map/ppermute | solution.py:642
  73.2 1.5 %collective-permute-start.19 = (bf16[256,128]{1,0:T(8,128)(2,1)S(1)}, bf16[256,128]{1,0:T(8,128)(2,1)S(1)}, u32[]{:S(2)}, u32[]{:S(2)}) collective-permute-start(bf16[256,128]{1,0:T(8,128)(2,1)S(1)} %get-tuple-element.109), channel_id=1, source_target_pairs={{0,12},{4,8},{8,4},{12,0},{1,13},{5,9},{9,5},{13,1},{2,14},{6,10},... | collective-permute-start | bytes 196616 | tf_op jit(solution)/shard_map/ppermute | solution.py:642
  75.2 1.6 %collective-permute-start.26 = (f32[96,128]{1,0:T(8,128)S(1)}, f32[96,128]{1,0:T(8,128)S(1)}, u32[]{:S(2)}, u32[]{:S(2)}) collective-permute-start(f32[96,128]{1,0:T(8,128)S(1)} %add.14), channel_id=1, source_target_pairs={{0,4},{4,0},{8,12},{12,8},{1,5},{5,1},{9,13},{13,9},{2,6},{6,2},{1... | collective-permute-start | bytes 147464 | tf_op jit(solution)/shard_map/ppermute | solution.py:650
  76.8 6.4 %outer.2 = (bf16[2,32,32,64,32]{4,3,2,1,0:T(8,128)(2,1)}, f32[8,128]{1,0:T(8,128)S(1)}) custom-call(bf16[8,2,64,128]{3,2,1,0:T(8,128)(2,1)S(1)} %get-tuple-element.111.modes, bf16[32,2,64,128]{3,2,1,0:T(8,128)(2,1)S(1)} %get-tuple-element.112.pmodes), custom_call_target="tpu_custom_call" | custom-call | bytes 15000000 | tf_op jit(solution)/shard_map/outer/pallas_call | solution.py:607
  85.1 1.1 %collective-permute-start.23 = (bf16[256,128]{1,0:T(8,128)(2,1)S(1)}, bf16[256,128]{1,0:T(8,128)(2,1)S(1)}, u32[]{:S(2)}, u32[]{:S(2)}) collective-permute-start(bf16[256,128]{1,0:T(8,128)(2,1)S(1)} %get-tuple-element.117), channel_id=1, source_target_pairs={{0,1},{1,0},{2,3},{3,2},{4,5},{5,4},{6,7},{7,6},{8,9},{9,8},{10,11... | collective-permute-start | bytes 196616 | tf_op jit(solution)/shard_map/ppermute | solution.py:642
  86.3 1.3 %collective-permute-start.27 = (f32[96,128]{1,0:T(8,128)S(1)}, f32[96,128]{1,0:T(8,128)S(1)}, u32[]{:S(2)}, u32[]{:S(2)}) collective-permute-start(f32[96,128]{1,0:T(8,128)S(1)} %add.15.part), channel_id=1, source_target_pairs={{0,8},{4,12},{8,0},{12,4},{1,9},{5,13},{9,1},{13,5},{2,10},{6,14},... | collective-permute-start | bytes 147464 | tf_op jit(solution)/shard_map/ppermute | solution.py:650
  87.5 6.9 %outer.3 = (bf16[2,32,32,64,32]{4,3,2,1,0:T(8,128)(2,1)}, f32[8,128]{1,0:T(8,128)}) custom-call(bf16[8,2,64,128]{3,2,1,0:T(8,128)(2,1)S(1)} %get-tuple-element.111.modes, bf16[32,2,64,128]{3,2,1,0:T(8,128)(2,1)S(1)} %get-tuple-element.112.pmodes, bf16[256,128]{1,0:T(8,128)(2,1)S(1)} %get-tuple-element.114.r0.rest_0_, ...), custom_call_target="tpu_custom_call", output_to_operand_aliasing={{0}: (3, {})} | custom-call | bytes 12000000 | tf_op jit(solution)/shard_map/outer/pallas_call | solution.py:607
  94.5 2.3 %finish.1 = (bf16[2048,128]{1,0:T(8,128)(2,1)}, f32[32,128]{1,0:T(8,128)}, f32[32,128]{1,0:T(8,128)}, f32[32,32]{1,0:T(8,128)}) custom-call(bf16[256,128]{1,0:T(8,128)(2,1)S(1)} %get-tuple-element.114.r0.rest_0_, bf16[256,128]{1,0:T(8,128)(2,1)S(1)} %collective-permute-done.21.r1, bf16[256,128]{1,0:T(8,128)(2,1)S(1)} %collective-permute-done.22.r2, ...), custom_call_target="tpu_custom_call" | custom-call | bytes 9000000 | tf_op jit(solution)/shard_map/finish/pallas_call | solution.py:607
  (73 shorter events, 11.7 us)
Async XLA Ops:
  4.4 7.0 %collective-permute-start = (bf16[256,128]{1,0:T(8,128)(2,1)S(1)}, bf16[256,128]{1,0:T(8,128)(2,1)S(1)}, u32[]{:S(2)}, u32[]{:S(2)}) collective-permute-start(bf16[256,128]{1,0:T(8,128)(2,1)S(1)} %get-tuple-element.66), channel_id=1, source_target_pairs={{0,2},{1,3},{2,0},{3,1},{4,6},{5,7},{6,4},{7,5},{8,10},{9,11},{10,... | collective-permute-start | bytes 196616 | tf_op jit(solution)/shard_map/ppermute | solution.py:642
  7.4 4.1 %collective-permute-start.1 = (bf16[256,128]{1,0:T(8,128)(2,1)S(1)}, bf16[256,128]{1,0:T(8,128)(2,1)S(1)}, u32[]{:S(2)}, u32[]{:S(2)}) collective-permute-start(bf16[256,128]{1,0:T(8,128)(2,1)S(1)} %get-tuple-element.67), channel_id=1, source_target_pairs={{0,3},{1,2},{2,1},{3,0},{4,7},{5,6},{6,5},{7,4},{8,11},{9,10},{10,... | collective-permute-start | bytes 196616 | tf_op jit(solution)/shard_map/ppermute | solution.py:642
  7.4 4.1 %collective-permute-start.2 = (bf16[256,128]{1,0:T(8,128)(2,1)S(1)}, bf16[256,128]{1,0:T(8,128)(2,1)S(1)}, u32[]{:S(2)}, u32[]{:S(2)}) collective-permute-start(bf16[256,128]{1,0:T(8,128)(2,1)S(1)} %get-tuple-element.68), channel_id=1, source_target_pairs={{0,1},{1,0},{2,3},{3,2},{4,5},{5,4},{6,7},{7,6},{8,9},{9,8},{10,11... | collective-permute-start | bytes 196616 | tf_op jit(solution)/shard_map/ppermute | solution.py:642
  12.4 10.1 %collective-permute-start.3 = (bf16[256,128]{1,0:T(8,128)(2,1)S(1)}, bf16[256,128]{1,0:T(8,128)(2,1)S(1)}, u32[]{:S(2)}, u32[]{:S(2)}) collective-permute-start(bf16[256,128]{1,0:T(8,128)(2,1)S(1)} %get-tuple-element.71), channel_id=1, source_target_pairs={{0,8},{4,12},{8,0},{12,4},{1,9},{5,13},{9,1},{13,5},{2,10},{6,14},... | collective-permute-start | bytes 196616 | tf_op jit(solution)/shard_map/ppermute | solution.py:642
  15.4 7.1 %collective-permute-start.4 = (bf16[256,128]{1,0:T(8,128)(2,1)S(1)}, bf16[256,128]{1,0:T(8,128)(2,1)S(1)}, u32[]{:S(2)}, u32[]{:S(2)}) collective-permute-start(bf16[256,128]{1,0:T(8,128)(2,1)S(1)} %get-tuple-element.72), channel_id=1, source_target_pairs={{0,12},{4,8},{8,4},{12,0},{1,13},{5,9},{9,5},{13,1},{2,14},{6,10},... | collective-permute-start | bytes 196616 | tf_op jit(solution)/shard_map/ppermute | solution.py:642
  16.7 5.8 %collective-permute-start.5 = (bf16[256,128]{1,0:T(8,128)(2,1)S(1)}, bf16[256,128]{1,0:T(8,128)(2,1)S(1)}, u32[]{:S(2)}, u32[]{:S(2)}) collective-permute-start(bf16[256,128]{1,0:T(8,128)(2,1)S(1)} %get-tuple-element.73), channel_id=1, source_target_pairs={{0,4},{4,0},{8,12},{12,8},{1,5},{5,1},{9,13},{13,9},{2,6},{6,2},{1... | collective-permute-start | bytes 196616 | tf_op jit(solution)/shard_map/ppermute | solution.py:642
  22.6 12.7 %copy-start.1 = (bf16[4,1024,128]{2,1,0:T(8,128)(2,1)S(1)}, bf16[4,1024,128]{2,1,0:T(8,128)(2,1)}, u32[]{:S(2)}) copy-start(bf16[4,1024,128]{2,1,0:T(8,128)(2,1)} %constant.29.clone.zf) | copy-start | bytes 3145732
  22.6 12.7 %copy-start.3 = (bf16[32,8,8,128]{3,2,1,0:T(8,128)(2,1)S(1)}, bf16[32,8,8,128]{3,2,1,0:T(8,128)(2,1)}, u32[]{:S(2)}) copy-start(bf16[32,8,8,128]{3,2,1,0:T(8,128)(2,1)} %param.14) | copy-start | bytes 1572868
  31.0 7.5 %collective-permute-start.6 = (bf16[256,128]{1,0:T(8,128)(2,1)S(1)}, bf16[256,128]{1,0:T(8,128)(2,1)S(1)}, u32[]{:S(2)}, u32[]{:S(2)}) collective-permute-start(bf16[256,128]{1,0:T(8,128)(2,1)S(1)} %get-tuple-element.77), channel_id=1, source_target_pairs={{0,8},{4,12},{8,0},{12,4},{1,9},{5,13},{9,1},{13,5},{2,10},{6,14},... | collective-permute-start | bytes 196616 | tf_op jit(solution)/shard_map/ppermute | solution.py:642
  33.9 6.2 %collective-permute-start.7 = (bf16[256,128]{1,0:T(8,128)(2,1)S(1)}, bf16[256,128]{1,0:T(8,128)(2,1)S(1)}, u32[]{:S(2)}, u32[]{:S(2)}) collective-permute-start(bf16[256,128]{1,0:T(8,128)(2,1)S(1)} %get-tuple-element.78), channel_id=1, source_target_pairs={{0,12},{4,8},{8,4},{12,0},{1,13},{5,9},{9,5},{13,1},{2,14},{6,10},... | collective-permute-start | bytes 196616 | tf_op jit(solution)/shard_map/ppermute | solution.py:642
  35.2 5.0 %collective-permute-start.8 = (bf16[256,128]{1,0:T(8,128)(2,1)S(1)}, bf16[256,128]{1,0:T(8,128)(2,1)S(1)}, u32[]{:S(2)}, u32[]{:S(2)}) collective-permute-start(bf16[256,128]{1,0:T(8,128)(2,1)S(1)} %get-tuple-element.79), channel_id=1, source_target_pairs={{0,4},{4,0},{8,12},{12,8},{1,5},{5,1},{9,13},{13,9},{2,6},{6,2},{1... | collective-permute-start | bytes 196616 | tf_op jit(solution)/shard_map/ppermute | solution.py:642
  41.1 4.3 %collective-permute-start.9 = (bf16[256,128]{1,0:T(8,128)(2,1)S(1)}, bf16[256,128]{1,0:T(8,128)(2,1)S(1)}, u32[]{:S(2)}, u32[]{:S(2)}) collective-permute-start(bf16[256,128]{1,0:T(8,128)(2,1)S(1)} %get-tuple-element.83), channel_id=1, source_target_pairs={{0,2},{1,3},{2,0},{3,1},{4,6},{5,7},{6,4},{7,5},{8,10},{9,11},{10,... | collective-permute-start | bytes 196616 | tf_op jit(solution)/shard_map/ppermute | solution.py:642
  42.6 4.2 %collective-permute-start.10 = (bf16[256,128]{1,0:T(8,128)(2,1)S(1)}, bf16[256,128]{1,0:T(8,128)(2,1)S(1)}, u32[]{:S(2)}, u32[]{:S(2)}) collective-permute-start(bf16[256,128]{1,0:T(8,128)(2,1)S(1)} %get-tuple-element.84), channel_id=1, source_target_pairs={{0,3},{1,2},{2,1},{3,0},{4,7},{5,6},{6,5},{7,4},{8,11},{9,10},{10,... | collective-permute-start | bytes 196616 | tf_op jit(solution)/shard_map/ppermute | solution.py:642
  42.6 4.2 %collective-permute-start.11 = (bf16[256,128]{1,0:T(8,128)(2,1)S(1)}, bf16[256,128]{1,0:T(8,128)(2,1)S(1)}, u32[]{:S(2)}, u32[]{:S(2)}) collective-permute-start(bf16[256,128]{1,0:T(8,128)(2,1)S(1)} %get-tuple-element.85), channel_id=1, source_target_pairs={{0,1},{1,0},{2,3},{3,2},{4,5},{5,4},{6,7},{7,6},{8,9},{9,8},{10,11... | collective-permute-start | bytes 196616 | tf_op jit(solution)/shard_map/ppermute | solution.py:642
  51.6 4.8 %collective-permute-start.12 = (bf16[256,128]{1,0:T(8,128)(2,1)S(1)}, bf16[256,128]{1,0:T(8,128)(2,1)S(1)}, u32[]{:S(2)}, u32[]{:S(2)}) collective-permute-start(bf16[256,128]{1,0:T(8,128)(2,1)S(1)} %get-tuple-element.94), channel_id=1, source_target_pairs={{0,2},{1,3},{2,0},{3,1},{4,6},{5,7},{6,4},{7,5},{8,10},{9,11},{10,... | collective-permute-start | bytes 196616 | tf_op jit(solution)/shard_map/ppermute | solution.py:642
  52.4 4.4 %collective-permute-start.13 = (bf16[256,128]{1,0:T(8,128)(2,1)S(1)}, bf16[256,128]{1,0:T(8,128)(2,1)S(1)}, u32[]{:S(2)}, u32[]{:S(2)}) collective-permute-start(bf16[256,128]{1,0:T(8,128)(2,1)S(1)} %get-tuple-element.95), channel_id=1, source_target_pairs={{0,3},{1,2},{2,1},{3,0},{4,7},{5,6},{6,5},{7,4},{8,11},{9,10},{10,... | collective-permute-start | bytes 196616 | tf_op jit(solution)/shard_map/ppermute | solution.py:642
  52.9 3.9 %collective-permute-start.14 = (bf16[256,128]{1,0:T(8,128)(2,1)S(1)}, bf16[256,128]{1,0:T(8,128)(2,1)S(1)}, u32[]{:S(2)}, u32[]{:S(2)}) collective-permute-start(bf16[256,128]{1,0:T(8,128)(2,1)S(1)} %get-tuple-element.96), channel_id=1, source_target_pairs={{0,1},{1,0},{2,3},{3,2},{4,5},{5,4},{6,7},{7,6},{8,9},{9,8},{10,11... | collective-permute-start | bytes 196616 | tf_op jit(solution)/shard_map/ppermute | solution.py:642
  53.8 13.1 %copy-start.7 = (bf16[4,2,32,1024]{3,2,1,0:T(8,128)(2,1)S(1)}, bf16[4,2,32,1024]{3,2,1,0:T(8,128)(2,1)}, u32[]{:S(2)}) copy-start(bf16[4,2,32,1024]{3,2,1,0:T(8,128)(2,1)} %constant.34.clone.xr) | copy-start | bytes 1572868
  53.8 13.1 %copy-start.10 = (bf16[4,32,256]{2,1,0:T(8,128)(2,1)S(1)}, bf16[4,32,256]{2,1,0:T(8,128)(2,1)}, u32[]{:S(2)}) copy-start(bf16[4,32,256]{2,1,0:T(8,128)(2,1)} %constant.36.clone.xd) | copy-start | bytes 196612
  57.7 8.0 %collective-permute-start.15 = (bf16[256,128]{1,0:T(8,128)(2,1)S(1)}, bf16[256,128]{1,0:T(8,128)(2,1)S(1)}, u32[]{:S(2)}, u32[]{:S(2)}) collective-permute-start(bf16[256,128]{1,0:T(8,128)(2,1)S(1)} %get-tuple-element.103), channel_id=1, source_target_pairs={{0,8},{4,12},{8,0},{12,4},{1,9},{5,13},{9,1},{13,5},{2,10},{6,14},... | collective-permute-start | bytes 196616 | tf_op jit(solution)/shard_map/ppermute | solution.py:642
  59.0 6.6 %collective-permute-start.16 = (bf16[256,128]{1,0:T(8,128)(2,1)S(1)}, bf16[256,128]{1,0:T(8,128)(2,1)S(1)}, u32[]{:S(2)}, u32[]{:S(2)}) collective-permute-start(bf16[256,128]{1,0:T(8,128)(2,1)S(1)} %get-tuple-element.104), channel_id=1, source_target_pairs={{0,12},{4,8},{8,4},{12,0},{1,13},{5,9},{9,5},{13,1},{2,14},{6,10},... | collective-permute-start | bytes 196616 | tf_op jit(solution)/shard_map/ppermute | solution.py:642
  60.4 6.5 %collective-permute-start.17 = (bf16[256,128]{1,0:T(8,128)(2,1)S(1)}, bf16[256,128]{1,0:T(8,128)(2,1)S(1)}, u32[]{:S(2)}, u32[]{:S(2)}) collective-permute-start(bf16[256,128]{1,0:T(8,128)(2,1)S(1)} %get-tuple-element.105), channel_id=1, source_target_pairs={{0,4},{4,0},{8,12},{12,8},{1,5},{5,1},{9,13},{13,9},{2,6},{6,2},{1... | collective-permute-start | bytes 196616 | tf_op jit(solution)/shard_map/ppermute | solution.py:642
  61.2 1.2 %collective-permute-start.24 = (f32[96,128]{1,0:T(8,128)S(1)}, f32[96,128]{1,0:T(8,128)S(1)}, u32[]{:S(2)}, u32[]{:S(2)}) collective-permute-start(f32[96,128]{1,0:T(8,128)S(1)} %sums.1.after), channel_id=1, source_target_pairs={{0,1},{1,0},{2,3},{3,2},{4,5},{5,4},{6,7},{7,6},{8,9},{9,8},{10,11... | collective-permute-start | bytes 147464 | tf_op jit(solution)/shard_map/ppermute | solution.py:650
  62.5 12.7 %collective-permute-start.25 = (f32[96,128]{1,0:T(8,128)S(1)}, f32[96,128]{1,0:T(8,128)S(1)}, u32[]{:S(2)}, u32[]{:S(2)}) collective-permute-start(f32[96,128]{1,0:T(8,128)S(1)} %add.13), channel_id=1, source_target_pairs={{0,2},{2,0},{1,3},{3,1},{4,6},{6,4},{5,7},{7,5},{8,10},{10,8},{9,1... | collective-permute-start | bytes 147464 | tf_op jit(solution)/shard_map/ppermute | solution.py:650
  71.6 11.6 %collective-permute-start.18 = (bf16[256,128]{1,0:T(8,128)(2,1)S(1)}, bf16[256,128]{1,0:T(8,128)(2,1)S(1)}, u32[]{:S(2)}, u32[]{:S(2)}) collective-permute-start(bf16[256,128]{1,0:T(8,128)(2,1)S(1)} %get-tuple-element.108), channel_id=1, source_target_pairs={{0,8},{4,12},{8,0},{12,4},{1,9},{5,13},{9,1},{13,5},{2,10},{6,14},... | collective-permute-start | bytes 196616 | tf_op jit(solution)/shard_map/ppermute | solution.py:642
  73.2 10.0 %collective-permute-start.19 = (bf16[256,128]{1,0:T(8,128)(2,1)S(1)}, bf16[256,128]{1,0:T(8,128)(2,1)S(1)}, u32[]{:S(2)}, u32[]{:S(2)}) collective-permute-start(bf16[256,128]{1,0:T(8,128)(2,1)S(1)} %get-tuple-element.109), channel_id=1, source_target_pairs={{0,12},{4,8},{8,4},{12,0},{1,13},{5,9},{9,5},{13,1},{2,14},{6,10},... | collective-permute-start | bytes 196616 | tf_op jit(solution)/shard_map/ppermute | solution.py:642
  74.7 8.5 %collective-permute-start.20 = (bf16[256,128]{1,0:T(8,128)(2,1)S(1)}, bf16[256,128]{1,0:T(8,128)(2,1)S(1)}, u32[]{:S(2)}, u32[]{:S(2)}) collective-permute-start(bf16[256,128]{1,0:T(8,128)(2,1)S(1)} %get-tuple-element.110), channel_id=1, source_target_pairs={{0,4},{4,0},{8,12},{12,8},{1,5},{5,1},{9,13},{13,9},{2,6},{6,2},{1... | collective-permute-start | bytes 196616 | tf_op jit(solution)/shard_map/ppermute | solution.py:642
  75.2 11.1 %collective-permute-start.26 = (f32[96,128]{1,0:T(8,128)S(1)}, f32[96,128]{1,0:T(8,128)S(1)}, u32[]{:S(2)}, u32[]{:S(2)}) collective-permute-start(f32[96,128]{1,0:T(8,128)S(1)} %add.14), channel_id=1, source_target_pairs={{0,4},{4,0},{8,12},{12,8},{1,5},{5,1},{9,13},{13,9},{2,6},{6,2},{1... | collective-permute-start | bytes 147464 | tf_op jit(solution)/shard_map/ppermute | solution.py:650
  84.1 10.4 %collective-permute-start.21 = (bf16[256,128]{1,0:T(8,128)(2,1)S(1)}, bf16[256,128]{1,0:T(8,128)(2,1)S(1)}, u32[]{:S(2)}, u32[]{:S(2)}) collective-permute-start(bf16[256,128]{1,0:T(8,128)(2,1)S(1)} %get-tuple-element.115), channel_id=1, source_target_pairs={{0,2},{1,3},{2,0},{3,1},{4,6},{5,7},{6,4},{7,5},{8,10},{9,11},{10,... | collective-permute-start | bytes 196616 | tf_op jit(solution)/shard_map/ppermute | solution.py:642
  85.1 9.4 %collective-permute-start.22 = (bf16[256,128]{1,0:T(8,128)(2,1)S(1)}, bf16[256,128]{1,0:T(8,128)(2,1)S(1)}, u32[]{:S(2)}, u32[]{:S(2)}) collective-permute-start(bf16[256,128]{1,0:T(8,128)(2,1)S(1)} %get-tuple-element.116), channel_id=1, source_target_pairs={{0,3},{1,2},{2,1},{3,0},{4,7},{5,6},{6,5},{7,4},{8,11},{9,10},{10,... | collective-permute-start | bytes 196616 | tf_op jit(solution)/shard_map/ppermute | solution.py:642
  85.1 9.4 %collective-permute-start.23 = (bf16[256,128]{1,0:T(8,128)(2,1)S(1)}, bf16[256,128]{1,0:T(8,128)(2,1)S(1)}, u32[]{:S(2)}, u32[]{:S(2)}) collective-permute-start(bf16[256,128]{1,0:T(8,128)(2,1)S(1)} %get-tuple-element.117), channel_id=1, source_target_pairs={{0,1},{1,0},{2,3},{3,2},{4,5},{5,4},{6,7},{7,6},{8,9},{9,8},{10,11... | collective-permute-start | bytes 196616 | tf_op jit(solution)/shard_map/ppermute | solution.py:642
  86.3 8.2 %collective-permute-start.27 = (f32[96,128]{1,0:T(8,128)S(1)}, f32[96,128]{1,0:T(8,128)S(1)}, u32[]{:S(2)}, u32[]{:S(2)}) collective-permute-start(f32[96,128]{1,0:T(8,128)S(1)} %add.15.part), channel_id=1, source_target_pairs={{0,8},{4,12},{8,0},{12,4},{1,9},{5,13},{9,1},{13,5},{2,10},{6,14},... | collective-permute-start | bytes 147464 | tf_op jit(solution)/shard_map/ppermute | solution.py:650
  (11 other events, 93.4 us)

commit v3 on v2

--- a/solution.py
+++ b/solution.py
@@ -202,6 +202,10 @@
     ]
 
 
+def place():
+    return lax.axis_index("gy") * lax.axis_size("col") + lax.axis_index("col"), lax.axis_index("gx")
+
+
 def dot(a, b):
     return lax.dot_general(a, b, (((1,), (0,)), ((), ())), preferred_element_type=jnp.float32)
 
@@ -215,26 +219,33 @@
 STEPS = (0, 2, 3, 1)
 
 
-def z_forward_kernel(rows, yrows, zlen, idx, field, zf, o0, o1, o2, o3, held, tab, wide, sem):
-    first = pltpu.make_async_copy(field, held, sem.at[0])
-    first.start()
-    second = pltpu.make_async_copy(zf, tab, sem.at[1])
-    second.start()
-    first.wait()
-    wide[...] = held[...].astype(F32)
+def z_table(own):
+    z, lane = (lax.broadcasted_iota(jnp.int32, (128, 64), axis) for axis in (0, 1))
+    block = jnp.zeros_like(lane)
+    for s, step in enumerate(STEPS):
+        block = jnp.where(lane // 16 == s, own ^ step, block)
+    turns = ((8 * block + lane % 8) * z + 32 * (lane // 8 % 2)) % 128
+    values = jnp.cos(turns.astype(F32) * (2.0 * math.pi / 128)) * (1.0 / math.sqrt(128))
+    row, at = (lax.broadcasted_iota(jnp.int32, (64, 512), axis) for axis in (0, 1))
+    copies = jnp.where((row // 16 == at // 128) & (row % 16 == at % 16), 1.0, 0.0)
+    every = dot(values.astype(BF), copies.astype(BF))
+    cell = lax.broadcasted_iota(jnp.int32, (128, 512), 1) // 16 % 8
+    return jnp.concatenate([jnp.where(cell == y, every, 0.0).astype(BF) for y in range(8)], axis=0)
+
+
+def z_forward_kernel(rows, yrows, field, o0, o1, o2, o3, wide):
+    wide[...] = field[...].astype(F32)
     side = jnp.concatenate(
         [wide[pl.ds(y, rows, stride=yrows), :].astype(BF) for y in range(yrows)], axis=1
     )
-    second.wait()
-    table = jnp.concatenate([tab[idx[0] ^ STEPS[s]] for s in range(4)], axis=1)
-    out = dot(side, table).astype(BF)
+    out = dot(side, z_table(place()[0])).astype(BF)
     for s, o in enumerate((o0, o1, o2, o3)):
         o[...] = out[:, s * 128 : (s + 1) * 128]
 
 
-def lane_kernel(idx, r0, r1, r2, r3, table, after, o0, o1, o2, o3):
+def lane_kernel(r0, r1, r2, r3, table, after, o0, o1, o2, o3):
     side = jnp.concatenate([r0[...], r1[...], r2[...], r3[...]], axis=1)
-    known = table[...] if len(table.shape) == 2 else lane_table(idx, 0, 1, table)
+    known = table[...] if len(table.shape) == 2 else lane_table(place(), 0, 1, table)
     out = dot(side, known).astype(BF)
     for t, o in enumerate((o0, o1, o2, o3)):
         o[...] = out[:, t * 128 : (t + 1) * 128]
@@ -262,9 +273,10 @@
 
 
 def mix_forward_kernel(
-    idx, r0, r1, r2, r3, xf, xi, early, late, weight, modes, o0, o1, o2, o3, last,
+    r0, r1, r2, r3, xf, xi, early, late, weight, modes, o0, o1, o2, o3, last,
     total, held, sem,
 ):
+    idx = place()
     known = early.shape[0] + late.shape[0]
     copies = pack_copies(known, weight, held, sem)
     side, table = x_side(idx, (r0, r1, r2, r3), xf)
@@ -282,7 +294,7 @@
         total[o, 0], total[o, 1] = add_products(got, late, modes, o, early.shape[0])
         return carry
 
-    lax.fori_loop(0, 32, begin, 0, unroll=2)
+    lax.fori_loop(0, 32, begin, 0, unroll=16)
     pack_finish(copies, held, last)
 
     def pair(k, carry):
@@ -300,12 +312,13 @@
             outs[s][pl.ds(pl.multiple_of(k * 16, 16), 16), :] = both.astype(BF)
         return carry
 
-    lax.fori_loop(0, 16, pair, 0, unroll=2)
+    lax.fori_loop(0, 16, pair, 0, unroll=8)
 
 
 def mix_backward_kernel(
-    idx, r0, r1, r2, r3, xr, xd, early, late, last, pmodes, o0, o1, o2, o3
+    r0, r1, r2, r3, xr, xd, early, late, last, pmodes, o0, o1, o2, o3
 ):
+    idx = place()
     side, table = x_side(idx, (r0, r1, r2, r3), xr)
     for d in range(4):
         got = dot(side, table[:, d * 256 : (d + 1) * 256]).astype(BF)
@@ -457,9 +470,10 @@
 
 
 def cells_kernel(
-    idx, field, cotangent, skip, lift_t, proj, zf, zi, yf, yi,
+    field, cotangent, skip, lift_t, proj, zf, zi, yf, yi,
     fx, cx, skipped, backed, dskip_t, dlift, dlift_t, zfp, zip_, yfp, yip, wide,
 ):
+    idx = place()
     for src, dst in ((field, fx), (cotangent, cx)):
         wide[...] = src[...].astype(F32)
 
@@ -565,8 +579,10 @@
 
 
 def finish_kernel(
-    r0, r1, r2, r3, back, pg, dskip_t, part, other, out, proj, lift, skip, spectral, wide
+    start, r0, r1, r2, r3, back, pg, dskip_t, part, other, modes, pmodes, so_far,
+    out, proj, lift, skip, grad, spectral, wide, held, turned, sem,
 ):
+    copies = outer_start(start, modes, pmodes, grad, held, turned, sem)
     sums = part[...] + other[...]
     proj[...] = sums[:32]
     lift[...] = sums[32:64]
@@ -585,14 +601,15 @@
 
     lax.fori_loop(0, 4, step, 0, unroll=2)
     out[...] = wide[...].astype(BF)
+    for copy in copies:
+        copy.wait()
 
 
 PACK = (2, 3, 3)
-OUTER = (4, 4)
+OUTER = (3, 2, 3)
 VM = pl.BlockSpec(memory_space=pltpu.VMEM)
 ANY = pl.BlockSpec(memory_space=pl.ANY)
 HBM = pl.BlockSpec(memory_space=pltpu.HBM)
-SM = pl.BlockSpec(memory_space=pltpu.SMEM)
 BLOCK = jax.ShapeDtypeStruct((256, 128), BF)
 MIB = 1024 * 1024
 
@@ -602,12 +619,12 @@
 
 
 def call(
-    kernel, ins, outs, scratch=(), name=None, mib=8, us=1.0, smem=1, free=0, far_out=(), alias={}
+    kernel, ins, outs, scratch=(), name=None, mib=8, us=1.0, free=0, far_out=(), alias={}
 ):
     return pl.pallas_call(
         kernel,
         out_shape=outs,
-        in_specs=[SM] * smem + [VM] * (len(ins) - smem - free) + [ANY] * free,
+        in_specs=[VM] * (len(ins) - free) + [ANY] * free,
         out_specs=[ANY if at in far_out else VM for at in range(len(outs))],
         scratch_shapes=list(scratch),
         input_output_aliases=alias,
@@ -655,7 +672,6 @@
     tables = make_tables(zlen, yrows * 4, xrows * 4, 4, xrows, yrows)
     zf, zi, yf, yi, xf, xr, xi, xd = [jnp.asarray(t) for t in tables]
     gyc = ("gy", "col")
-    idx = jnp.stack([lax.axis_index(gyc), lax.axis_index("gx")]).astype(jnp.int32)
     four = [BLOCK] * 4
     cells = chans * xrows * yrows
     flat_field = field.reshape(cells, zlen)
@@ -670,18 +686,11 @@
         return jax.ShapeDtypeStruct(shape, BF)
 
     def lanes(got, table, after, name):
-        return call(lane_kernel, (idx, *got, table, after), four, (), name, 4, 1.0, free=1)
+        return call(lane_kernel, (*got, table, after), four, (), name, 4, 1.0, free=1)
 
     sent = call(
-        functools.partial(z_forward_kernel, rows, yrows, zlen),
-        (idx, flat_field, zf), four,
-        [
-            pltpu.VMEM((cells, zlen), BF),
-            pltpu.VMEM(zf.shape, BF),
-            wide,
-            pltpu.SemaphoreType.DMA((2,)),
-        ],
-        "z_forward", 8, 2.0, free=2,
+        functools.partial(z_forward_kernel, rows, yrows), (flat_field,), four, [wide],
+        "z_forward", 8, 2.0,
     )
     got = exchange(sent, gyc)
     one, two, three = PACK
@@ -690,7 +699,7 @@
     got = exchange(sent, "gx")
     late, _ = pack(weight, one, two, sent[0], 5.0)
     modes, *sent, last = call(
-        mix_forward_kernel, (idx, *got, xf, xi, early, late, weight),
+        mix_forward_kernel, (*got, xf, xi, early, late, weight),
         [bf(8, 2, 64, 128)] + four + [bf(three, 2, chans, 64, 128)],
         [
             pltpu.VMEM((chans, 2, 64, 128), F32),
@@ -702,7 +711,7 @@
     got = exchange(sent, "gx")
     fx, cx, skipped, backed, dskip_t, dlift, dlift_t, zfp, zip_, yfp, yip = call(
         cells_kernel,
-        (idx, flat_field, flat_cot, skip_weight, lift_t, proj_weight, zf, zi, yf, yi),
+        (flat_field, flat_cot, skip_weight, lift_t, proj_weight, zf, zi, yf, yi),
         [bf(4, 256, 256)] * 2
         + [jax.ShapeDtypeStruct((4, 256, 256), F32), jax.ShapeDtypeStruct((4, 1024, 256), F32)]
         + [bf(256, 256), bf(1024, 256), bf(64, 256)]
@@ -715,12 +724,12 @@
         point_kernel,
         (*got, zip_, zfp, cx, skipped, backed, dlift, dlift_t),
         four + [bf(4, 256, 256), bf(4, 1024, 256), bf(4, 1024, 256), bf(4, 256, 256)],
-        [tall, tall], "point", 8, 6.0, 0,
+        [tall, tall], "point", 8, 6.0,
     )
     got = exchange(sent, gyc)
     (part,) = call(
         sums_kernel, (fx, cx, pg, act, hid, lif),
-        [jax.ShapeDtypeStruct((96, 128), F32)], (), "sums", 4, 2.5, 0,
+        [jax.ShapeDtypeStruct((96, 128), F32)], (), "sums", 4, 2.5,
     )
     sent = lanes(got, yfp, part, "y_forward")
     got = exchange(sent, "gx")
@@ -728,28 +737,31 @@
         part = part + swap(part, axis, 1)
     other = swap(part, "gx", 2)
     grads = bf(2, chans, chans, 64, 32)
-    begin, end = OUTER
+    begin, middle, end = OUTER
     pmodes, *sent = call(
-        mix_backward_kernel, (idx, *got, xr, xd, early, late, last),
+        mix_backward_kernel, (*got, xr, xd, early, late, last),
         [bf(32, 2, 64, 128)] + four, (), "mix_backward", 12, 5.0,
     )
     got = exchange(sent, "gx")
     grad, token = call(
         functools.partial(outer_kernel, 0), (modes, pmodes), [grads, TOKEN],
-        outer_scratch(begin, chans), "outer", 20, 5.0, 0, far_out=(0,),
+        outer_scratch(begin, chans), "outer", 20, 5.0, far_out=(0,),
     )
     sent = lanes(got, yip, token, "y_inverse")
     got = exchange(sent, gyc)
-    mode_grad, _ = call(
+    grad, _ = call(
         functools.partial(outer_kernel, begin), (modes, pmodes, sent[0], grad),
-        [grads, TOKEN], outer_scratch(end, chans), "outer", 20, 4.0, 0, free=2,
+        [grads, TOKEN], outer_scratch(middle, chans), "outer", 20, 4.0, free=2,
         far_out=(0,), alias={3: 0},
     )
-    field_grad, proj_grad, lift_grad, skip_grad = call(
-        finish_kernel, (*got, zip_, pg, dskip_t, part, other),
+    field_grad, proj_grad, lift_grad, skip_grad, mode_grad = call(
+        functools.partial(finish_kernel, begin + middle),
+        (*got, zip_, pg, dskip_t, part, other, modes, pmodes, grad),
         [bf(cells, zlen)]
-        + [jax.ShapeDtypeStruct((chans, n), F32) for n in (128, 128, 32)],
-        [tall, wide], "finish", 8, 3.0, 0,
+        + [jax.ShapeDtypeStruct((chans, n), F32) for n in (128, 128, 32)]
+        + [grads],
+        [tall, wide] + outer_scratch(end, chans), "finish", 24, 4.0, free=1,
+        far_out=(4,), alias={11: 4},
     )
     return (
         field_grad.reshape(field.shape),

time: 97 us -> 91.1 us (0.939)
  Pallas kernels: 52.6 us -> 47.2 us
  local copies, waits for them, and re-layouts: 2.34 us -> 1.11 us
    pallas_call x13, Pallas kernels: 43.2 us -> 37.9 us  [call(): pl.pallas_call(kernel, out_shape=outs, in_specs=[VM] * (len(ins) - free)...]
    unnamed x30 -> x28, local copies, waits for them, and re-layouts: 2.34 us -> 1.11 us
  transfers between devices with their start and end apart: 28 -> 28, of which waited for: 11 -> 12; matrix products, arithmetic and copies ran while one was open for 0% -> 0% of each run, Pallas kernels for 34% -> 31%
where the time goes in v3:
time: 91.1 us; the launch traced here: 90.9 us
  Pallas kernels  47.2 us (52%)
  starting transfers between devices  30.1 us (33%)
  waiting for transfers between devices  11.3 us (12%)
  between operations  1.19 us (1%)
  local copies, waits for them, and re-layouts  1.11 us (1%)
    pallas_call x13, Pallas kernels, call(): pl.pallas_call(kernel, out_shape=outs, in_specs=[VM] * (len(ins) - free)...  37.9 us
    ppermute x24, starting transfers between devices, exchange(): lax.ppermute(block, axes, [(a, a ^ step) for a in range(4)])  25.8 us
    ppermute x24, waiting for transfers between devices, exchange(): lax.ppermute(block, axes, [(a, a ^ step) for a in range(4)])  10 us
    pallas_call x2, Pallas kernels, pack(): pl.pallas_call(functools.partial(pack_kernel, first), out_shape=[jax.Shap...  9.31 us
    ppermute x4, starting transfers between devices, swap(): return lax.ppermute(part, axis, [(a, a ^ step) for a in range(size)])  4.34 us
  transfers between devices with their start and end apart: 28, of which 12 were waited for; matrix products, arithmetic and copies ran while one was open for 0% of the time, Pallas kernels for 31%

profile of v3, /device:TPU:0, one launch (start us, length us, event | category | flops | bytes accessed | tf_op | source)
XLA Modules:
  0.0 90.9 jit_solution(3744113719079090075)
XLA Ops:
  2.5 3.0 %collective-permute-start = (bf16[256,128]{1,0:T(8,128)(2,1)S(1)}, bf16[256,128]{1,0:T(8,128)(2,1)S(1)}, u32[]{:S(2)}, u32[]{:S(2)}) collective-permute-start(bf16[256,128]{1,0:T(8,128)(2,1)S(1)} %get-tuple-element.67), channel_id=1, source_target_pairs={{0,2},{1,3},{2,0},{3,1},{4,6},{5,7},{6,4},{7,5},{8,10},{9,11},{10,... | collective-permute-start | bytes 196616 | tf_op jit(solution)/shard_map/ppermute | solution.py:659
  5.7 3.8 %pack.2 = (bf16[2,2,32,64,128]{4,3,2,1,0:T(8,128)(2,1)S(1)}, f32[8,128]{1,0:T(8,128)S(1)}) custom-call(bf16[2,32,32,64,32]{4,3,2,1,0:T(8,128)(2,1)} %bitcast.11, bf16[256,128]{1,0:T(8,128)(2,1)S(1)} %get-tuple-element.66.after.r0), custom_call_target="tpu_custom_call" | custom-call | bytes 9000000 | tf_op jit(solution)/shard_map/pack/pallas_call | solution.py:642
  10.0 3.0 %collective-permute-start.3 = (bf16[256,128]{1,0:T(8,128)(2,1)S(1)}, bf16[256,128]{1,0:T(8,128)(2,1)S(1)}, u32[]{:S(2)}, u32[]{:S(2)}) collective-permute-start(bf16[256,128]{1,0:T(8,128)(2,1)S(1)} %get-tuple-element.72), channel_id=1, source_target_pairs={{0,8},{4,12},{8,0},{12,4},{1,9},{5,13},{9,1},{13,5},{2,10},{6,14},... | collective-permute-start | bytes 196616 | tf_op jit(solution)/shard_map/ppermute | solution.py:659
  13.0 1.4 %collective-permute-start.4 = (bf16[256,128]{1,0:T(8,128)(2,1)S(1)}, bf16[256,128]{1,0:T(8,128)(2,1)S(1)}, u32[]{:S(2)}, u32[]{:S(2)}) collective-permute-start(bf16[256,128]{1,0:T(8,128)(2,1)S(1)} %get-tuple-element.73), channel_id=1, source_target_pairs={{0,12},{4,8},{8,4},{12,0},{1,13},{5,9},{9,5},{13,1},{2,14},{6,10},... | collective-permute-start | bytes 196616 | tf_op jit(solution)/shard_map/ppermute | solution.py:659
  14.6 5.5 %pack.3 = (bf16[3,2,32,64,128]{4,3,2,1,0:T(8,128)(2,1)S(1)}, f32[8,128]{1,0:T(8,128)}) custom-call(bf16[2,32,32,64,32]{4,3,2,1,0:T(8,128)(2,1)} %bitcast.12, bf16[256,128]{1,0:T(8,128)(2,1)S(1)} %get-tuple-element.71.after.r0), custom_call_target="tpu_custom_call" | custom-call | bytes 15000000 | tf_op jit(solution)/shard_map/pack/pallas_call | solution.py:642
  20.3 7.1 %mix_forward.1 = (bf16[8,2,64,128]{3,2,1,0:T(8,128)(2,1)S(1)}, bf16[256,128]{1,0:T(8,128)(2,1)S(1)}, bf16[256,128]{1,0:T(8,128)(2,1)S(1)}, bf16[256,128]{1,0:T(8...) custom-call(bf16[256,128]{1,0:T(8,128)(2,1)S(1)} %get-tuple-element.71.after.r0, ...), custom_call_target="tpu_custom_call" | custom-call | bytes 24000000 | tf_op jit(solution)/shard_map/mix_forward/pallas_call | solution.py:624
  27.4 2.9 %collective-permute-start.6 = (bf16[256,128]{1,0:T(8,128)(2,1)S(1)}, bf16[256,128]{1,0:T(8,128)(2,1)S(1)}, u32[]{:S(2)}, u32[]{:S(2)}) collective-permute-start(bf16[256,128]{1,0:T(8,128)(2,1)S(1)} %get-tuple-element.78), channel_id=1, source_target_pairs={{0,8},{4,12},{8,0},{12,4},{1,9},{5,13},{9,1},{13,5},{2,10},{6,14},... | collective-permute-start | bytes 196616 | tf_op jit(solution)/shard_map/ppermute | solution.py:659
  30.2 1.4 %collective-permute-start.7 = (bf16[256,128]{1,0:T(8,128)(2,1)S(1)}, bf16[256,128]{1,0:T(8,128)(2,1)S(1)}, u32[]{:S(2)}, u32[]{:S(2)}) collective-permute-start(bf16[256,128]{1,0:T(8,128)(2,1)S(1)} %get-tuple-element.79), channel_id=1, source_target_pairs={{0,12},{4,8},{8,4},{12,0},{1,13},{5,9},{9,5},{13,1},{2,14},{6,10},... | collective-permute-start | bytes 196616 | tf_op jit(solution)/shard_map/ppermute | solution.py:659
  31.7 2.6 %cells.1 = (bf16[4,256,256]{2,1,0:T(8,128)(2,1)S(1)}, bf16[4,256,256]{2,1,0:T(8,128)(2,1)S(1)}, f32[4,256,256]{2,1,0:T(8,128)S(1)}, f32[4,1024,256]{2,1,0:T(8,12...) custom-call(bf16[2048,128]{1,0:T(8,128)(2,1)S(1)} %bitcast.8, ...), custom_call_target="tpu_custom_call" | custom-call | bytes 9000000 | tf_op jit(solution)/shard_map/cells/pallas_call | solution.py:624
  34.9 1.6 %collective-permute-done.7.r2 = bf16[256,128]{1,0:T(8,128)(2,1)S(1)} collective-permute-done((bf16[256,128]{1,0:T(8,128)(2,1)S(1)}, bf16[256,128]{1,0:T(8,128)(2,1)S(1)}, u32[]{:S(2)}, u32[]{:S(2)}) %collective-permute-start.7) | collective-permute-done | bytes 65568 | tf_op jit(solution)/shard_map/ppermute | solution.py:659
  36.9 1.6 %collective-permute-start.9 = (bf16[256,128]{1,0:T(8,128)(2,1)S(1)}, bf16[256,128]{1,0:T(8,128)(2,1)S(1)}, u32[]{:S(2)}, u32[]{:S(2)}) collective-permute-start(bf16[256,128]{1,0:T(8,128)(2,1)S(1)} %get-tuple-element.84), channel_id=1, source_target_pairs={{0,2},{1,3},{2,0},{3,1},{4,6},{5,7},{6,4},{7,5},{8,10},{9,11},{10,... | collective-permute-start | bytes 196616 | tf_op jit(solution)/shard_map/ppermute | solution.py:659
  39.1 2.1 %collective-permute-done.9.r1 = bf16[256,128]{1,0:T(8,128)(2,1)S(1)} collective-permute-done((bf16[256,128]{1,0:T(8,128)(2,1)S(1)}, bf16[256,128]{1,0:T(8,128)(2,1)S(1)}, u32[]{:S(2)}, u32[]{:S(2)}) %collective-permute-start.9) | collective-permute-done | bytes 65568 | tf_op jit(solution)/shard_map/ppermute | solution.py:659
  41.2 1.4 %collective-permute-done.10.r2 = bf16[256,128]{1,0:T(8,128)(2,1)S(1)} collective-permute-done((bf16[256,128]{1,0:T(8,128)(2,1)S(1)}, bf16[256,128]{1,0:T(8,128)(2,1)S(1)}, u32[]{:S(2)}, u32[]{:S(2)}) %collective-permute-start.10) | collective-permute-done | bytes 65568 | tf_op jit(solution)/shard_map/ppermute | solution.py:659
  42.6 4.6 %point.1 = (bf16[256,128]{1,0:T(8,128)(2,1)S(1)}, bf16[256,128]{1,0:T(8,128)(2,1)S(1)}, bf16[256,128]{1,0:T(8,128)(2,1)S(1)}, bf16[256,128]{1,0:T(8,128)(2,1)S(1...) custom-call(bf16[256,128]{1,0:T(8,128)(2,1)S(1)} %get-tuple-element., ...), custom_call_target="tpu_custom_call" | custom-call | bytes 18000000 | tf_op jit(solution)/shard_map/point/pallas_call | solution.py:624
  49.5 1.9 %sums.1.after = f32[96,128]{1,0:T(8,128)S(1)} custom-call(bf16[4,256,256]{2,1,0:T(8,128)(2,1)S(1)} %get-tuple-element.82.after.fx, bf16[4,256,256]{2,1,0:T(8,128)(2,1)S(1)} %get-tuple-element.89.cx, bf16[4,256,256]{2,1,0:T(8,128)(2,1)S(1)} %get-tuple-element.99.pg, bf16[4,1024,256]{2,1,0:T(8,128)(2,1)S(1)} %get-tuple-element.100.act, ...), custom_call_target="tpu_custom_call" | custom-call | bytes 7500000 | tf_op jit(solution)/shard_map/sums/pallas_call | solution.py:624
  52.8 1.2 %collective-permute-start.15 = (bf16[256,128]{1,0:T(8,128)(2,1)S(1)}, bf16[256,128]{1,0:T(8,128)(2,1)S(1)}, u32[]{:S(2)}, u32[]{:S(2)}) collective-permute-start(bf16[256,128]{1,0:T(8,128)(2,1)S(1)} %get-tuple-element.104), channel_id=1, source_target_pairs={{0,8},{4,12},{8,0},{12,4},{1,9},{5,13},{9,1},{13,5},{2,10},{6,14},... | collective-permute-start | bytes 196616 | tf_op jit(solution)/shard_map/ppermute | solution.py:659
  54.0 1.2 %collective-permute-start.16 = (bf16[256,128]{1,0:T(8,128)(2,1)S(1)}, bf16[256,128]{1,0:T(8,128)(2,1)S(1)}, u32[]{:S(2)}, u32[]{:S(2)}) collective-permute-start(bf16[256,128]{1,0:T(8,128)(2,1)S(1)} %get-tuple-element.105), channel_id=1, source_target_pairs={{0,12},{4,8},{8,4},{12,0},{1,13},{5,9},{9,5},{13,1},{2,14},{6,10},... | collective-permute-start | bytes 196616 | tf_op jit(solution)/shard_map/ppermute | solution.py:659
  55.2 1.1 %collective-permute-start.17 = (bf16[256,128]{1,0:T(8,128)(2,1)S(1)}, bf16[256,128]{1,0:T(8,128)(2,1)S(1)}, u32[]{:S(2)}, u32[]{:S(2)}) collective-permute-start(bf16[256,128]{1,0:T(8,128)(2,1)S(1)} %get-tuple-element.106), channel_id=1, source_target_pairs={{0,4},{4,0},{8,12},{12,8},{1,5},{5,1},{9,13},{13,9},{2,6},{6,2},{1... | collective-permute-start | bytes 196616 | tf_op jit(solution)/shard_map/ppermute | solution.py:659
  56.3 1.2 %collective-permute-done.24 = f32[96,128]{1,0:T(8,128)S(1)} collective-permute-done((f32[96,128]{1,0:T(8,128)S(1)}, f32[96,128]{1,0:T(8,128)S(1)}, u32[]{:S(2)}, u32[]{:S(2)}) %collective-permute-start.24) | collective-permute-done | bytes 49184 | tf_op jit(solution)/shard_map/ppermute | solution.py:667
  57.6 1.3 %collective-permute-start.25 = (f32[96,128]{1,0:T(8,128)S(1)}, f32[96,128]{1,0:T(8,128)S(1)}, u32[]{:S(2)}, u32[]{:S(2)}) collective-permute-start(f32[96,128]{1,0:T(8,128)S(1)} %add.9), channel_id=1, source_target_pairs={{0,2},{2,0},{1,3},{3,1},{4,6},{6,4},{5,7},{7,5},{8,10},{10,8},{9,1... | collective-permute-start | bytes 147464 | tf_op jit(solution)/shard_map/ppermute | solution.py:667
  58.9 1.3 %collective-permute-done.15.r1 = bf16[256,128]{1,0:T(8,128)(2,1)S(1)} collective-permute-done((bf16[256,128]{1,0:T(8,128)(2,1)S(1)}, bf16[256,128]{1,0:T(8,128)(2,1)S(1)}, u32[]{:S(2)}, u32[]{:S(2)}) %collective-permute-start.15) | collective-permute-done | bytes 65568 | tf_op jit(solution)/shard_map/ppermute | solution.py:659
  60.6 1.2 %collective-permute-done.17.r3 = bf16[256,128]{1,0:T(8,128)(2,1)S(1)} collective-permute-done((bf16[256,128]{1,0:T(8,128)(2,1)S(1)}, bf16[256,128]{1,0:T(8,128)(2,1)S(1)}, u32[]{:S(2)}, u32[]{:S(2)}) %collective-permute-start.17) | collective-permute-done | bytes 65568 | tf_op jit(solution)/shard_map/ppermute | solution.py:659
  61.8 4.4 %mix_backward.1 = (bf16[32,2,64,128]{3,2,1,0:T(8,128)(2,1)S(1)}, bf16[256,128]{1,0:T(8,128)(2,1)S(1)}, bf16[256,128]{1,0:T(8,128)(2,1)S(1)}, bf16[256,128]{1,0:T(8,128)(2,1)S(1)}, bf16[256,128]{1,0:T(8,128)(2,1)S(1)}) custom-call(bf16[256,128]{1,0:T(8,128)(2,1)S(1)} %get-tuple-element.103.r0, bf16[256,128]{1,0:T(8,128)(2,1)S(1)} %collective-permute-done.15.r1, ...), custom_call_target="tpu_custom_call" | custom-call | bytes 15000000 | tf_op jit(solution)/shard_map/mix_backward/pallas_call | solution.py:624
  66.2 1.8 %collective-permute-start.18 = (bf16[256,128]{1,0:T(8,128)(2,1)S(1)}, bf16[256,128]{1,0:T(8,128)(2,1)S(1)}, u32[]{:S(2)}, u32[]{:S(2)}) collective-permute-start(bf16[256,128]{1,0:T(8,128)(2,1)S(1)} %get-tuple-element.109), channel_id=1, source_target_pairs={{0,8},{4,12},{8,0},{12,4},{1,9},{5,13},{9,1},{13,5},{2,10},{6,14},... | collective-permute-start | bytes 196616 | tf_op jit(solution)/shard_map/ppermute | solution.py:659
  68.0 1.2 %collective-permute-start.19 = (bf16[256,128]{1,0:T(8,128)(2,1)S(1)}, bf16[256,128]{1,0:T(8,128)(2,1)S(1)}, u32[]{:S(2)}, u32[]{:S(2)}) collective-permute-start(bf16[256,128]{1,0:T(8,128)(2,1)S(1)} %get-tuple-element.110), channel_id=1, source_target_pairs={{0,12},{4,8},{8,4},{12,0},{1,13},{5,9},{9,5},{13,1},{2,14},{6,10},... | collective-permute-start | bytes 196616 | tf_op jit(solution)/shard_map/ppermute | solution.py:659
  69.8 1.6 %collective-permute-start.26 = (f32[96,128]{1,0:T(8,128)S(1)}, f32[96,128]{1,0:T(8,128)S(1)}, u32[]{:S(2)}, u32[]{:S(2)}) collective-permute-start(f32[96,128]{1,0:T(8,128)S(1)} %add.10), channel_id=1, source_target_pairs={{0,4},{4,0},{8,12},{12,8},{1,5},{5,1},{9,13},{13,9},{2,6},{6,2},{1... | collective-permute-start | bytes 147464 | tf_op jit(solution)/shard_map/ppermute | solution.py:667
  71.4 5.0 %outer.2 = (bf16[2,32,32,64,32]{4,3,2,1,0:T(8,128)(2,1)}, f32[8,128]{1,0:T(8,128)S(1)}) custom-call(bf16[8,2,64,128]{3,2,1,0:T(8,128)(2,1)S(1)} %get-tuple-element.112.modes, bf16[32,2,64,128]{3,2,1,0:T(8,128)(2,1)S(1)} %get-tuple-element.113.pmodes), custom_call_target="tpu_custom_call" | custom-call | bytes 15000000 | tf_op jit(solution)/shard_map/outer/pallas_call | solution.py:624
  76.7 1.1 %collective-permute-start.21 = (bf16[256,128]{1,0:T(8,128)(2,1)S(1)}, bf16[256,128]{1,0:T(8,128)(2,1)S(1)}, u32[]{:S(2)}, u32[]{:S(2)}) collective-permute-start(bf16[256,128]{1,0:T(8,128)(2,1)S(1)} %get-tuple-element.116), channel_id=1, source_target_pairs={{0,2},{1,3},{2,0},{3,1},{4,6},{5,7},{6,4},{7,5},{8,10},{9,11},{10,... | collective-permute-start | bytes 196616 | tf_op jit(solution)/shard_map/ppermute | solution.py:659
  77.8 1.1 %collective-permute-start.23 = (bf16[256,128]{1,0:T(8,128)(2,1)S(1)}, bf16[256,128]{1,0:T(8,128)(2,1)S(1)}, u32[]{:S(2)}, u32[]{:S(2)}) collective-permute-start(bf16[256,128]{1,0:T(8,128)(2,1)S(1)} %get-tuple-element.118), channel_id=1, source_target_pairs={{0,1},{1,0},{2,3},{3,2},{4,5},{5,4},{6,7},{7,6},{8,9},{9,8},{10,11... | collective-permute-start | bytes 196616 | tf_op jit(solution)/shard_map/ppermute | solution.py:659
  79.0 1.5 %collective-permute-start.27 = (f32[96,128]{1,0:T(8,128)S(1)}, f32[96,128]{1,0:T(8,128)S(1)}, u32[]{:S(2)}, u32[]{:S(2)}) collective-permute-start(f32[96,128]{1,0:T(8,128)S(1)} %add.11.part), channel_id=1, source_target_pairs={{0,8},{4,12},{8,0},{12,4},{1,9},{5,13},{9,1},{13,5},{2,10},{6,14},... | collective-permute-start | bytes 147464 | tf_op jit(solution)/shard_map/ppermute | solution.py:667
  80.4 4.3 %outer.3 = (bf16[2,32,32,64,32]{4,3,2,1,0:T(8,128)(2,1)}, f32[8,128]{1,0:T(8,128)}) custom-call(bf16[8,2,64,128]{3,2,1,0:T(8,128)(2,1)S(1)} %get-tuple-element.112.modes, bf16[32,2,64,128]{3,2,1,0:T(8,128)(2,1)S(1)} %get-tuple-element.113.pmodes, bf16[256,128]{1,0:T(8,128)(2,1)S(1)} %get-tuple-element.115.rest_0_.r0, ...), custom_call_target="tpu_custom_call", output_to_operand_aliasing={{0}: (3, {})} | custom-call | bytes 12000000 | tf_op jit(solution)/shard_map/outer/pallas_call | solution.py:624
  84.8 5.9 %finish.1 = (bf16[2048,128]{1,0:T(8,128)(2,1)}, f32[32,128]{1,0:T(8,128)}, f32[32,128]{1,0:T(8,128)}, f32[32,32]{1,0:T(8,128)}, bf16[2,32,32,64,32]{4,3,2,1,0:T(8,128)(2,1)}) custom-call(bf16[256,128]{1,0:T(8,128)(2,1)S(1)} %get-tuple-element.115.rest_0_.r0, bf16[256,128]{1,0:T(8,128)(2,1)S(1)} %collective-permute-done.21.r1, ...), custom_call_target="tpu_custom_call", output_to_operand_aliasing={{4}: (11, {})} | custom-call | bytes 12000000 | tf_op jit(solution)/shard_map/finish/pallas_call | solution.py:624
  (70 shorter events, 9.4 us)
Async XLA Ops:
  2.5 7.0 %collective-permute-start = (bf16[256,128]{1,0:T(8,128)(2,1)S(1)}, bf16[256,128]{1,0:T(8,128)(2,1)S(1)}, u32[]{:S(2)}, u32[]{:S(2)}) collective-permute-start(bf16[256,128]{1,0:T(8,128)(2,1)S(1)} %get-tuple-element.67), channel_id=1, source_target_pairs={{0,2},{1,3},{2,0},{3,1},{4,6},{5,7},{6,4},{7,5},{8,10},{9,11},{10,... | collective-permute-start | bytes 196616 | tf_op jit(solution)/shard_map/ppermute | solution.py:659
  5.5 4.1 %collective-permute-start.1 = (bf16[256,128]{1,0:T(8,128)(2,1)S(1)}, bf16[256,128]{1,0:T(8,128)(2,1)S(1)}, u32[]{:S(2)}, u32[]{:S(2)}) collective-permute-start(bf16[256,128]{1,0:T(8,128)(2,1)S(1)} %get-tuple-element.68), channel_id=1, source_target_pairs={{0,3},{1,2},{2,1},{3,0},{4,7},{5,6},{6,5},{7,4},{8,11},{9,10},{10,... | collective-permute-start | bytes 196616 | tf_op jit(solution)/shard_map/ppermute | solution.py:659
  5.5 4.1 %collective-permute-start.2 = (bf16[256,128]{1,0:T(8,128)(2,1)S(1)}, bf16[256,128]{1,0:T(8,128)(2,1)S(1)}, u32[]{:S(2)}, u32[]{:S(2)}) collective-permute-start(bf16[256,128]{1,0:T(8,128)(2,1)S(1)} %get-tuple-element.69), channel_id=1, source_target_pairs={{0,1},{1,0},{2,3},{3,2},{4,5},{5,4},{6,7},{7,6},{8,9},{9,8},{10,11... | collective-permute-start | bytes 196616 | tf_op jit(solution)/shard_map/ppermute | solution.py:659
  10.0 10.1 %collective-permute-start.3 = (bf16[256,128]{1,0:T(8,128)(2,1)S(1)}, bf16[256,128]{1,0:T(8,128)(2,1)S(1)}, u32[]{:S(2)}, u32[]{:S(2)}) collective-permute-start(bf16[256,128]{1,0:T(8,128)(2,1)S(1)} %get-tuple-element.72), channel_id=1, source_target_pairs={{0,8},{4,12},{8,0},{12,4},{1,9},{5,13},{9,1},{13,5},{2,10},{6,14},... | collective-permute-start | bytes 196616 | tf_op jit(solution)/shard_map/ppermute | solution.py:659
  13.0 7.1 %collective-permute-start.4 = (bf16[256,128]{1,0:T(8,128)(2,1)S(1)}, bf16[256,128]{1,0:T(8,128)(2,1)S(1)}, u32[]{:S(2)}, u32[]{:S(2)}) collective-permute-start(bf16[256,128]{1,0:T(8,128)(2,1)S(1)} %get-tuple-element.73), channel_id=1, source_target_pairs={{0,12},{4,8},{8,4},{12,0},{1,13},{5,9},{9,5},{13,1},{2,14},{6,10},... | collective-permute-start | bytes 196616 | tf_op jit(solution)/shard_map/ppermute | solution.py:659
  14.4 5.8 %collective-permute-start.5 = (bf16[256,128]{1,0:T(8,128)(2,1)S(1)}, bf16[256,128]{1,0:T(8,128)(2,1)S(1)}, u32[]{:S(2)}, u32[]{:S(2)}) collective-permute-start(bf16[256,128]{1,0:T(8,128)(2,1)S(1)} %get-tuple-element.74), channel_id=1, source_target_pairs={{0,4},{4,0},{8,12},{12,8},{1,5},{5,1},{9,13},{13,9},{2,6},{6,2},{1... | collective-permute-start | bytes 196616 | tf_op jit(solution)/shard_map/ppermute | solution.py:659
  20.2 11.4 %copy-start.1 = (bf16[32,8,8,128]{3,2,1,0:T(8,128)(2,1)S(1)}, bf16[32,8,8,128]{3,2,1,0:T(8,128)(2,1)}, u32[]{:S(2)}) copy-start(bf16[32,8,8,128]{3,2,1,0:T(8,128)(2,1)} %param.14) | copy-start | bytes 1572868
  20.2 11.4 %copy-start.3 = (bf16[4,128,1024]{2,1,0:T(8,128)(2,1)S(1)}, bf16[4,128,1024]{2,1,0:T(8,128)(2,1)}, u32[]{:S(2)}) copy-start(bf16[4,128,1024]{2,1,0:T(8,128)(2,1)} %constant.17.clone.zi) | copy-start | bytes 3145732
  27.4 7.5 %collective-permute-start.6 = (bf16[256,128]{1,0:T(8,128)(2,1)S(1)}, bf16[256,128]{1,0:T(8,128)(2,1)S(1)}, u32[]{:S(2)}, u32[]{:S(2)}) collective-permute-start(bf16[256,128]{1,0:T(8,128)(2,1)S(1)} %get-tuple-element.78), channel_id=1, source_target_pairs={{0,8},{4,12},{8,0},{12,4},{1,9},{5,13},{9,1},{13,5},{2,10},{6,14},... | collective-permute-start | bytes 196616 | tf_op jit(solution)/shard_map/ppermute | solution.py:659
  30.2 6.2 %collective-permute-start.7 = (bf16[256,128]{1,0:T(8,128)(2,1)S(1)}, bf16[256,128]{1,0:T(8,128)(2,1)S(1)}, u32[]{:S(2)}, u32[]{:S(2)}) collective-permute-start(bf16[256,128]{1,0:T(8,128)(2,1)S(1)} %get-tuple-element.79), channel_id=1, source_target_pairs={{0,12},{4,8},{8,4},{12,0},{1,13},{5,9},{9,5},{13,1},{2,14},{6,10},... | collective-permute-start | bytes 196616 | tf_op jit(solution)/shard_map/ppermute | solution.py:659
  31.6 5.0 %collective-permute-start.8 = (bf16[256,128]{1,0:T(8,128)(2,1)S(1)}, bf16[256,128]{1,0:T(8,128)(2,1)S(1)}, u32[]{:S(2)}, u32[]{:S(2)}) collective-permute-start(bf16[256,128]{1,0:T(8,128)(2,1)S(1)} %get-tuple-element.80), channel_id=1, source_target_pairs={{0,4},{4,0},{8,12},{12,8},{1,5},{5,1},{9,13},{13,9},{2,6},{6,2},{1... | collective-permute-start | bytes 196616 | tf_op jit(solution)/shard_map/ppermute | solution.py:659
  36.9 4.3 %collective-permute-start.9 = (bf16[256,128]{1,0:T(8,128)(2,1)S(1)}, bf16[256,128]{1,0:T(8,128)(2,1)S(1)}, u32[]{:S(2)}, u32[]{:S(2)}) collective-permute-start(bf16[256,128]{1,0:T(8,128)(2,1)S(1)} %get-tuple-element.84), channel_id=1, source_target_pairs={{0,2},{1,3},{2,0},{3,1},{4,6},{5,7},{6,4},{7,5},{8,10},{9,11},{10,... | collective-permute-start | bytes 196616 | tf_op jit(solution)/shard_map/ppermute | solution.py:659
  38.4 4.2 %collective-permute-start.10 = (bf16[256,128]{1,0:T(8,128)(2,1)S(1)}, bf16[256,128]{1,0:T(8,128)(2,1)S(1)}, u32[]{:S(2)}, u32[]{:S(2)}) collective-permute-start(bf16[256,128]{1,0:T(8,128)(2,1)S(1)} %get-tuple-element.85), channel_id=1, source_target_pairs={{0,3},{1,2},{2,1},{3,0},{4,7},{5,6},{6,5},{7,4},{8,11},{9,10},{10,... | collective-permute-start | bytes 196616 | tf_op jit(solution)/shard_map/ppermute | solution.py:659
  38.4 4.2 %collective-permute-start.11 = (bf16[256,128]{1,0:T(8,128)(2,1)S(1)}, bf16[256,128]{1,0:T(8,128)(2,1)S(1)}, u32[]{:S(2)}, u32[]{:S(2)}) collective-permute-start(bf16[256,128]{1,0:T(8,128)(2,1)S(1)} %get-tuple-element.86), channel_id=1, source_target_pairs={{0,1},{1,0},{2,3},{3,2},{4,5},{5,4},{6,7},{7,6},{8,9},{9,8},{10,11... | collective-permute-start | bytes 196616 | tf_op jit(solution)/shard_map/ppermute | solution.py:659
  47.2 14.5 %copy-start.5 = (bf16[4,2,32,1024]{3,2,1,0:T(8,128)(2,1)S(1)}, bf16[4,2,32,1024]{3,2,1,0:T(8,128)(2,1)}, u32[]{:S(2)}) copy-start(bf16[4,2,32,1024]{3,2,1,0:T(8,128)(2,1)} %constant.21.clone.xr) | copy-start | bytes 1572868
  47.2 14.5 %copy-start.9 = (bf16[4,32,256]{2,1,0:T(8,128)(2,1)S(1)}, bf16[4,32,256]{2,1,0:T(8,128)(2,1)}, u32[]{:S(2)}) copy-start(bf16[4,32,256]{2,1,0:T(8,128)(2,1)} %constant.23.clone.xd) | copy-start | bytes 196612
  47.2 4.8 %collective-permute-start.12 = (bf16[256,128]{1,0:T(8,128)(2,1)S(1)}, bf16[256,128]{1,0:T(8,128)(2,1)S(1)}, u32[]{:S(2)}, u32[]{:S(2)}) collective-permute-start(bf16[256,128]{1,0:T(8,128)(2,1)S(1)} %get-tuple-element.95), channel_id=1, source_target_pairs={{0,2},{1,3},{2,0},{3,1},{4,6},{5,7},{6,4},{7,5},{8,10},{9,11},{10,... | collective-permute-start | bytes 196616 | tf_op jit(solution)/shard_map/ppermute | solution.py:659
  48.1 4.4 %collective-permute-start.13 = (bf16[256,128]{1,0:T(8,128)(2,1)S(1)}, bf16[256,128]{1,0:T(8,128)(2,1)S(1)}, u32[]{:S(2)}, u32[]{:S(2)}) collective-permute-start(bf16[256,128]{1,0:T(8,128)(2,1)S(1)} %get-tuple-element.96), channel_id=1, source_target_pairs={{0,3},{1,2},{2,1},{3,0},{4,7},{5,6},{6,5},{7,4},{8,11},{9,10},{10,... | collective-permute-start | bytes 196616 | tf_op jit(solution)/shard_map/ppermute | solution.py:659
  48.6 3.9 %collective-permute-start.14 = (bf16[256,128]{1,0:T(8,128)(2,1)S(1)}, bf16[256,128]{1,0:T(8,128)(2,1)S(1)}, u32[]{:S(2)}, u32[]{:S(2)}) collective-permute-start(bf16[256,128]{1,0:T(8,128)(2,1)S(1)} %get-tuple-element.97), channel_id=1, source_target_pairs={{0,1},{1,0},{2,3},{3,2},{4,5},{5,4},{6,7},{7,6},{8,9},{9,8},{10,11... | collective-permute-start | bytes 196616 | tf_op jit(solution)/shard_map/ppermute | solution.py:659
  52.8 7.4 %collective-permute-start.15 = (bf16[256,128]{1,0:T(8,128)(2,1)S(1)}, bf16[256,128]{1,0:T(8,128)(2,1)S(1)}, u32[]{:S(2)}, u32[]{:S(2)}) collective-permute-start(bf16[256,128]{1,0:T(8,128)(2,1)S(1)} %get-tuple-element.104), channel_id=1, source_target_pairs={{0,8},{4,12},{8,0},{12,4},{1,9},{5,13},{9,1},{13,5},{2,10},{6,14},... | collective-permute-start | bytes 196616 | tf_op jit(solution)/shard_map/ppermute | solution.py:659
  54.0 6.6 %collective-permute-start.16 = (bf16[256,128]{1,0:T(8,128)(2,1)S(1)}, bf16[256,128]{1,0:T(8,128)(2,1)S(1)}, u32[]{:S(2)}, u32[]{:S(2)}) collective-permute-start(bf16[256,128]{1,0:T(8,128)(2,1)S(1)} %get-tuple-element.105), channel_id=1, source_target_pairs={{0,12},{4,8},{8,4},{12,0},{1,13},{5,9},{9,5},{13,1},{2,14},{6,10},... | collective-permute-start | bytes 196616 | tf_op jit(solution)/shard_map/ppermute | solution.py:659
  55.2 6.5 %collective-permute-start.17 = (bf16[256,128]{1,0:T(8,128)(2,1)S(1)}, bf16[256,128]{1,0:T(8,128)(2,1)S(1)}, u32[]{:S(2)}, u32[]{:S(2)}) collective-permute-start(bf16[256,128]{1,0:T(8,128)(2,1)S(1)} %get-tuple-element.106), channel_id=1, source_target_pairs={{0,4},{4,0},{8,12},{12,8},{1,5},{5,1},{9,13},{13,9},{2,6},{6,2},{1... | collective-permute-start | bytes 196616 | tf_op jit(solution)/shard_map/ppermute | solution.py:659
  56.3 1.2 %collective-permute-start.24 = (f32[96,128]{1,0:T(8,128)S(1)}, f32[96,128]{1,0:T(8,128)S(1)}, u32[]{:S(2)}, u32[]{:S(2)}) collective-permute-start(f32[96,128]{1,0:T(8,128)S(1)} %sums.1.after), channel_id=1, source_target_pairs={{0,1},{1,0},{2,3},{3,2},{4,5},{5,4},{6,7},{7,6},{8,9},{9,8},{10,11... | collective-permute-start | bytes 147464 | tf_op jit(solution)/shard_map/ppermute | solution.py:667
  57.6 12.2 %collective-permute-start.25 = (f32[96,128]{1,0:T(8,128)S(1)}, f32[96,128]{1,0:T(8,128)S(1)}, u32[]{:S(2)}, u32[]{:S(2)}) collective-permute-start(f32[96,128]{1,0:T(8,128)S(1)} %add.9), channel_id=1, source_target_pairs={{0,2},{2,0},{1,3},{3,1},{4,6},{6,4},{5,7},{7,5},{8,10},{10,8},{9,1... | collective-permute-start | bytes 147464 | tf_op jit(solution)/shard_map/ppermute | solution.py:667
  66.2 10.2 %collective-permute-start.18 = (bf16[256,128]{1,0:T(8,128)(2,1)S(1)}, bf16[256,128]{1,0:T(8,128)(2,1)S(1)}, u32[]{:S(2)}, u32[]{:S(2)}) collective-permute-start(bf16[256,128]{1,0:T(8,128)(2,1)S(1)} %get-tuple-element.109), channel_id=1, source_target_pairs={{0,8},{4,12},{8,0},{12,4},{1,9},{5,13},{9,1},{13,5},{2,10},{6,14},... | collective-permute-start | bytes 196616 | tf_op jit(solution)/shard_map/ppermute | solution.py:659
  68.0 8.4 %collective-permute-start.19 = (bf16[256,128]{1,0:T(8,128)(2,1)S(1)}, bf16[256,128]{1,0:T(8,128)(2,1)S(1)}, u32[]{:S(2)}, u32[]{:S(2)}) collective-permute-start(bf16[256,128]{1,0:T(8,128)(2,1)S(1)} %get-tuple-element.110), channel_id=1, source_target_pairs={{0,12},{4,8},{8,4},{12,0},{1,13},{5,9},{9,5},{13,1},{2,14},{6,10},... | collective-permute-start | bytes 196616 | tf_op jit(solution)/shard_map/ppermute | solution.py:659
  69.2 7.2 %collective-permute-start.20 = (bf16[256,128]{1,0:T(8,128)(2,1)S(1)}, bf16[256,128]{1,0:T(8,128)(2,1)S(1)}, u32[]{:S(2)}, u32[]{:S(2)}) collective-permute-start(bf16[256,128]{1,0:T(8,128)(2,1)S(1)} %get-tuple-element.111), channel_id=1, source_target_pairs={{0,4},{4,0},{8,12},{12,8},{1,5},{5,1},{9,13},{13,9},{2,6},{6,2},{1... | collective-permute-start | bytes 196616 | tf_op jit(solution)/shard_map/ppermute | solution.py:659
  69.8 9.2 %collective-permute-start.26 = (f32[96,128]{1,0:T(8,128)S(1)}, f32[96,128]{1,0:T(8,128)S(1)}, u32[]{:S(2)}, u32[]{:S(2)}) collective-permute-start(f32[96,128]{1,0:T(8,128)S(1)} %add.10), channel_id=1, source_target_pairs={{0,4},{4,0},{8,12},{12,8},{1,5},{5,1},{9,13},{13,9},{2,6},{6,2},{1... | collective-permute-start | bytes 147464 | tf_op jit(solution)/shard_map/ppermute | solution.py:667
  76.7 8.0 %collective-permute-start.21 = (bf16[256,128]{1,0:T(8,128)(2,1)S(1)}, bf16[256,128]{1,0:T(8,128)(2,1)S(1)}, u32[]{:S(2)}, u32[]{:S(2)}) collective-permute-start(bf16[256,128]{1,0:T(8,128)(2,1)S(1)} %get-tuple-element.116), channel_id=1, source_target_pairs={{0,2},{1,3},{2,0},{3,1},{4,6},{5,7},{6,4},{7,5},{8,10},{9,11},{10,... | collective-permute-start | bytes 196616 | tf_op jit(solution)/shard_map/ppermute | solution.py:659
  77.8 7.0 %collective-permute-start.22 = (bf16[256,128]{1,0:T(8,128)(2,1)S(1)}, bf16[256,128]{1,0:T(8,128)(2,1)S(1)}, u32[]{:S(2)}, u32[]{:S(2)}) collective-permute-start(bf16[256,128]{1,0:T(8,128)(2,1)S(1)} %get-tuple-element.117), channel_id=1, source_target_pairs={{0,3},{1,2},{2,1},{3,0},{4,7},{5,6},{6,5},{7,4},{8,11},{9,10},{10,... | collective-permute-start | bytes 196616 | tf_op jit(solution)/shard_map/ppermute | solution.py:659
  77.8 7.0 %collective-permute-start.23 = (bf16[256,128]{1,0:T(8,128)(2,1)S(1)}, bf16[256,128]{1,0:T(8,128)(2,1)S(1)}, u32[]{:S(2)}, u32[]{:S(2)}) collective-permute-start(bf16[256,128]{1,0:T(8,128)(2,1)S(1)} %get-tuple-element.118), channel_id=1, source_target_pairs={{0,1},{1,0},{2,3},{3,2},{4,5},{5,4},{6,7},{7,6},{8,9},{9,8},{10,11... | collective-permute-start | bytes 196616 | tf_op jit(solution)/shard_map/ppermute | solution.py:659
  79.0 5.8 %collective-permute-start.27 = (f32[96,128]{1,0:T(8,128)S(1)}, f32[96,128]{1,0:T(8,128)S(1)}, u32[]{:S(2)}, u32[]{:S(2)}) collective-permute-start(f32[96,128]{1,0:T(8,128)S(1)} %add.11.part), channel_id=1, source_target_pairs={{0,8},{4,12},{8,0},{12,4},{1,9},{5,13},{9,1},{13,5},{2,10},{6,14},... | collective-permute-start | bytes 147464 | tf_op jit(solution)/shard_map/ppermute | solution.py:667
  (10 other events, 84.6 us)

commit v4 on v3

--- a/solution.py
+++ b/solution.py
@@ -371,6 +371,8 @@
 
 
 def pack_finish(copies, held, packed):
+    row, lane = (lax.broadcasted_iota(jnp.int32, (32, 128), axis) for axis in (0, 1))
+    moved = jnp.where(lane == row + 96, 1.0, 0.0).astype(BF)
     span = held.shape[3] // 4
     for g in range(held.shape[0]):
         for h in range(4):
@@ -378,9 +380,9 @@
 
             def step(o, carry):
                 for p in range(2):
-                    packed[g, p, o] = jnp.concatenate(
-                        [held[g, p, k, o] for k in range(4)], axis=1
-                    )
+                    three = [held[g, p, k, o] for k in range(3)] + [jnp.zeros((64, 32), BF)]
+                    fourth = dot(held[g, p, 3, o], moved).astype(BF)
+                    packed[g, p, o] = jnp.concatenate(three, axis=1) + fourth
                 return carry
 
             lax.fori_loop(h * span, (h + 1) * span, step, 0, unroll=8)
@@ -397,16 +399,19 @@
     for g in range(held.shape[0]):
         for p in range(2):
             m = modes[start + g, p].astype(F32)
-            for k in range(4):
+            for k in range(3):
                 turned[k, p] = (pltpu.roll(m, (128 - 32 * k) % 128, 1) if k else m).astype(BF)
         for h in range(4):
 
             def step(o, carry):
                 pr, pi = pmodes[o, 0], pmodes[o, 1]
-                for k in range(4):
+                for k in range(3):
                     mr, mi = turned[k, 0], turned[k, 1]
-                    held[g, 0, k, o] = (mr * pr + mi * pi)[:, :32]
-                    held[g, 1, k, o] = (mr * pi - mi * pr)[:, :32]
+                    both = mr * pr + mi * pi, mr * pi - mi * pr
+                    for p in range(2):
+                        held[g, p, k, o] = both[p][:, :32]
+                        if k == 1:
+                            held[g, p, 3, o] = pltpu.roll(both[p], 64, 1)[:, :32]
                 return carry
 
             lax.fori_loop(h * span, (h + 1) * span, step, 0, unroll=8)
@@ -425,7 +430,7 @@
 def outer_scratch(count, chans):
     return [
         pltpu.VMEM((count, 2, 4, chans, 64, 32), BF),
-        pltpu.VMEM((4, 2, 64, 128), BF),
+        pltpu.VMEM((3, 2, 64, 128), BF),
         pltpu.SemaphoreType.DMA((count, 4)),
     ]
 
@@ -553,7 +558,7 @@
                 ]
         return carry
 
-    lax.fori_loop(0, 4, step, 0, unroll=2)
+    lax.fori_loop(0, 4, step, 0, unroll=4)
     side = jnp.concatenate([wide[y].astype(BF) for y in range(8)], axis=1)
     out = dot(side, table[...]).astype(BF)
     for s, o in enumerate((o0, o1, o2, o3)):
@@ -599,7 +604,7 @@
                 ]
         return carry
 
-    lax.fori_loop(0, 4, step, 0, unroll=2)
+    lax.fori_loop(0, 4, step, 0, unroll=4)
     out[...] = wide[...].astype(BF)
     for copy in copies:
         copy.wait()

time: 91.1 us -> 90.3 us (level)
  no operation moved by 1% of the time
where the time goes in v4:
time: 90.3 us; the launch traced here: 90.2 us
  Pallas kernels  46.5 us (51%)
  starting transfers between devices  30.1 us (33%)
  waiting for transfers between devices  11.3 us (13%)
  between operations  1.19 us (1%)
  local copies, waits for them, and re-layouts  1.11 us (1%)
    pallas_call x13, Pallas kernels, call(): pl.pallas_call(kernel, out_shape=outs, in_specs=[VM] * (len(ins) - free)...  37.2 us
    ppermute x24, starting transfers between devices, exchange(): lax.ppermute(block, axes, [(a, a ^ step) for a in range(4)])  25.7 us
    ppermute x24, waiting for transfers between devices, exchange(): lax.ppermute(block, axes, [(a, a ^ step) for a in range(4)])  10.1 us
    pallas_call x2, Pallas kernels, pack(): pl.pallas_call(functools.partial(pack_kernel, first), out_shape=[jax.Shap...  9.27 us
    ppermute x4, starting transfers between devices, swap(): return lax.ppermute(part, axis, [(a, a ^ step) for a in range(size)])  4.34 us
  transfers between devices with their start and end apart: 28, of which 12 were waited for; matrix products, arithmetic and copies ran while one was open for 0% of the time, Pallas kernels for 31%

profile of v4, /device:TPU:0, one launch (start us, length us, event | category | flops | bytes accessed | tf_op | source)
XLA Modules:
  0.0 90.2 jit_solution(18224272297879418865)
XLA Ops:
  2.5 3.0 %collective-permute-start = (bf16[256,128]{1,0:T(8,128)(2,1)S(1)}, bf16[256,128]{1,0:T(8,128)(2,1)S(1)}, u32[]{:S(2)}, u32[]{:S(2)}) collective-permute-start(bf16[256,128]{1,0:T(8,128)(2,1)S(1)} %get-tuple-element.67), channel_id=1, source_target_pairs={{0,2},{1,3},{2,0},{3,1},{4,6},{5,7},{6,4},{7,5},{8,10},{9,11},{10,... | collective-permute-start | bytes 196616 | tf_op jit(solution)/shard_map/ppermute | solution.py:664
  5.7 3.8 %pack.2 = (bf16[2,2,32,64,128]{4,3,2,1,0:T(8,128)(2,1)S(1)}, f32[8,128]{1,0:T(8,128)S(1)}) custom-call(bf16[2,32,32,64,32]{4,3,2,1,0:T(8,128)(2,1)} %bitcast.11, bf16[256,128]{1,0:T(8,128)(2,1)S(1)} %get-tuple-element.66.after.r0), custom_call_target="tpu_custom_call" | custom-call | bytes 9000000 | tf_op jit(solution)/shard_map/pack/pallas_call | solution.py:647
  10.0 3.0 %collective-permute-start.3 = (bf16[256,128]{1,0:T(8,128)(2,1)S(1)}, bf16[256,128]{1,0:T(8,128)(2,1)S(1)}, u32[]{:S(2)}, u32[]{:S(2)}) collective-permute-start(bf16[256,128]{1,0:T(8,128)(2,1)S(1)} %get-tuple-element.72), channel_id=1, source_target_pairs={{0,8},{4,12},{8,0},{12,4},{1,9},{5,13},{9,1},{13,5},{2,10},{6,14},... | collective-permute-start | bytes 196616 | tf_op jit(solution)/shard_map/ppermute | solution.py:664
  13.0 1.4 %collective-permute-start.4 = (bf16[256,128]{1,0:T(8,128)(2,1)S(1)}, bf16[256,128]{1,0:T(8,128)(2,1)S(1)}, u32[]{:S(2)}, u32[]{:S(2)}) collective-permute-start(bf16[256,128]{1,0:T(8,128)(2,1)S(1)} %get-tuple-element.73), channel_id=1, source_target_pairs={{0,12},{4,8},{8,4},{12,0},{1,13},{5,9},{9,5},{13,1},{2,14},{6,10},... | collective-permute-start | bytes 196616 | tf_op jit(solution)/shard_map/ppermute | solution.py:664
  14.6 5.5 %pack.3 = (bf16[3,2,32,64,128]{4,3,2,1,0:T(8,128)(2,1)S(1)}, f32[8,128]{1,0:T(8,128)}) custom-call(bf16[2,32,32,64,32]{4,3,2,1,0:T(8,128)(2,1)} %bitcast.12, bf16[256,128]{1,0:T(8,128)(2,1)S(1)} %get-tuple-element.71.after.r0), custom_call_target="tpu_custom_call" | custom-call | bytes 15000000 | tf_op jit(solution)/shard_map/pack/pallas_call | solution.py:647
  20.2 6.8 %mix_forward.1 = (bf16[8,2,64,128]{3,2,1,0:T(8,128)(2,1)S(1)}, bf16[256,128]{1,0:T(8,128)(2,1)S(1)}, bf16[256,128]{1,0:T(8,128)(2,1)S(1)}, bf16[256,128]{1,0:T(8...) custom-call(bf16[256,128]{1,0:T(8,128)(2,1)S(1)} %get-tuple-element.71.after.r0, ...), custom_call_target="tpu_custom_call" | custom-call | bytes 24000000 | tf_op jit(solution)/shard_map/mix_forward/pallas_call | solution.py:629
  27.0 2.9 %collective-permute-start.6 = (bf16[256,128]{1,0:T(8,128)(2,1)S(1)}, bf16[256,128]{1,0:T(8,128)(2,1)S(1)}, u32[]{:S(2)}, u32[]{:S(2)}) collective-permute-start(bf16[256,128]{1,0:T(8,128)(2,1)S(1)} %get-tuple-element.78), channel_id=1, source_target_pairs={{0,8},{4,12},{8,0},{12,4},{1,9},{5,13},{9,1},{13,5},{2,10},{6,14},... | collective-permute-start | bytes 196616 | tf_op jit(solution)/shard_map/ppermute | solution.py:664
  29.9 1.4 %collective-permute-start.7 = (bf16[256,128]{1,0:T(8,128)(2,1)S(1)}, bf16[256,128]{1,0:T(8,128)(2,1)S(1)}, u32[]{:S(2)}, u32[]{:S(2)}) collective-permute-start(bf16[256,128]{1,0:T(8,128)(2,1)S(1)} %get-tuple-element.79), channel_id=1, source_target_pairs={{0,12},{4,8},{8,4},{12,0},{1,13},{5,9},{9,5},{13,1},{2,14},{6,10},... | collective-permute-start | bytes 196616 | tf_op jit(solution)/shard_map/ppermute | solution.py:664
  31.3 2.6 %cells.1 = (bf16[4,256,256]{2,1,0:T(8,128)(2,1)S(1)}, bf16[4,256,256]{2,1,0:T(8,128)(2,1)S(1)}, f32[4,256,256]{2,1,0:T(8,128)S(1)}, f32[4,1024,256]{2,1,0:T(8,12...) custom-call(bf16[2048,128]{1,0:T(8,128)(2,1)S(1)} %bitcast.8, ...), custom_call_target="tpu_custom_call" | custom-call | bytes 9000000 | tf_op jit(solution)/shard_map/cells/pallas_call | solution.py:629
  34.5 1.6 %collective-permute-done.7.r2 = bf16[256,128]{1,0:T(8,128)(2,1)S(1)} collective-permute-done((bf16[256,128]{1,0:T(8,128)(2,1)S(1)}, bf16[256,128]{1,0:T(8,128)(2,1)S(1)}, u32[]{:S(2)}, u32[]{:S(2)}) %collective-permute-start.7) | collective-permute-done | bytes 65568 | tf_op jit(solution)/shard_map/ppermute | solution.py:664
  36.5 1.6 %collective-permute-start.9 = (bf16[256,128]{1,0:T(8,128)(2,1)S(1)}, bf16[256,128]{1,0:T(8,128)(2,1)S(1)}, u32[]{:S(2)}, u32[]{:S(2)}) collective-permute-start(bf16[256,128]{1,0:T(8,128)(2,1)S(1)} %get-tuple-element.84), channel_id=1, source_target_pairs={{0,2},{1,3},{2,0},{3,1},{4,6},{5,7},{6,4},{7,5},{8,10},{9,11},{10,... | collective-permute-start | bytes 196616 | tf_op jit(solution)/shard_map/ppermute | solution.py:664
  38.7 2.1 %collective-permute-done.9.r1 = bf16[256,128]{1,0:T(8,128)(2,1)S(1)} collective-permute-done((bf16[256,128]{1,0:T(8,128)(2,1)S(1)}, bf16[256,128]{1,0:T(8,128)(2,1)S(1)}, u32[]{:S(2)}, u32[]{:S(2)}) %collective-permute-start.9) | collective-permute-done | bytes 65568 | tf_op jit(solution)/shard_map/ppermute | solution.py:664
  40.8 1.4 %collective-permute-done.10.r2 = bf16[256,128]{1,0:T(8,128)(2,1)S(1)} collective-permute-done((bf16[256,128]{1,0:T(8,128)(2,1)S(1)}, bf16[256,128]{1,0:T(8,128)(2,1)S(1)}, u32[]{:S(2)}, u32[]{:S(2)}) %collective-permute-start.10) | collective-permute-done | bytes 65568 | tf_op jit(solution)/shard_map/ppermute | solution.py:664
  42.2 4.5 %point.1 = (bf16[256,128]{1,0:T(8,128)(2,1)S(1)}, bf16[256,128]{1,0:T(8,128)(2,1)S(1)}, bf16[256,128]{1,0:T(8,128)(2,1)S(1)}, bf16[256,128]{1,0:T(8,128)(2,1)S(1...) custom-call(bf16[256,128]{1,0:T(8,128)(2,1)S(1)} %get-tuple-element., ...), custom_call_target="tpu_custom_call" | custom-call | bytes 18000000 | tf_op jit(solution)/shard_map/point/pallas_call | solution.py:629
  49.0 1.9 %sums.1.after = f32[96,128]{1,0:T(8,128)S(1)} custom-call(bf16[4,256,256]{2,1,0:T(8,128)(2,1)S(1)} %get-tuple-element.82.after.fx, bf16[4,256,256]{2,1,0:T(8,128)(2,1)S(1)} %get-tuple-element.89.cx, bf16[4,256,256]{2,1,0:T(8,128)(2,1)S(1)} %get-tuple-element.99.pg, bf16[4,1024,256]{2,1,0:T(8,128)(2,1)S(1)} %get-tuple-element.100.act, ...), custom_call_target="tpu_custom_call" | custom-call | bytes 7500000 | tf_op jit(solution)/shard_map/sums/pallas_call | solution.py:629
  52.3 1.2 %collective-permute-start.15 = (bf16[256,128]{1,0:T(8,128)(2,1)S(1)}, bf16[256,128]{1,0:T(8,128)(2,1)S(1)}, u32[]{:S(2)}, u32[]{:S(2)}) collective-permute-start(bf16[256,128]{1,0:T(8,128)(2,1)S(1)} %get-tuple-element.104), channel_id=1, source_target_pairs={{0,8},{4,12},{8,0},{12,4},{1,9},{5,13},{9,1},{13,5},{2,10},{6,14},... | collective-permute-start | bytes 196616 | tf_op jit(solution)/shard_map/ppermute | solution.py:664
  53.5 1.2 %collective-permute-start.16 = (bf16[256,128]{1,0:T(8,128)(2,1)S(1)}, bf16[256,128]{1,0:T(8,128)(2,1)S(1)}, u32[]{:S(2)}, u32[]{:S(2)}) collective-permute-start(bf16[256,128]{1,0:T(8,128)(2,1)S(1)} %get-tuple-element.105), channel_id=1, source_target_pairs={{0,12},{4,8},{8,4},{12,0},{1,13},{5,9},{9,5},{13,1},{2,14},{6,10},... | collective-permute-start | bytes 196616 | tf_op jit(solution)/shard_map/ppermute | solution.py:664
  54.7 1.1 %collective-permute-start.17 = (bf16[256,128]{1,0:T(8,128)(2,1)S(1)}, bf16[256,128]{1,0:T(8,128)(2,1)S(1)}, u32[]{:S(2)}, u32[]{:S(2)}) collective-permute-start(bf16[256,128]{1,0:T(8,128)(2,1)S(1)} %get-tuple-element.106), channel_id=1, source_target_pairs={{0,4},{4,0},{8,12},{12,8},{1,5},{5,1},{9,13},{13,9},{2,6},{6,2},{1... | collective-permute-start | bytes 196616 | tf_op jit(solution)/shard_map/ppermute | solution.py:664
  55.8 1.2 %collective-permute-done.24 = f32[96,128]{1,0:T(8,128)S(1)} collective-permute-done((f32[96,128]{1,0:T(8,128)S(1)}, f32[96,128]{1,0:T(8,128)S(1)}, u32[]{:S(2)}, u32[]{:S(2)}) %collective-permute-start.24) | collective-permute-done | bytes 49184 | tf_op jit(solution)/shard_map/ppermute | solution.py:672
  57.1 1.3 %collective-permute-start.25 = (f32[96,128]{1,0:T(8,128)S(1)}, f32[96,128]{1,0:T(8,128)S(1)}, u32[]{:S(2)}, u32[]{:S(2)}) collective-permute-start(f32[96,128]{1,0:T(8,128)S(1)} %add.9), channel_id=1, source_target_pairs={{0,2},{2,0},{1,3},{3,1},{4,6},{6,4},{5,7},{7,5},{8,10},{10,8},{9,1... | collective-permute-start | bytes 147464 | tf_op jit(solution)/shard_map/ppermute | solution.py:672
  58.3 1.3 %collective-permute-done.15.r1 = bf16[256,128]{1,0:T(8,128)(2,1)S(1)} collective-permute-done((bf16[256,128]{1,0:T(8,128)(2,1)S(1)}, bf16[256,128]{1,0:T(8,128)(2,1)S(1)}, u32[]{:S(2)}, u32[]{:S(2)}) %collective-permute-start.15) | collective-permute-done | bytes 65568 | tf_op jit(solution)/shard_map/ppermute | solution.py:664
  60.1 1.2 %collective-permute-done.17.r3 = bf16[256,128]{1,0:T(8,128)(2,1)S(1)} collective-permute-done((bf16[256,128]{1,0:T(8,128)(2,1)S(1)}, bf16[256,128]{1,0:T(8,128)(2,1)S(1)}, u32[]{:S(2)}, u32[]{:S(2)}) %collective-permute-start.17) | collective-permute-done | bytes 65568 | tf_op jit(solution)/shard_map/ppermute | solution.py:664
  61.3 4.4 %mix_backward.1 = (bf16[32,2,64,128]{3,2,1,0:T(8,128)(2,1)S(1)}, bf16[256,128]{1,0:T(8,128)(2,1)S(1)}, bf16[256,128]{1,0:T(8,128)(2,1)S(1)}, bf16[256,128]{1,0:T(8,128)(2,1)S(1)}, bf16[256,128]{1,0:T(8,128)(2,1)S(1)}) custom-call(bf16[256,128]{1,0:T(8,128)(2,1)S(1)} %get-tuple-element.103.r0, bf16[256,128]{1,0:T(8,128)(2,1)S(1)} %collective-permute-done.15.r1, ...), custom_call_target="tpu_custom_call" | custom-call | bytes 15000000 | tf_op jit(solution)/shard_map/mix_backward/pallas_call | solution.py:629
  65.7 1.8 %collective-permute-start.18 = (bf16[256,128]{1,0:T(8,128)(2,1)S(1)}, bf16[256,128]{1,0:T(8,128)(2,1)S(1)}, u32[]{:S(2)}, u32[]{:S(2)}) collective-permute-start(bf16[256,128]{1,0:T(8,128)(2,1)S(1)} %get-tuple-element.109), channel_id=1, source_target_pairs={{0,8},{4,12},{8,0},{12,4},{1,9},{5,13},{9,1},{13,5},{2,10},{6,14},... | collective-permute-start | bytes 196616 | tf_op jit(solution)/shard_map/ppermute | solution.py:664
  67.5 1.2 %collective-permute-start.19 = (bf16[256,128]{1,0:T(8,128)(2,1)S(1)}, bf16[256,128]{1,0:T(8,128)(2,1)S(1)}, u32[]{:S(2)}, u32[]{:S(2)}) collective-permute-start(bf16[256,128]{1,0:T(8,128)(2,1)S(1)} %get-tuple-element.110), channel_id=1, source_target_pairs={{0,12},{4,8},{8,4},{12,0},{1,13},{5,9},{9,5},{13,1},{2,14},{6,10},... | collective-permute-start | bytes 196616 | tf_op jit(solution)/shard_map/ppermute | solution.py:664
  69.3 1.6 %collective-permute-start.26 = (f32[96,128]{1,0:T(8,128)S(1)}, f32[96,128]{1,0:T(8,128)S(1)}, u32[]{:S(2)}, u32[]{:S(2)}) collective-permute-start(f32[96,128]{1,0:T(8,128)S(1)} %add.10), channel_id=1, source_target_pairs={{0,4},{4,0},{8,12},{12,8},{1,5},{5,1},{9,13},{13,9},{2,6},{6,2},{1... | collective-permute-start | bytes 147464 | tf_op jit(solution)/shard_map/ppermute | solution.py:672
  70.8 5.0 %outer.2 = (bf16[2,32,32,64,32]{4,3,2,1,0:T(8,128)(2,1)}, f32[8,128]{1,0:T(8,128)S(1)}) custom-call(bf16[8,2,64,128]{3,2,1,0:T(8,128)(2,1)S(1)} %get-tuple-element.112.modes, bf16[32,2,64,128]{3,2,1,0:T(8,128)(2,1)S(1)} %get-tuple-element.113.pmodes), custom_call_target="tpu_custom_call" | custom-call | bytes 15000000 | tf_op jit(solution)/shard_map/outer/pallas_call | solution.py:629
  76.2 1.1 %collective-permute-start.21 = (bf16[256,128]{1,0:T(8,128)(2,1)S(1)}, bf16[256,128]{1,0:T(8,128)(2,1)S(1)}, u32[]{:S(2)}, u32[]{:S(2)}) collective-permute-start(bf16[256,128]{1,0:T(8,128)(2,1)S(1)} %get-tuple-element.116), channel_id=1, source_target_pairs={{0,2},{1,3},{2,0},{3,1},{4,6},{5,7},{6,4},{7,5},{8,10},{9,11},{10,... | collective-permute-start | bytes 196616 | tf_op jit(solution)/shard_map/ppermute | solution.py:664
  77.2 1.1 %collective-permute-start.23 = (bf16[256,128]{1,0:T(8,128)(2,1)S(1)}, bf16[256,128]{1,0:T(8,128)(2,1)S(1)}, u32[]{:S(2)}, u32[]{:S(2)}) collective-permute-start(bf16[256,128]{1,0:T(8,128)(2,1)S(1)} %get-tuple-element.118), channel_id=1, source_target_pairs={{0,1},{1,0},{2,3},{3,2},{4,5},{5,4},{6,7},{7,6},{8,9},{9,8},{10,11... | collective-permute-start | bytes 196616 | tf_op jit(solution)/shard_map/ppermute | solution.py:664
  78.4 1.5 %collective-permute-start.27 = (f32[96,128]{1,0:T(8,128)S(1)}, f32[96,128]{1,0:T(8,128)S(1)}, u32[]{:S(2)}, u32[]{:S(2)}) collective-permute-start(f32[96,128]{1,0:T(8,128)S(1)} %add.11.part), channel_id=1, source_target_pairs={{0,8},{4,12},{8,0},{12,4},{1,9},{5,13},{9,1},{13,5},{2,10},{6,14},... | collective-permute-start | bytes 147464 | tf_op jit(solution)/shard_map/ppermute | solution.py:672
  79.8 4.3 %outer.3 = (bf16[2,32,32,64,32]{4,3,2,1,0:T(8,128)(2,1)}, f32[8,128]{1,0:T(8,128)}) custom-call(bf16[8,2,64,128]{3,2,1,0:T(8,128)(2,1)S(1)} %get-tuple-element.112.modes, bf16[32,2,64,128]{3,2,1,0:T(8,128)(2,1)S(1)} %get-tuple-element.113.pmodes, bf16[256,128]{1,0:T(8,128)(2,1)S(1)} %get-tuple-element.115.rest_0_.r0, ...), custom_call_target="tpu_custom_call", output_to_operand_aliasing={{0}: (3, {})} | custom-call | bytes 12000000 | tf_op jit(solution)/shard_map/outer/pallas_call | solution.py:629
  84.2 5.8 %finish.1 = (bf16[2048,128]{1,0:T(8,128)(2,1)}, f32[32,128]{1,0:T(8,128)}, f32[32,128]{1,0:T(8,128)}, f32[32,32]{1,0:T(8,128)}, bf16[2,32,32,64,32]{4,3,2,1,0:T(8,128)(2,1)}) custom-call(bf16[256,128]{1,0:T(8,128)(2,1)S(1)} %get-tuple-element.115.rest_0_.r0, bf16[256,128]{1,0:T(8,128)(2,1)S(1)} %collective-permute-done.21.r1, ...), custom_call_target="tpu_custom_call", output_to_operand_aliasing={{4}: (11, {})} | custom-call | bytes 12000000 | tf_op jit(solution)/shard_map/finish/pallas_call | solution.py:629
  (70 shorter events, 9.4 us)
Async XLA Ops:
  2.5 7.0 %collective-permute-start = (bf16[256,128]{1,0:T(8,128)(2,1)S(1)}, bf16[256,128]{1,0:T(8,128)(2,1)S(1)}, u32[]{:S(2)}, u32[]{:S(2)}) collective-permute-start(bf16[256,128]{1,0:T(8,128)(2,1)S(1)} %get-tuple-element.67), channel_id=1, source_target_pairs={{0,2},{1,3},{2,0},{3,1},{4,6},{5,7},{6,4},{7,5},{8,10},{9,11},{10,... | collective-permute-start | bytes 196616 | tf_op jit(solution)/shard_map/ppermute | solution.py:664
  5.5 4.1 %collective-permute-start.1 = (bf16[256,128]{1,0:T(8,128)(2,1)S(1)}, bf16[256,128]{1,0:T(8,128)(2,1)S(1)}, u32[]{:S(2)}, u32[]{:S(2)}) collective-permute-start(bf16[256,128]{1,0:T(8,128)(2,1)S(1)} %get-tuple-element.68), channel_id=1, source_target_pairs={{0,3},{1,2},{2,1},{3,0},{4,7},{5,6},{6,5},{7,4},{8,11},{9,10},{10,... | collective-permute-start | bytes 196616 | tf_op jit(solution)/shard_map/ppermute | solution.py:664
  5.5 4.1 %collective-permute-start.2 = (bf16[256,128]{1,0:T(8,128)(2,1)S(1)}, bf16[256,128]{1,0:T(8,128)(2,1)S(1)}, u32[]{:S(2)}, u32[]{:S(2)}) collective-permute-start(bf16[256,128]{1,0:T(8,128)(2,1)S(1)} %get-tuple-element.69), channel_id=1, source_target_pairs={{0,1},{1,0},{2,3},{3,2},{4,5},{5,4},{6,7},{7,6},{8,9},{9,8},{10,11... | collective-permute-start | bytes 196616 | tf_op jit(solution)/shard_map/ppermute | solution.py:664
  10.0 10.1 %collective-permute-start.3 = (bf16[256,128]{1,0:T(8,128)(2,1)S(1)}, bf16[256,128]{1,0:T(8,128)(2,1)S(1)}, u32[]{:S(2)}, u32[]{:S(2)}) collective-permute-start(bf16[256,128]{1,0:T(8,128)(2,1)S(1)} %get-tuple-element.72), channel_id=1, source_target_pairs={{0,8},{4,12},{8,0},{12,4},{1,9},{5,13},{9,1},{13,5},{2,10},{6,14},... | collective-permute-start | bytes 196616 | tf_op jit(solution)/shard_map/ppermute | solution.py:664
  13.0 7.1 %collective-permute-start.4 = (bf16[256,128]{1,0:T(8,128)(2,1)S(1)}, bf16[256,128]{1,0:T(8,128)(2,1)S(1)}, u32[]{:S(2)}, u32[]{:S(2)}) collective-permute-start(bf16[256,128]{1,0:T(8,128)(2,1)S(1)} %get-tuple-element.73), channel_id=1, source_target_pairs={{0,12},{4,8},{8,4},{12,0},{1,13},{5,9},{9,5},{13,1},{2,14},{6,10},... | collective-permute-start | bytes 196616 | tf_op jit(solution)/shard_map/ppermute | solution.py:664
  14.3 5.8 %collective-permute-start.5 = (bf16[256,128]{1,0:T(8,128)(2,1)S(1)}, bf16[256,128]{1,0:T(8,128)(2,1)S(1)}, u32[]{:S(2)}, u32[]{:S(2)}) collective-permute-start(bf16[256,128]{1,0:T(8,128)(2,1)S(1)} %get-tuple-element.74), channel_id=1, source_target_pairs={{0,4},{4,0},{8,12},{12,8},{1,5},{5,1},{9,13},{13,9},{2,6},{6,2},{1... | collective-permute-start | bytes 196616 | tf_op jit(solution)/shard_map/ppermute | solution.py:664
  20.1 11.1 %copy-start.1 = (bf16[32,8,8,128]{3,2,1,0:T(8,128)(2,1)S(1)}, bf16[32,8,8,128]{3,2,1,0:T(8,128)(2,1)}, u32[]{:S(2)}) copy-start(bf16[32,8,8,128]{3,2,1,0:T(8,128)(2,1)} %param.14) | copy-start | bytes 1572868
  20.1 11.1 %copy-start.3 = (bf16[4,128,1024]{2,1,0:T(8,128)(2,1)S(1)}, bf16[4,128,1024]{2,1,0:T(8,128)(2,1)}, u32[]{:S(2)}) copy-start(bf16[4,128,1024]{2,1,0:T(8,128)(2,1)} %constant.17.clone.zi) | copy-start | bytes 3145732
  27.0 7.5 %collective-permute-start.6 = (bf16[256,128]{1,0:T(8,128)(2,1)S(1)}, bf16[256,128]{1,0:T(8,128)(2,1)S(1)}, u32[]{:S(2)}, u32[]{:S(2)}) collective-permute-start(bf16[256,128]{1,0:T(8,128)(2,1)S(1)} %get-tuple-element.78), channel_id=1, source_target_pairs={{0,8},{4,12},{8,0},{12,4},{1,9},{5,13},{9,1},{13,5},{2,10},{6,14},... | collective-permute-start | bytes 196616 | tf_op jit(solution)/shard_map/ppermute | solution.py:664
  29.9 6.2 %collective-permute-start.7 = (bf16[256,128]{1,0:T(8,128)(2,1)S(1)}, bf16[256,128]{1,0:T(8,128)(2,1)S(1)}, u32[]{:S(2)}, u32[]{:S(2)}) collective-permute-start(bf16[256,128]{1,0:T(8,128)(2,1)S(1)} %get-tuple-element.79), channel_id=1, source_target_pairs={{0,12},{4,8},{8,4},{12,0},{1,13},{5,9},{9,5},{13,1},{2,14},{6,10},... | collective-permute-start | bytes 196616 | tf_op jit(solution)/shard_map/ppermute | solution.py:664
  31.2 5.0 %collective-permute-start.8 = (bf16[256,128]{1,0:T(8,128)(2,1)S(1)}, bf16[256,128]{1,0:T(8,128)(2,1)S(1)}, u32[]{:S(2)}, u32[]{:S(2)}) collective-permute-start(bf16[256,128]{1,0:T(8,128)(2,1)S(1)} %get-tuple-element.80), channel_id=1, source_target_pairs={{0,4},{4,0},{8,12},{12,8},{1,5},{5,1},{9,13},{13,9},{2,6},{6,2},{1... | collective-permute-start | bytes 196616 | tf_op jit(solution)/shard_map/ppermute | solution.py:664
  36.5 4.3 %collective-permute-start.9 = (bf16[256,128]{1,0:T(8,128)(2,1)S(1)}, bf16[256,128]{1,0:T(8,128)(2,1)S(1)}, u32[]{:S(2)}, u32[]{:S(2)}) collective-permute-start(bf16[256,128]{1,0:T(8,128)(2,1)S(1)} %get-tuple-element.84), channel_id=1, source_target_pairs={{0,2},{1,3},{2,0},{3,1},{4,6},{5,7},{6,4},{7,5},{8,10},{9,11},{10,... | collective-permute-start | bytes 196616 | tf_op jit(solution)/shard_map/ppermute | solution.py:664
  38.0 4.2 %collective-permute-start.10 = (bf16[256,128]{1,0:T(8,128)(2,1)S(1)}, bf16[256,128]{1,0:T(8,128)(2,1)S(1)}, u32[]{:S(2)}, u32[]{:S(2)}) collective-permute-start(bf16[256,128]{1,0:T(8,128)(2,1)S(1)} %get-tuple-element.85), channel_id=1, source_target_pairs={{0,3},{1,2},{2,1},{3,0},{4,7},{5,6},{6,5},{7,4},{8,11},{9,10},{10,... | collective-permute-start | bytes 196616 | tf_op jit(solution)/shard_map/ppermute | solution.py:664
  38.0 4.2 %collective-permute-start.11 = (bf16[256,128]{1,0:T(8,128)(2,1)S(1)}, bf16[256,128]{1,0:T(8,128)(2,1)S(1)}, u32[]{:S(2)}, u32[]{:S(2)}) collective-permute-start(bf16[256,128]{1,0:T(8,128)(2,1)S(1)} %get-tuple-element.86), channel_id=1, source_target_pairs={{0,1},{1,0},{2,3},{3,2},{4,5},{5,4},{6,7},{7,6},{8,9},{9,8},{10,11... | collective-permute-start | bytes 196616 | tf_op jit(solution)/shard_map/ppermute | solution.py:664
  46.7 14.5 %copy-start.5 = (bf16[4,2,32,1024]{3,2,1,0:T(8,128)(2,1)S(1)}, bf16[4,2,32,1024]{3,2,1,0:T(8,128)(2,1)}, u32[]{:S(2)}) copy-start(bf16[4,2,32,1024]{3,2,1,0:T(8,128)(2,1)} %constant.21.clone.xr) | copy-start | bytes 1572868
  46.7 14.5 %copy-start.9 = (bf16[4,32,256]{2,1,0:T(8,128)(2,1)S(1)}, bf16[4,32,256]{2,1,0:T(8,128)(2,1)}, u32[]{:S(2)}) copy-start(bf16[4,32,256]{2,1,0:T(8,128)(2,1)} %constant.23.clone.xd) | copy-start | bytes 196612
  46.7 4.9 %collective-permute-start.12 = (bf16[256,128]{1,0:T(8,128)(2,1)S(1)}, bf16[256,128]{1,0:T(8,128)(2,1)S(1)}, u32[]{:S(2)}, u32[]{:S(2)}) collective-permute-start(bf16[256,128]{1,0:T(8,128)(2,1)S(1)} %get-tuple-element.95), channel_id=1, source_target_pairs={{0,2},{1,3},{2,0},{3,1},{4,6},{5,7},{6,4},{7,5},{8,10},{9,11},{10,... | collective-permute-start | bytes 196616 | tf_op jit(solution)/shard_map/ppermute | solution.py:664
  47.6 4.4 %collective-permute-start.13 = (bf16[256,128]{1,0:T(8,128)(2,1)S(1)}, bf16[256,128]{1,0:T(8,128)(2,1)S(1)}, u32[]{:S(2)}, u32[]{:S(2)}) collective-permute-start(bf16[256,128]{1,0:T(8,128)(2,1)S(1)} %get-tuple-element.96), channel_id=1, source_target_pairs={{0,3},{1,2},{2,1},{3,0},{4,7},{5,6},{6,5},{7,4},{8,11},{9,10},{10,... | collective-permute-start | bytes 196616 | tf_op jit(solution)/shard_map/ppermute | solution.py:664
  48.1 3.9 %collective-permute-start.14 = (bf16[256,128]{1,0:T(8,128)(2,1)S(1)}, bf16[256,128]{1,0:T(8,128)(2,1)S(1)}, u32[]{:S(2)}, u32[]{:S(2)}) collective-permute-start(bf16[256,128]{1,0:T(8,128)(2,1)S(1)} %get-tuple-element.97), channel_id=1, source_target_pairs={{0,1},{1,0},{2,3},{3,2},{4,5},{5,4},{6,7},{7,6},{8,9},{9,8},{10,11... | collective-permute-start | bytes 196616 | tf_op jit(solution)/shard_map/ppermute | solution.py:664
  52.3 7.4 %collective-permute-start.15 = (bf16[256,128]{1,0:T(8,128)(2,1)S(1)}, bf16[256,128]{1,0:T(8,128)(2,1)S(1)}, u32[]{:S(2)}, u32[]{:S(2)}) collective-permute-start(bf16[256,128]{1,0:T(8,128)(2,1)S(1)} %get-tuple-element.104), channel_id=1, source_target_pairs={{0,8},{4,12},{8,0},{12,4},{1,9},{5,13},{9,1},{13,5},{2,10},{6,14},... | collective-permute-start | bytes 196616 | tf_op jit(solution)/shard_map/ppermute | solution.py:664
  53.5 6.6 %collective-permute-start.16 = (bf16[256,128]{1,0:T(8,128)(2,1)S(1)}, bf16[256,128]{1,0:T(8,128)(2,1)S(1)}, u32[]{:S(2)}, u32[]{:S(2)}) collective-permute-start(bf16[256,128]{1,0:T(8,128)(2,1)S(1)} %get-tuple-element.105), channel_id=1, source_target_pairs={{0,12},{4,8},{8,4},{12,0},{1,13},{5,9},{9,5},{13,1},{2,14},{6,10},... | collective-permute-start | bytes 196616 | tf_op jit(solution)/shard_map/ppermute | solution.py:664
  54.7 6.5 %collective-permute-start.17 = (bf16[256,128]{1,0:T(8,128)(2,1)S(1)}, bf16[256,128]{1,0:T(8,128)(2,1)S(1)}, u32[]{:S(2)}, u32[]{:S(2)}) collective-permute-start(bf16[256,128]{1,0:T(8,128)(2,1)S(1)} %get-tuple-element.106), channel_id=1, source_target_pairs={{0,4},{4,0},{8,12},{12,8},{1,5},{5,1},{9,13},{13,9},{2,6},{6,2},{1... | collective-permute-start | bytes 196616 | tf_op jit(solution)/shard_map/ppermute | solution.py:664
  55.8 1.2 %collective-permute-start.24 = (f32[96,128]{1,0:T(8,128)S(1)}, f32[96,128]{1,0:T(8,128)S(1)}, u32[]{:S(2)}, u32[]{:S(2)}) collective-permute-start(f32[96,128]{1,0:T(8,128)S(1)} %sums.1.after), channel_id=1, source_target_pairs={{0,1},{1,0},{2,3},{3,2},{4,5},{5,4},{6,7},{7,6},{8,9},{9,8},{10,11... | collective-permute-start | bytes 147464 | tf_op jit(solution)/shard_map/ppermute | solution.py:672
  57.1 12.2 %collective-permute-start.25 = (f32[96,128]{1,0:T(8,128)S(1)}, f32[96,128]{1,0:T(8,128)S(1)}, u32[]{:S(2)}, u32[]{:S(2)}) collective-permute-start(f32[96,128]{1,0:T(8,128)S(1)} %add.9), channel_id=1, source_target_pairs={{0,2},{2,0},{1,3},{3,1},{4,6},{6,4},{5,7},{7,5},{8,10},{10,8},{9,1... | collective-permute-start | bytes 147464 | tf_op jit(solution)/shard_map/ppermute | solution.py:672
  65.7 10.1 %collective-permute-start.18 = (bf16[256,128]{1,0:T(8,128)(2,1)S(1)}, bf16[256,128]{1,0:T(8,128)(2,1)S(1)}, u32[]{:S(2)}, u32[]{:S(2)}) collective-permute-start(bf16[256,128]{1,0:T(8,128)(2,1)S(1)} %get-tuple-element.109), channel_id=1, source_target_pairs={{0,8},{4,12},{8,0},{12,4},{1,9},{5,13},{9,1},{13,5},{2,10},{6,14},... | collective-permute-start | bytes 196616 | tf_op jit(solution)/shard_map/ppermute | solution.py:664
  67.5 8.3 %collective-permute-start.19 = (bf16[256,128]{1,0:T(8,128)(2,1)S(1)}, bf16[256,128]{1,0:T(8,128)(2,1)S(1)}, u32[]{:S(2)}, u32[]{:S(2)}) collective-permute-start(bf16[256,128]{1,0:T(8,128)(2,1)S(1)} %get-tuple-element.110), channel_id=1, source_target_pairs={{0,12},{4,8},{8,4},{12,0},{1,13},{5,9},{9,5},{13,1},{2,14},{6,10},... | collective-permute-start | bytes 196616 | tf_op jit(solution)/shard_map/ppermute | solution.py:664
  68.7 7.1 %collective-permute-start.20 = (bf16[256,128]{1,0:T(8,128)(2,1)S(1)}, bf16[256,128]{1,0:T(8,128)(2,1)S(1)}, u32[]{:S(2)}, u32[]{:S(2)}) collective-permute-start(bf16[256,128]{1,0:T(8,128)(2,1)S(1)} %get-tuple-element.111), channel_id=1, source_target_pairs={{0,4},{4,0},{8,12},{12,8},{1,5},{5,1},{9,13},{13,9},{2,6},{6,2},{1... | collective-permute-start | bytes 196616 | tf_op jit(solution)/shard_map/ppermute | solution.py:664
  69.3 9.1 %collective-permute-start.26 = (f32[96,128]{1,0:T(8,128)S(1)}, f32[96,128]{1,0:T(8,128)S(1)}, u32[]{:S(2)}, u32[]{:S(2)}) collective-permute-start(f32[96,128]{1,0:T(8,128)S(1)} %add.10), channel_id=1, source_target_pairs={{0,4},{4,0},{8,12},{12,8},{1,5},{5,1},{9,13},{13,9},{2,6},{6,2},{1... | collective-permute-start | bytes 147464 | tf_op jit(solution)/shard_map/ppermute | solution.py:672
  76.2 8.0 %collective-permute-start.21 = (bf16[256,128]{1,0:T(8,128)(2,1)S(1)}, bf16[256,128]{1,0:T(8,128)(2,1)S(1)}, u32[]{:S(2)}, u32[]{:S(2)}) collective-permute-start(bf16[256,128]{1,0:T(8,128)(2,1)S(1)} %get-tuple-element.116), channel_id=1, source_target_pairs={{0,2},{1,3},{2,0},{3,1},{4,6},{5,7},{6,4},{7,5},{8,10},{9,11},{10,... | collective-permute-start | bytes 196616 | tf_op jit(solution)/shard_map/ppermute | solution.py:664
  77.2 6.9 %collective-permute-start.22 = (bf16[256,128]{1,0:T(8,128)(2,1)S(1)}, bf16[256,128]{1,0:T(8,128)(2,1)S(1)}, u32[]{:S(2)}, u32[]{:S(2)}) collective-permute-start(bf16[256,128]{1,0:T(8,128)(2,1)S(1)} %get-tuple-element.117), channel_id=1, source_target_pairs={{0,3},{1,2},{2,1},{3,0},{4,7},{5,6},{6,5},{7,4},{8,11},{9,10},{10,... | collective-permute-start | bytes 196616 | tf_op jit(solution)/shard_map/ppermute | solution.py:664
  77.2 6.9 %collective-permute-start.23 = (bf16[256,128]{1,0:T(8,128)(2,1)S(1)}, bf16[256,128]{1,0:T(8,128)(2,1)S(1)}, u32[]{:S(2)}, u32[]{:S(2)}) collective-permute-start(bf16[256,128]{1,0:T(8,128)(2,1)S(1)} %get-tuple-element.118), channel_id=1, source_target_pairs={{0,1},{1,0},{2,3},{3,2},{4,5},{5,4},{6,7},{7,6},{8,9},{9,8},{10,11... | collective-permute-start | bytes 196616 | tf_op jit(solution)/shard_map/ppermute | solution.py:664
  78.4 5.7 %collective-permute-start.27 = (f32[96,128]{1,0:T(8,128)S(1)}, f32[96,128]{1,0:T(8,128)S(1)}, u32[]{:S(2)}, u32[]{:S(2)}) collective-permute-start(f32[96,128]{1,0:T(8,128)S(1)} %add.11.part), channel_id=1, source_target_pairs={{0,8},{4,12},{8,0},{12,4},{1,9},{5,13},{9,1},{13,5},{2,10},{6,14},... | collective-permute-start | bytes 147464 | tf_op jit(solution)/shard_map/ppermute | solution.py:672
  (10 other events, 82.5 us)

commit v5 on v4

--- a/solution.py
+++ b/solution.py
@@ -234,7 +234,7 @@
 
 
 def z_forward_kernel(rows, yrows, field, o0, o1, o2, o3, wide):
-    wide[...] = field[...].astype(F32)
+    wide[: field.shape[0]] = field[...].astype(F32)
     side = jnp.concatenate(
         [wide[pl.ds(y, rows, stride=yrows), :].astype(BF) for y in range(yrows)], axis=1
     )
@@ -480,7 +480,7 @@
 ):
     idx = place()
     for src, dst in ((field, fx), (cotangent, cx)):
-        wide[...] = src[...].astype(F32)
+        wide[: src.shape[0]] = src[...].astype(F32)
 
         def step(k, carry):
             parts = []
@@ -513,8 +513,8 @@
     side = jnp.concatenate([r[...] for r in refs], axis=1)
     for y in range(4):
         got = dot(side, back[:, y * 256 : (y + 1) * 256])
-        spectral[2 * y] = got[:, :128]
-        spectral[2 * y + 1] = got[:, 128:]
+        spectral[2 * y, : got.shape[0]] = got[:, :128]
+        spectral[2 * y + 1, : got.shape[0]] = got[:, 128:]
 
 
 def cell_rows(spectral, k):
@@ -559,7 +559,7 @@
         return carry
 
     lax.fori_loop(0, 4, step, 0, unroll=4)
-    side = jnp.concatenate([wide[y].astype(BF) for y in range(8)], axis=1)
+    side = jnp.concatenate([wide[y, :256].astype(BF) for y in range(8)], axis=1)
     out = dot(side, table[...]).astype(BF)
     for s, o in enumerate((o0, o1, o2, o3)):
         o[...] = out[:, s * 128 : (s + 1) * 128]
@@ -605,7 +605,7 @@
         return carry
 
     lax.fori_loop(0, 4, step, 0, unroll=4)
-    out[...] = wide[...].astype(BF)
+    out[...] = wide[: out.shape[0]].astype(BF)
     for copy in copies:
         copy.wait()
 
@@ -682,8 +682,8 @@
     flat_field = field.reshape(cells, zlen)
     flat_cot = cotangent.reshape(cells, zlen)
     rows = chans * xrows
-    wide = pltpu.VMEM((cells, zlen), F32)
-    tall = pltpu.VMEM((yrows, rows, zlen), F32)
+    wide = pltpu.VMEM((cells + 64, zlen), F32)
+    tall = pltpu.VMEM((yrows, rows + 8, zlen), F32)
     weight = mode_weight.reshape(2, chans, chans, 64, 32)
     lift_t = lift_weight.T
 

time: 90.3 us -> 90.3 us (level)
  no operation moved by 1% of the time
where the time goes in v5:
time: 90.3 us; the launch traced here: 90.2 us
  Pallas kernels  46.5 us (51%)
  starting transfers between devices  30.1 us (33%)
  waiting for transfers between devices  11.3 us (13%)
  between operations  1.19 us (1%)
  local copies, waits for them, and re-layouts  1.11 us (1%)
    pallas_call x13, Pallas kernels, call(): pl.pallas_call(kernel, out_shape=outs, in_specs=[VM] * (len(ins) - free)...  37.2 us
    ppermute x24, starting transfers between devices, exchange(): lax.ppermute(block, axes, [(a, a ^ step) for a in range(4)])  25.7 us
    ppermute x24, waiting for transfers between devices, exchange(): lax.ppermute(block, axes, [(a, a ^ step) for a in range(4)])  10.1 us
    pallas_call x2, Pallas kernels, pack(): pl.pallas_call(functools.partial(pack_kernel, first), out_shape=[jax.Shap...  9.27 us
    ppermute x4, starting transfers between devices, swap(): return lax.ppermute(part, axis, [(a, a ^ step) for a in range(size)])  4.35 us
  transfers between devices with their start and end apart: 28, of which 12 were waited for; matrix products, arithmetic and copies ran while one was open for 0% of the time, Pallas kernels for 31%

profile of v5, /device:TPU:0, one launch (start us, length us, event | category | flops | bytes accessed | tf_op | source)
XLA Modules:
  0.0 90.2 jit_solution(4907334725276886599)
XLA Ops:
  2.5 3.0 %collective-permute-start = (bf16[256,128]{1,0:T(8,128)(2,1)S(1)}, bf16[256,128]{1,0:T(8,128)(2,1)S(1)}, u32[]{:S(2)}, u32[]{:S(2)}) collective-permute-start(bf16[256,128]{1,0:T(8,128)(2,1)S(1)} %get-tuple-element.67), channel_id=1, source_target_pairs={{0,2},{1,3},{2,0},{3,1},{4,6},{5,7},{6,4},{7,5},{8,10},{9,11},{10,... | collective-permute-start | bytes 196616 | tf_op jit(solution)/shard_map/ppermute | solution.py:664
  5.7 3.8 %pack.2 = (bf16[2,2,32,64,128]{4,3,2,1,0:T(8,128)(2,1)S(1)}, f32[8,128]{1,0:T(8,128)S(1)}) custom-call(bf16[2,32,32,64,32]{4,3,2,1,0:T(8,128)(2,1)} %bitcast.11, bf16[256,128]{1,0:T(8,128)(2,1)S(1)} %get-tuple-element.66.after.r0), custom_call_target="tpu_custom_call" | custom-call | bytes 9000000 | tf_op jit(solution)/shard_map/pack/pallas_call | solution.py:647
  10.0 3.0 %collective-permute-start.3 = (bf16[256,128]{1,0:T(8,128)(2,1)S(1)}, bf16[256,128]{1,0:T(8,128)(2,1)S(1)}, u32[]{:S(2)}, u32[]{:S(2)}) collective-permute-start(bf16[256,128]{1,0:T(8,128)(2,1)S(1)} %get-tuple-element.72), channel_id=1, source_target_pairs={{0,8},{4,12},{8,0},{12,4},{1,9},{5,13},{9,1},{13,5},{2,10},{6,14},... | collective-permute-start | bytes 196616 | tf_op jit(solution)/shard_map/ppermute | solution.py:664
  13.0 1.4 %collective-permute-start.4 = (bf16[256,128]{1,0:T(8,128)(2,1)S(1)}, bf16[256,128]{1,0:T(8,128)(2,1)S(1)}, u32[]{:S(2)}, u32[]{:S(2)}) collective-permute-start(bf16[256,128]{1,0:T(8,128)(2,1)S(1)} %get-tuple-element.73), channel_id=1, source_target_pairs={{0,12},{4,8},{8,4},{12,0},{1,13},{5,9},{9,5},{13,1},{2,14},{6,10},... | collective-permute-start | bytes 196616 | tf_op jit(solution)/shard_map/ppermute | solution.py:664
  14.6 5.5 %pack.3 = (bf16[3,2,32,64,128]{4,3,2,1,0:T(8,128)(2,1)S(1)}, f32[8,128]{1,0:T(8,128)}) custom-call(bf16[2,32,32,64,32]{4,3,2,1,0:T(8,128)(2,1)} %bitcast.12, bf16[256,128]{1,0:T(8,128)(2,1)S(1)} %get-tuple-element.71.after.r0), custom_call_target="tpu_custom_call" | custom-call | bytes 15000000 | tf_op jit(solution)/shard_map/pack/pallas_call | solution.py:647
  20.2 6.8 %mix_forward.1 = (bf16[8,2,64,128]{3,2,1,0:T(8,128)(2,1)S(1)}, bf16[256,128]{1,0:T(8,128)(2,1)S(1)}, bf16[256,128]{1,0:T(8,128)(2,1)S(1)}, bf16[256,128]{1,0:T(8...) custom-call(bf16[256,128]{1,0:T(8,128)(2,1)S(1)} %get-tuple-element.71.after.r0, ...), custom_call_target="tpu_custom_call" | custom-call | bytes 24000000 | tf_op jit(solution)/shard_map/mix_forward/pallas_call | solution.py:629
  27.0 2.9 %collective-permute-start.6 = (bf16[256,128]{1,0:T(8,128)(2,1)S(1)}, bf16[256,128]{1,0:T(8,128)(2,1)S(1)}, u32[]{:S(2)}, u32[]{:S(2)}) collective-permute-start(bf16[256,128]{1,0:T(8,128)(2,1)S(1)} %get-tuple-element.78), channel_id=1, source_target_pairs={{0,8},{4,12},{8,0},{12,4},{1,9},{5,13},{9,1},{13,5},{2,10},{6,14},... | collective-permute-start | bytes 196616 | tf_op jit(solution)/shard_map/ppermute | solution.py:664
  29.9 1.4 %collective-permute-start.7 = (bf16[256,128]{1,0:T(8,128)(2,1)S(1)}, bf16[256,128]{1,0:T(8,128)(2,1)S(1)}, u32[]{:S(2)}, u32[]{:S(2)}) collective-permute-start(bf16[256,128]{1,0:T(8,128)(2,1)S(1)} %get-tuple-element.79), channel_id=1, source_target_pairs={{0,12},{4,8},{8,4},{12,0},{1,13},{5,9},{9,5},{13,1},{2,14},{6,10},... | collective-permute-start | bytes 196616 | tf_op jit(solution)/shard_map/ppermute | solution.py:664
  31.3 2.6 %cells.1 = (bf16[4,256,256]{2,1,0:T(8,128)(2,1)S(1)}, bf16[4,256,256]{2,1,0:T(8,128)(2,1)S(1)}, f32[4,256,256]{2,1,0:T(8,128)S(1)}, f32[4,1024,256]{2,1,0:T(8,12...) custom-call(bf16[2048,128]{1,0:T(8,128)(2,1)S(1)} %bitcast.8, ...), custom_call_target="tpu_custom_call" | custom-call | bytes 9000000 | tf_op jit(solution)/shard_map/cells/pallas_call | solution.py:629
  34.5 1.6 %collective-permute-done.7.r2 = bf16[256,128]{1,0:T(8,128)(2,1)S(1)} collective-permute-done((bf16[256,128]{1,0:T(8,128)(2,1)S(1)}, bf16[256,128]{1,0:T(8,128)(2,1)S(1)}, u32[]{:S(2)}, u32[]{:S(2)}) %collective-permute-start.7) | collective-permute-done | bytes 65568 | tf_op jit(solution)/shard_map/ppermute | solution.py:664
  36.5 1.6 %collective-permute-start.9 = (bf16[256,128]{1,0:T(8,128)(2,1)S(1)}, bf16[256,128]{1,0:T(8,128)(2,1)S(1)}, u32[]{:S(2)}, u32[]{:S(2)}) collective-permute-start(bf16[256,128]{1,0:T(8,128)(2,1)S(1)} %get-tuple-element.84), channel_id=1, source_target_pairs={{0,2},{1,3},{2,0},{3,1},{4,6},{5,7},{6,4},{7,5},{8,10},{9,11},{10,... | collective-permute-start | bytes 196616 | tf_op jit(solution)/shard_map/ppermute | solution.py:664
  38.7 2.1 %collective-permute-done.9.r1 = bf16[256,128]{1,0:T(8,128)(2,1)S(1)} collective-permute-done((bf16[256,128]{1,0:T(8,128)(2,1)S(1)}, bf16[256,128]{1,0:T(8,128)(2,1)S(1)}, u32[]{:S(2)}, u32[]{:S(2)}) %collective-permute-start.9) | collective-permute-done | bytes 65568 | tf_op jit(solution)/shard_map/ppermute | solution.py:664
  40.8 1.4 %collective-permute-done.10.r2 = bf16[256,128]{1,0:T(8,128)(2,1)S(1)} collective-permute-done((bf16[256,128]{1,0:T(8,128)(2,1)S(1)}, bf16[256,128]{1,0:T(8,128)(2,1)S(1)}, u32[]{:S(2)}, u32[]{:S(2)}) %collective-permute-start.10) | collective-permute-done | bytes 65568 | tf_op jit(solution)/shard_map/ppermute | solution.py:664
  42.2 4.5 %point.1 = (bf16[256,128]{1,0:T(8,128)(2,1)S(1)}, bf16[256,128]{1,0:T(8,128)(2,1)S(1)}, bf16[256,128]{1,0:T(8,128)(2,1)S(1)}, bf16[256,128]{1,0:T(8,128)(2,1)S(1...) custom-call(bf16[256,128]{1,0:T(8,128)(2,1)S(1)} %get-tuple-element., ...), custom_call_target="tpu_custom_call" | custom-call | bytes 18000000 | tf_op jit(solution)/shard_map/point/pallas_call | solution.py:629
  49.0 1.9 %sums.1.after = f32[96,128]{1,0:T(8,128)S(1)} custom-call(bf16[4,256,256]{2,1,0:T(8,128)(2,1)S(1)} %get-tuple-element.82.after.fx, bf16[4,256,256]{2,1,0:T(8,128)(2,1)S(1)} %get-tuple-element.89.cx, bf16[4,256,256]{2,1,0:T(8,128)(2,1)S(1)} %get-tuple-element.99.pg, bf16[4,1024,256]{2,1,0:T(8,128)(2,1)S(1)} %get-tuple-element.100.act, ...), custom_call_target="tpu_custom_call" | custom-call | bytes 7500000 | tf_op jit(solution)/shard_map/sums/pallas_call | solution.py:629
  52.3 1.2 %collective-permute-start.15 = (bf16[256,128]{1,0:T(8,128)(2,1)S(1)}, bf16[256,128]{1,0:T(8,128)(2,1)S(1)}, u32[]{:S(2)}, u32[]{:S(2)}) collective-permute-start(bf16[256,128]{1,0:T(8,128)(2,1)S(1)} %get-tuple-element.104), channel_id=1, source_target_pairs={{0,8},{4,12},{8,0},{12,4},{1,9},{5,13},{9,1},{13,5},{2,10},{6,14},... | collective-permute-start | bytes 196616 | tf_op jit(solution)/shard_map/ppermute | solution.py:664
  53.5 1.2 %collective-permute-start.16 = (bf16[256,128]{1,0:T(8,128)(2,1)S(1)}, bf16[256,128]{1,0:T(8,128)(2,1)S(1)}, u32[]{:S(2)}, u32[]{:S(2)}) collective-permute-start(bf16[256,128]{1,0:T(8,128)(2,1)S(1)} %get-tuple-element.105), channel_id=1, source_target_pairs={{0,12},{4,8},{8,4},{12,0},{1,13},{5,9},{9,5},{13,1},{2,14},{6,10},... | collective-permute-start | bytes 196616 | tf_op jit(solution)/shard_map/ppermute | solution.py:664
  54.7 1.1 %collective-permute-start.17 = (bf16[256,128]{1,0:T(8,128)(2,1)S(1)}, bf16[256,128]{1,0:T(8,128)(2,1)S(1)}, u32[]{:S(2)}, u32[]{:S(2)}) collective-permute-start(bf16[256,128]{1,0:T(8,128)(2,1)S(1)} %get-tuple-element.106), channel_id=1, source_target_pairs={{0,4},{4,0},{8,12},{12,8},{1,5},{5,1},{9,13},{13,9},{2,6},{6,2},{1... | collective-permute-start | bytes 196616 | tf_op jit(solution)/shard_map/ppermute | solution.py:664
  55.8 1.2 %collective-permute-done.24 = f32[96,128]{1,0:T(8,128)S(1)} collective-permute-done((f32[96,128]{1,0:T(8,128)S(1)}, f32[96,128]{1,0:T(8,128)S(1)}, u32[]{:S(2)}, u32[]{:S(2)}) %collective-permute-start.24) | collective-permute-done | bytes 49184 | tf_op jit(solution)/shard_map/ppermute | solution.py:672
  57.1 1.3 %collective-permute-start.25 = (f32[96,128]{1,0:T(8,128)S(1)}, f32[96,128]{1,0:T(8,128)S(1)}, u32[]{:S(2)}, u32[]{:S(2)}) collective-permute-start(f32[96,128]{1,0:T(8,128)S(1)} %add.9), channel_id=1, source_target_pairs={{0,2},{2,0},{1,3},{3,1},{4,6},{6,4},{5,7},{7,5},{8,10},{10,8},{9,1... | collective-permute-start | bytes 147464 | tf_op jit(solution)/shard_map/ppermute | solution.py:672
  58.3 1.3 %collective-permute-done.15.r1 = bf16[256,128]{1,0:T(8,128)(2,1)S(1)} collective-permute-done((bf16[256,128]{1,0:T(8,128)(2,1)S(1)}, bf16[256,128]{1,0:T(8,128)(2,1)S(1)}, u32[]{:S(2)}, u32[]{:S(2)}) %collective-permute-start.15) | collective-permute-done | bytes 65568 | tf_op jit(solution)/shard_map/ppermute | solution.py:664
  60.1 1.2 %collective-permute-done.17.r3 = bf16[256,128]{1,0:T(8,128)(2,1)S(1)} collective-permute-done((bf16[256,128]{1,0:T(8,128)(2,1)S(1)}, bf16[256,128]{1,0:T(8,128)(2,1)S(1)}, u32[]{:S(2)}, u32[]{:S(2)}) %collective-permute-start.17) | collective-permute-done | bytes 65568 | tf_op jit(solution)/shard_map/ppermute | solution.py:664
  61.3 4.4 %mix_backward.1 = (bf16[32,2,64,128]{3,2,1,0:T(8,128)(2,1)S(1)}, bf16[256,128]{1,0:T(8,128)(2,1)S(1)}, bf16[256,128]{1,0:T(8,128)(2,1)S(1)}, bf16[256,128]{1,0:T(8,128)(2,1)S(1)}, bf16[256,128]{1,0:T(8,128)(2,1)S(1)}) custom-call(bf16[256,128]{1,0:T(8,128)(2,1)S(1)} %get-tuple-element.103.r0, bf16[256,128]{1,0:T(8,128)(2,1)S(1)} %collective-permute-done.15.r1, ...), custom_call_target="tpu_custom_call" | custom-call | bytes 15000000 | tf_op jit(solution)/shard_map/mix_backward/pallas_call | solution.py:629
  65.7 1.8 %collective-permute-start.18 = (bf16[256,128]{1,0:T(8,128)(2,1)S(1)}, bf16[256,128]{1,0:T(8,128)(2,1)S(1)}, u32[]{:S(2)}, u32[]{:S(2)}) collective-permute-start(bf16[256,128]{1,0:T(8,128)(2,1)S(1)} %get-tuple-element.109), channel_id=1, source_target_pairs={{0,8},{4,12},{8,0},{12,4},{1,9},{5,13},{9,1},{13,5},{2,10},{6,14},... | collective-permute-start | bytes 196616 | tf_op jit(solution)/shard_map/ppermute | solution.py:664
  67.5 1.2 %collective-permute-start.19 = (bf16[256,128]{1,0:T(8,128)(2,1)S(1)}, bf16[256,128]{1,0:T(8,128)(2,1)S(1)}, u32[]{:S(2)}, u32[]{:S(2)}) collective-permute-start(bf16[256,128]{1,0:T(8,128)(2,1)S(1)} %get-tuple-element.110), channel_id=1, source_target_pairs={{0,12},{4,8},{8,4},{12,0},{1,13},{5,9},{9,5},{13,1},{2,14},{6,10},... | collective-permute-start | bytes 196616 | tf_op jit(solution)/shard_map/ppermute | solution.py:664
  69.3 1.6 %collective-permute-start.26 = (f32[96,128]{1,0:T(8,128)S(1)}, f32[96,128]{1,0:T(8,128)S(1)}, u32[]{:S(2)}, u32[]{:S(2)}) collective-permute-start(f32[96,128]{1,0:T(8,128)S(1)} %add.10), channel_id=1, source_target_pairs={{0,4},{4,0},{8,12},{12,8},{1,5},{5,1},{9,13},{13,9},{2,6},{6,2},{1... | collective-permute-start | bytes 147464 | tf_op jit(solution)/shard_map/ppermute | solution.py:672
  70.8 5.0 %outer.2 = (bf16[2,32,32,64,32]{4,3,2,1,0:T(8,128)(2,1)}, f32[8,128]{1,0:T(8,128)S(1)}) custom-call(bf16[8,2,64,128]{3,2,1,0:T(8,128)(2,1)S(1)} %get-tuple-element.112.modes, bf16[32,2,64,128]{3,2,1,0:T(8,128)(2,1)S(1)} %get-tuple-element.113.pmodes), custom_call_target="tpu_custom_call" | custom-call | bytes 15000000 | tf_op jit(solution)/shard_map/outer/pallas_call | solution.py:629
  76.2 1.1 %collective-permute-start.21 = (bf16[256,128]{1,0:T(8,128)(2,1)S(1)}, bf16[256,128]{1,0:T(8,128)(2,1)S(1)}, u32[]{:S(2)}, u32[]{:S(2)}) collective-permute-start(bf16[256,128]{1,0:T(8,128)(2,1)S(1)} %get-tuple-element.116), channel_id=1, source_target_pairs={{0,2},{1,3},{2,0},{3,1},{4,6},{5,7},{6,4},{7,5},{8,10},{9,11},{10,... | collective-permute-start | bytes 196616 | tf_op jit(solution)/shard_map/ppermute | solution.py:664
  77.2 1.1 %collective-permute-start.23 = (bf16[256,128]{1,0:T(8,128)(2,1)S(1)}, bf16[256,128]{1,0:T(8,128)(2,1)S(1)}, u32[]{:S(2)}, u32[]{:S(2)}) collective-permute-start(bf16[256,128]{1,0:T(8,128)(2,1)S(1)} %get-tuple-element.118), channel_id=1, source_target_pairs={{0,1},{1,0},{2,3},{3,2},{4,5},{5,4},{6,7},{7,6},{8,9},{9,8},{10,11... | collective-permute-start | bytes 196616 | tf_op jit(solution)/shard_map/ppermute | solution.py:664
  78.4 1.5 %collective-permute-start.27 = (f32[96,128]{1,0:T(8,128)S(1)}, f32[96,128]{1,0:T(8,128)S(1)}, u32[]{:S(2)}, u32[]{:S(2)}) collective-permute-start(f32[96,128]{1,0:T(8,128)S(1)} %add.11.part), channel_id=1, source_target_pairs={{0,8},{4,12},{8,0},{12,4},{1,9},{5,13},{9,1},{13,5},{2,10},{6,14},... | collective-permute-start | bytes 147464 | tf_op jit(solution)/shard_map/ppermute | solution.py:672
  79.9 4.3 %outer.3 = (bf16[2,32,32,64,32]{4,3,2,1,0:T(8,128)(2,1)}, f32[8,128]{1,0:T(8,128)}) custom-call(bf16[8,2,64,128]{3,2,1,0:T(8,128)(2,1)S(1)} %get-tuple-element.112.modes, bf16[32,2,64,128]{3,2,1,0:T(8,128)(2,1)S(1)} %get-tuple-element.113.pmodes, bf16[256,128]{1,0:T(8,128)(2,1)S(1)} %get-tuple-element.115.rest_0_.r0, ...), custom_call_target="tpu_custom_call", output_to_operand_aliasing={{0}: (3, {})} | custom-call | bytes 12000000 | tf_op jit(solution)/shard_map/outer/pallas_call | solution.py:629
  84.2 5.8 %finish.1 = (bf16[2048,128]{1,0:T(8,128)(2,1)}, f32[32,128]{1,0:T(8,128)}, f32[32,128]{1,0:T(8,128)}, f32[32,32]{1,0:T(8,128)}, bf16[2,32,32,64,32]{4,3,2,1,0:T(8,128)(2,1)}) custom-call(bf16[256,128]{1,0:T(8,128)(2,1)S(1)} %get-tuple-element.115.rest_0_.r0, bf16[256,128]{1,0:T(8,128)(2,1)S(1)} %collective-permute-done.21.r1, ...), custom_call_target="tpu_custom_call", output_to_operand_aliasing={{4}: (11, {})} | custom-call | bytes 12000000 | tf_op jit(solution)/shard_map/finish/pallas_call | solution.py:629
  (70 shorter events, 9.4 us)
Async XLA Ops:
  2.5 7.0 %collective-permute-start = (bf16[256,128]{1,0:T(8,128)(2,1)S(1)}, bf16[256,128]{1,0:T(8,128)(2,1)S(1)}, u32[]{:S(2)}, u32[]{:S(2)}) collective-permute-start(bf16[256,128]{1,0:T(8,128)(2,1)S(1)} %get-tuple-element.67), channel_id=1, source_target_pairs={{0,2},{1,3},{2,0},{3,1},{4,6},{5,7},{6,4},{7,5},{8,10},{9,11},{10,... | collective-permute-start | bytes 196616 | tf_op jit(solution)/shard_map/ppermute | solution.py:664
  5.5 4.1 %collective-permute-start.1 = (bf16[256,128]{1,0:T(8,128)(2,1)S(1)}, bf16[256,128]{1,0:T(8,128)(2,1)S(1)}, u32[]{:S(2)}, u32[]{:S(2)}) collective-permute-start(bf16[256,128]{1,0:T(8,128)(2,1)S(1)} %get-tuple-element.68), channel_id=1, source_target_pairs={{0,3},{1,2},{2,1},{3,0},{4,7},{5,6},{6,5},{7,4},{8,11},{9,10},{10,... | collective-permute-start | bytes 196616 | tf_op jit(solution)/shard_map/ppermute | solution.py:664
  5.5 4.1 %collective-permute-start.2 = (bf16[256,128]{1,0:T(8,128)(2,1)S(1)}, bf16[256,128]{1,0:T(8,128)(2,1)S(1)}, u32[]{:S(2)}, u32[]{:S(2)}) collective-permute-start(bf16[256,128]{1,0:T(8,128)(2,1)S(1)} %get-tuple-element.69), channel_id=1, source_target_pairs={{0,1},{1,0},{2,3},{3,2},{4,5},{5,4},{6,7},{7,6},{8,9},{9,8},{10,11... | collective-permute-start | bytes 196616 | tf_op jit(solution)/shard_map/ppermute | solution.py:664
  10.0 10.1 %collective-permute-start.3 = (bf16[256,128]{1,0:T(8,128)(2,1)S(1)}, bf16[256,128]{1,0:T(8,128)(2,1)S(1)}, u32[]{:S(2)}, u32[]{:S(2)}) collective-permute-start(bf16[256,128]{1,0:T(8,128)(2,1)S(1)} %get-tuple-element.72), channel_id=1, source_target_pairs={{0,8},{4,12},{8,0},{12,4},{1,9},{5,13},{9,1},{13,5},{2,10},{6,14},... | collective-permute-start | bytes 196616 | tf_op jit(solution)/shard_map/ppermute | solution.py:664
  13.0 7.1 %collective-permute-start.4 = (bf16[256,128]{1,0:T(8,128)(2,1)S(1)}, bf16[256,128]{1,0:T(8,128)(2,1)S(1)}, u32[]{:S(2)}, u32[]{:S(2)}) collective-permute-start(bf16[256,128]{1,0:T(8,128)(2,1)S(1)} %get-tuple-element.73), channel_id=1, source_target_pairs={{0,12},{4,8},{8,4},{12,0},{1,13},{5,9},{9,5},{13,1},{2,14},{6,10},... | collective-permute-start | bytes 196616 | tf_op jit(solution)/shard_map/ppermute | solution.py:664
  14.3 5.8 %collective-permute-start.5 = (bf16[256,128]{1,0:T(8,128)(2,1)S(1)}, bf16[256,128]{1,0:T(8,128)(2,1)S(1)}, u32[]{:S(2)}, u32[]{:S(2)}) collective-permute-start(bf16[256,128]{1,0:T(8,128)(2,1)S(1)} %get-tuple-element.74), channel_id=1, source_target_pairs={{0,4},{4,0},{8,12},{12,8},{1,5},{5,1},{9,13},{13,9},{2,6},{6,2},{1... | collective-permute-start | bytes 196616 | tf_op jit(solution)/shard_map/ppermute | solution.py:664
  20.1 11.1 %copy-start.1 = (bf16[32,8,8,128]{3,2,1,0:T(8,128)(2,1)S(1)}, bf16[32,8,8,128]{3,2,1,0:T(8,128)(2,1)}, u32[]{:S(2)}) copy-start(bf16[32,8,8,128]{3,2,1,0:T(8,128)(2,1)} %param.14) | copy-start | bytes 1572868
  20.1 11.1 %copy-start.3 = (bf16[4,128,1024]{2,1,0:T(8,128)(2,1)S(1)}, bf16[4,128,1024]{2,1,0:T(8,128)(2,1)}, u32[]{:S(2)}) copy-start(bf16[4,128,1024]{2,1,0:T(8,128)(2,1)} %constant.17.clone.zi) | copy-start | bytes 3145732
  27.0 7.5 %collective-permute-start.6 = (bf16[256,128]{1,0:T(8,128)(2,1)S(1)}, bf16[256,128]{1,0:T(8,128)(2,1)S(1)}, u32[]{:S(2)}, u32[]{:S(2)}) collective-permute-start(bf16[256,128]{1,0:T(8,128)(2,1)S(1)} %get-tuple-element.78), channel_id=1, source_target_pairs={{0,8},{4,12},{8,0},{12,4},{1,9},{5,13},{9,1},{13,5},{2,10},{6,14},... | collective-permute-start | bytes 196616 | tf_op jit(solution)/shard_map/ppermute | solution.py:664
  29.9 6.2 %collective-permute-start.7 = (bf16[256,128]{1,0:T(8,128)(2,1)S(1)}, bf16[256,128]{1,0:T(8,128)(2,1)S(1)}, u32[]{:S(2)}, u32[]{:S(2)}) collective-permute-start(bf16[256,128]{1,0:T(8,128)(2,1)S(1)} %get-tuple-element.79), channel_id=1, source_target_pairs={{0,12},{4,8},{8,4},{12,0},{1,13},{5,9},{9,5},{13,1},{2,14},{6,10},... | collective-permute-start | bytes 196616 | tf_op jit(solution)/shard_map/ppermute | solution.py:664
  31.2 5.0 %collective-permute-start.8 = (bf16[256,128]{1,0:T(8,128)(2,1)S(1)}, bf16[256,128]{1,0:T(8,128)(2,1)S(1)}, u32[]{:S(2)}, u32[]{:S(2)}) collective-permute-start(bf16[256,128]{1,0:T(8,128)(2,1)S(1)} %get-tuple-element.80), channel_id=1, source_target_pairs={{0,4},{4,0},{8,12},{12,8},{1,5},{5,1},{9,13},{13,9},{2,6},{6,2},{1... | collective-permute-start | bytes 196616 | tf_op jit(solution)/shard_map/ppermute | solution.py:664
  36.5 4.3 %collective-permute-start.9 = (bf16[256,128]{1,0:T(8,128)(2,1)S(1)}, bf16[256,128]{1,0:T(8,128)(2,1)S(1)}, u32[]{:S(2)}, u32[]{:S(2)}) collective-permute-start(bf16[256,128]{1,0:T(8,128)(2,1)S(1)} %get-tuple-element.84), channel_id=1, source_target_pairs={{0,2},{1,3},{2,0},{3,1},{4,6},{5,7},{6,4},{7,5},{8,10},{9,11},{10,... | collective-permute-start | bytes 196616 | tf_op jit(solution)/shard_map/ppermute | solution.py:664
  38.0 4.2 %collective-permute-start.10 = (bf16[256,128]{1,0:T(8,128)(2,1)S(1)}, bf16[256,128]{1,0:T(8,128)(2,1)S(1)}, u32[]{:S(2)}, u32[]{:S(2)}) collective-permute-start(bf16[256,128]{1,0:T(8,128)(2,1)S(1)} %get-tuple-element.85), channel_id=1, source_target_pairs={{0,3},{1,2},{2,1},{3,0},{4,7},{5,6},{6,5},{7,4},{8,11},{9,10},{10,... | collective-permute-start | bytes 196616 | tf_op jit(solution)/shard_map/ppermute | solution.py:664
  38.0 4.2 %collective-permute-start.11 = (bf16[256,128]{1,0:T(8,128)(2,1)S(1)}, bf16[256,128]{1,0:T(8,128)(2,1)S(1)}, u32[]{:S(2)}, u32[]{:S(2)}) collective-permute-start(bf16[256,128]{1,0:T(8,128)(2,1)S(1)} %get-tuple-element.86), channel_id=1, source_target_pairs={{0,1},{1,0},{2,3},{3,2},{4,5},{5,4},{6,7},{7,6},{8,9},{9,8},{10,11... | collective-permute-start | bytes 196616 | tf_op jit(solution)/shard_map/ppermute | solution.py:664
  46.7 14.5 %copy-start.5 = (bf16[4,2,32,1024]{3,2,1,0:T(8,128)(2,1)S(1)}, bf16[4,2,32,1024]{3,2,1,0:T(8,128)(2,1)}, u32[]{:S(2)}) copy-start(bf16[4,2,32,1024]{3,2,1,0:T(8,128)(2,1)} %constant.21.clone.xr) | copy-start | bytes 1572868
  46.7 14.5 %copy-start.9 = (bf16[4,32,256]{2,1,0:T(8,128)(2,1)S(1)}, bf16[4,32,256]{2,1,0:T(8,128)(2,1)}, u32[]{:S(2)}) copy-start(bf16[4,32,256]{2,1,0:T(8,128)(2,1)} %constant.23.clone.xd) | copy-start | bytes 196612
  46.7 4.9 %collective-permute-start.12 = (bf16[256,128]{1,0:T(8,128)(2,1)S(1)}, bf16[256,128]{1,0:T(8,128)(2,1)S(1)}, u32[]{:S(2)}, u32[]{:S(2)}) collective-permute-start(bf16[256,128]{1,0:T(8,128)(2,1)S(1)} %get-tuple-element.95), channel_id=1, source_target_pairs={{0,2},{1,3},{2,0},{3,1},{4,6},{5,7},{6,4},{7,5},{8,10},{9,11},{10,... | collective-permute-start | bytes 196616 | tf_op jit(solution)/shard_map/ppermute | solution.py:664
  47.6 4.4 %collective-permute-start.13 = (bf16[256,128]{1,0:T(8,128)(2,1)S(1)}, bf16[256,128]{1,0:T(8,128)(2,1)S(1)}, u32[]{:S(2)}, u32[]{:S(2)}) collective-permute-start(bf16[256,128]{1,0:T(8,128)(2,1)S(1)} %get-tuple-element.96), channel_id=1, source_target_pairs={{0,3},{1,2},{2,1},{3,0},{4,7},{5,6},{6,5},{7,4},{8,11},{9,10},{10,... | collective-permute-start | bytes 196616 | tf_op jit(solution)/shard_map/ppermute | solution.py:664
  48.1 3.9 %collective-permute-start.14 = (bf16[256,128]{1,0:T(8,128)(2,1)S(1)}, bf16[256,128]{1,0:T(8,128)(2,1)S(1)}, u32[]{:S(2)}, u32[]{:S(2)}) collective-permute-start(bf16[256,128]{1,0:T(8,128)(2,1)S(1)} %get-tuple-element.97), channel_id=1, source_target_pairs={{0,1},{1,0},{2,3},{3,2},{4,5},{5,4},{6,7},{7,6},{8,9},{9,8},{10,11... | collective-permute-start | bytes 196616 | tf_op jit(solution)/shard_map/ppermute | solution.py:664
  52.3 7.4 %collective-permute-start.15 = (bf16[256,128]{1,0:T(8,128)(2,1)S(1)}, bf16[256,128]{1,0:T(8,128)(2,1)S(1)}, u32[]{:S(2)}, u32[]{:S(2)}) collective-permute-start(bf16[256,128]{1,0:T(8,128)(2,1)S(1)} %get-tuple-element.104), channel_id=1, source_target_pairs={{0,8},{4,12},{8,0},{12,4},{1,9},{5,13},{9,1},{13,5},{2,10},{6,14},... | collective-permute-start | bytes 196616 | tf_op jit(solution)/shard_map/ppermute | solution.py:664
  53.5 6.6 %collective-permute-start.16 = (bf16[256,128]{1,0:T(8,128)(2,1)S(1)}, bf16[256,128]{1,0:T(8,128)(2,1)S(1)}, u32[]{:S(2)}, u32[]{:S(2)}) collective-permute-start(bf16[256,128]{1,0:T(8,128)(2,1)S(1)} %get-tuple-element.105), channel_id=1, source_target_pairs={{0,12},{4,8},{8,4},{12,0},{1,13},{5,9},{9,5},{13,1},{2,14},{6,10},... | collective-permute-start | bytes 196616 | tf_op jit(solution)/shard_map/ppermute | solution.py:664
  54.7 6.5 %collective-permute-start.17 = (bf16[256,128]{1,0:T(8,128)(2,1)S(1)}, bf16[256,128]{1,0:T(8,128)(2,1)S(1)}, u32[]{:S(2)}, u32[]{:S(2)}) collective-permute-start(bf16[256,128]{1,0:T(8,128)(2,1)S(1)} %get-tuple-element.106), channel_id=1, source_target_pairs={{0,4},{4,0},{8,12},{12,8},{1,5},{5,1},{9,13},{13,9},{2,6},{6,2},{1... | collective-permute-start | bytes 196616 | tf_op jit(solution)/shard_map/ppermute | solution.py:664
  55.8 1.2 %collective-permute-start.24 = (f32[96,128]{1,0:T(8,128)S(1)}, f32[96,128]{1,0:T(8,128)S(1)}, u32[]{:S(2)}, u32[]{:S(2)}) collective-permute-start(f32[96,128]{1,0:T(8,128)S(1)} %sums.1.after), channel_id=1, source_target_pairs={{0,1},{1,0},{2,3},{3,2},{4,5},{5,4},{6,7},{7,6},{8,9},{9,8},{10,11... | collective-permute-start | bytes 147464 | tf_op jit(solution)/shard_map/ppermute | solution.py:672
  57.1 12.2 %collective-permute-start.25 = (f32[96,128]{1,0:T(8,128)S(1)}, f32[96,128]{1,0:T(8,128)S(1)}, u32[]{:S(2)}, u32[]{:S(2)}) collective-permute-start(f32[96,128]{1,0:T(8,128)S(1)} %add.9), channel_id=1, source_target_pairs={{0,2},{2,0},{1,3},{3,1},{4,6},{6,4},{5,7},{7,5},{8,10},{10,8},{9,1... | collective-permute-start | bytes 147464 | tf_op jit(solution)/shard_map/ppermute | solution.py:672
  65.7 10.1 %collective-permute-start.18 = (bf16[256,128]{1,0:T(8,128)(2,1)S(1)}, bf16[256,128]{1,0:T(8,128)(2,1)S(1)}, u32[]{:S(2)}, u32[]{:S(2)}) collective-permute-start(bf16[256,128]{1,0:T(8,128)(2,1)S(1)} %get-tuple-element.109), channel_id=1, source_target_pairs={{0,8},{4,12},{8,0},{12,4},{1,9},{5,13},{9,1},{13,5},{2,10},{6,14},... | collective-permute-start | bytes 196616 | tf_op jit(solution)/shard_map/ppermute | solution.py:664
  67.5 8.3 %collective-permute-start.19 = (bf16[256,128]{1,0:T(8,128)(2,1)S(1)}, bf16[256,128]{1,0:T(8,128)(2,1)S(1)}, u32[]{:S(2)}, u32[]{:S(2)}) collective-permute-start(bf16[256,128]{1,0:T(8,128)(2,1)S(1)} %get-tuple-element.110), channel_id=1, source_target_pairs={{0,12},{4,8},{8,4},{12,0},{1,13},{5,9},{9,5},{13,1},{2,14},{6,10},... | collective-permute-start | bytes 196616 | tf_op jit(solution)/shard_map/ppermute | solution.py:664
  68.7 7.1 %collective-permute-start.20 = (bf16[256,128]{1,0:T(8,128)(2,1)S(1)}, bf16[256,128]{1,0:T(8,128)(2,1)S(1)}, u32[]{:S(2)}, u32[]{:S(2)}) collective-permute-start(bf16[256,128]{1,0:T(8,128)(2,1)S(1)} %get-tuple-element.111), channel_id=1, source_target_pairs={{0,4},{4,0},{8,12},{12,8},{1,5},{5,1},{9,13},{13,9},{2,6},{6,2},{1... | collective-permute-start | bytes 196616 | tf_op jit(solution)/shard_map/ppermute | solution.py:664
  69.3 9.1 %collective-permute-start.26 = (f32[96,128]{1,0:T(8,128)S(1)}, f32[96,128]{1,0:T(8,128)S(1)}, u32[]{:S(2)}, u32[]{:S(2)}) collective-permute-start(f32[96,128]{1,0:T(8,128)S(1)} %add.10), channel_id=1, source_target_pairs={{0,4},{4,0},{8,12},{12,8},{1,5},{5,1},{9,13},{13,9},{2,6},{6,2},{1... | collective-permute-start | bytes 147464 | tf_op jit(solution)/shard_map/ppermute | solution.py:672
  76.2 8.0 %collective-permute-start.21 = (bf16[256,128]{1,0:T(8,128)(2,1)S(1)}, bf16[256,128]{1,0:T(8,128)(2,1)S(1)}, u32[]{:S(2)}, u32[]{:S(2)}) collective-permute-start(bf16[256,128]{1,0:T(8,128)(2,1)S(1)} %get-tuple-element.116), channel_id=1, source_target_pairs={{0,2},{1,3},{2,0},{3,1},{4,6},{5,7},{6,4},{7,5},{8,10},{9,11},{10,... | collective-permute-start | bytes 196616 | tf_op jit(solution)/shard_map/ppermute | solution.py:664
  77.2 6.9 %collective-permute-start.22 = (bf16[256,128]{1,0:T(8,128)(2,1)S(1)}, bf16[256,128]{1,0:T(8,128)(2,1)S(1)}, u32[]{:S(2)}, u32[]{:S(2)}) collective-permute-start(bf16[256,128]{1,0:T(8,128)(2,1)S(1)} %get-tuple-element.117), channel_id=1, source_target_pairs={{0,3},{1,2},{2,1},{3,0},{4,7},{5,6},{6,5},{7,4},{8,11},{9,10},{10,... | collective-permute-start | bytes 196616 | tf_op jit(solution)/shard_map/ppermute | solution.py:664
  77.2 6.9 %collective-permute-start.23 = (bf16[256,128]{1,0:T(8,128)(2,1)S(1)}, bf16[256,128]{1,0:T(8,128)(2,1)S(1)}, u32[]{:S(2)}, u32[]{:S(2)}) collective-permute-start(bf16[256,128]{1,0:T(8,128)(2,1)S(1)} %get-tuple-element.118), channel_id=1, source_target_pairs={{0,1},{1,0},{2,3},{3,2},{4,5},{5,4},{6,7},{7,6},{8,9},{9,8},{10,11... | collective-permute-start | bytes 196616 | tf_op jit(solution)/shard_map/ppermute | solution.py:664
  78.4 5.7 %collective-permute-start.27 = (f32[96,128]{1,0:T(8,128)S(1)}, f32[96,128]{1,0:T(8,128)S(1)}, u32[]{:S(2)}, u32[]{:S(2)}) collective-permute-start(f32[96,128]{1,0:T(8,128)S(1)} %add.11.part), channel_id=1, source_target_pairs={{0,8},{4,12},{8,0},{12,4},{1,9},{5,13},{9,1},{13,5},{2,10},{6,14},... | collective-permute-start | bytes 147464 | tf_op jit(solution)/shard_map/ppermute | solution.py:672
  (10 other events, 82.5 us)
